TPU v7x, 32 devices: a whole 2x2x4 slice. The times are simulated.
32 devices in a mesh: seq: 4 (over z), fsdp: 8 (over y, x, core).
Axes of the slice: x: 2, y: 2, z: 4, core: 2. Of those that a mesh axis runs over, the one named last changes fastest.
Arguments:
- tokens: bfloat16 [8, 1024, 2048], P('fsdp', 'seq'), may hold values from -6 to 6
- segments: int32 [8, 1024], P('fsdp'), may hold values from 0 to 3, never falling along the last dimension, each value on 1 to 512 neighbouring positions
- expert_ids: int32 [8, 1024, 4], P('fsdp', 'seq'), may hold values from 0 to 7, all different within a row; in each aligned block of 256 rows (0 to 255, 256 to 511, ..., all dimensions but the last counted through in order) at most 192 rows name the same one
- expert_gates: float32 [8, 1024, 4], P('fsdp', 'seq'), may hold values from 0.15 to 0.35
- attn_gain: bfloat16 [2048], P('fsdp'), may hold values from 0.5 to 1.5
- qkv_weight: bfloat16 [2048, 6144], P('fsdp'), may hold values from -0.125 to 0.125
- qkv_bias: bfloat16 [6144], P('fsdp'), may hold values from -0.59765625 to 0.59765625
- out_weight: bfloat16 [2048, 2048], P('fsdp'), may hold values from -1 to 1
- ffn_gain: bfloat16 [2048], P('fsdp'), may hold values from 0.5 to 1.5
- shared_gate_up: bfloat16 [2048, 2, 5632], P(None, None, 'fsdp'), may hold values from -0.125 to 0.125
- shared_down: bfloat16 [5632, 2048], P('fsdp'), may hold values from -0.078125 to 0.078125
- shared_gate: bfloat16 [2048], P('fsdp'), may hold values from -0.125 to 0.125
- expert_gate_up: bfloat16 [8, 2048, 2816], P(None, 'fsdp'), may hold values from -0.125 to 0.125
- expert_down: bfloat16 [8, 1408, 2048], P(None, 'fsdp'), may hold values from -0.15625 to 0.15625
- cotangent: bfloat16 [8, 1024, 2048], P('fsdp', 'seq'), may hold values from -6 to 6
Outputs:
- output: bfloat16 [8, 1024, 2048], P('fsdp', 'seq')
- input_grad: bfloat16 [8, 1024, 2048], P('fsdp', 'seq')
- attn_gain_grad: float32 [2048], P('fsdp')
- qkv_weight_grad: float32 [2048, 6144], P('fsdp')
- qkv_bias_grad: float32 [6144], P('fsdp')
- out_weight_grad: float32 [2048, 2048], P('fsdp')
- ffn_gain_grad: float32 [2048], P('fsdp')
- shared_gate_up_grad: float32 [2048, 2, 5632], P(None, None, 'fsdp')
- shared_down_grad: float32 [5632, 2048], P('fsdp')
- shared_gate_grad: float32 [2048], P('fsdp')
- expert_gate_up_grad: float32 [8, 2048, 2816], P(None, 'fsdp')
- expert_down_grad: float32 [8, 1408, 2048], P(None, 'fsdp')
Inputs may be any that keep to these rules, and one draw needn't show every extreme that they name: `segments`: segment numbers never fall along a sequence; a document holds at most 512 positions, and some document exactly that many. `expert_ids`: each position names 4 different experts. Among the 256 positions that one device holds, no expert is named more than 192 times, and some expert exactly that often.
All inputs are finite; a program needn't handle non-finite values.
Results may differ from a plain program's by a relative error of at most 0.019.
Values may be sent and summed in bfloat16 or wider, within the bound.
A program may use at most 448 MiB of HBM per device.

v0:
```python
import math

import jax
import jax.numpy as jnp
from jax import lax
from jax.sharding import PartitionSpec as P

D = 2048
HEADS = 16
HEAD_DIM = 128
FF_EXPERT = 1408
TOP = 4
EXPERTS = 8
QBLOCK = 512


EPSILON = 1e-06
THETA = 1000000.0


def prefix(value, axis, join, neutral):
    count, mine = (lax.axis_size(axis), lax.axis_index(axis))
    pieces = lax.all_gather(value, axis)
    so_far = jnp.full_like(value, 0) + jnp.asarray(neutral, value.dtype)

    def hop(position, so_far):
        longer = join(so_far, pieces[position])
        return jnp.where(position < mine, longer, so_far)

    return lax.fori_loop(0, count - 1, hop, so_far)


def norm_rows(values, norm_gain):
    return (
        values * lax.rsqrt(jnp.mean(values * values, axis=-1, keepdims=True) + EPSILON) * norm_gain
    )


def rope_tables(positions):
    steps_half = jnp.arange(HEAD_DIM // 2, dtype=jnp.int32).astype(jnp.float32)
    frequency = jnp.exp(steps_half * (-2.0 * math.log(THETA) / HEAD_DIM))
    angles = positions.astype(jnp.float32)[:, None] * frequency[None, :]
    angles = jnp.concatenate([angles, angles], axis=-1)
    return (jnp.cos(angles), jnp.sin(angles))


def rotate(head_rows, cosine, sine_table):
    middle = head_rows.shape[-1] // 2
    turned = jnp.concatenate([-head_rows[..., middle:], head_rows[..., :middle]], axis=-1)
    return head_rows * cosine[:, None, :] + turned * sine_table[:, None, :]


def gated_product(gate_part, up_part):
    return jax.nn.silu(gate_part) * up_part


def expert_swiglu_back(both_parts, grad_inner):
    _, pullback = jax.vjp(gated_product, both_parts[..., :FF_EXPERT], both_parts[..., FF_EXPERT:])
    grad_gate, grad_up = pullback(grad_inner)
    return jnp.concatenate([grad_gate, grad_up], axis=-1)


def shared_swiglu_back(both_parts, grad_inner):
    _, pullback = jax.vjp(gated_product, both_parts[:, 0], both_parts[:, 1])
    grad_gate, grad_up = pullback(grad_inner)
    return jnp.stack([grad_gate, grad_up], axis=1)


def expert_weights(gate_up_piece, down_piece):
    return (
        lax.all_gather(gate_up_piece, "fsdp", axis=0, tiled=True),
        lax.all_gather(down_piece, "fsdp", axis=0, tiled=True),
    )


def add_counts(earlier, later):
    return earlier + later


def on_device(
    tokens,
    segments,
    expert_ids,
    expert_gates,
    attn_gain,
    qkv_weight,
    qkv_bias,
    out_weight,
    ffn_gain,
    shared_gate_up,
    shared_down,
    shared_gate,
    expert_gate_up,
    expert_down,
    cotangent,
):
    row_count = tokens.shape[1]
    length = segments.shape[1]
    local_heads = HEADS // lax.axis_size("seq")
    factor = 1.0 / math.sqrt(HEAD_DIM)
    capacity = length * TOP // EXPERTS
    slot_count = 3 * row_count * TOP // (2 * EXPERTS)
    block_count = length // QBLOCK
    bf16 = jnp.bfloat16
    f32 = jnp.float32
    gain_one, weight_qkv, bias_qkv, weight_out, gain_two, gate_vector = (
        lax.all_gather(attn_gain, "fsdp", axis=0, tiled=True),
        lax.all_gather(qkv_weight, "fsdp", axis=0, tiled=True),
        lax.all_gather(qkv_bias, "fsdp", axis=0, tiled=True),
        lax.all_gather(out_weight, "fsdp", axis=0, tiled=True),
        lax.all_gather(ffn_gain, "fsdp", axis=0, tiled=True),
        lax.all_gather(shared_gate, "fsdp", axis=0, tiled=True),
    )
    inputs = tokens[0].astype(f32)
    documents = segments[0]
    positions = lax.axis_index("seq") * row_count + jnp.arange(row_count, dtype=jnp.int32)
    cosine, sine_table = rope_tables(positions)
    normed, first_back = jax.vjp(norm_rows, inputs, gain_one.astype(f32))
    normed_low = normed.astype(bf16)
    joined_qkv = jnp.dot(normed_low, weight_qkv, preferred_element_type=f32) + bias_qkv.astype(f32)
    split_heads = joined_qkv.reshape(row_count, 3, HEADS, HEAD_DIM)
    queries = rotate(split_heads[:, 0], cosine, sine_table).astype(bf16)
    key_rows = rotate(split_heads[:, 1], cosine, sine_table).astype(bf16)
    value_rows = split_heads[:, 2].astype(bf16)
    head_queries, head_keys, head_values = (
        lax.all_to_all(queries, "seq", split_axis=1, concat_axis=0, tiled=True),
        lax.all_to_all(key_rows, "seq", split_axis=1, concat_axis=0, tiled=True),
        lax.all_to_all(value_rows, "seq", split_axis=1, concat_axis=0, tiled=True),
    )
    key_place = jnp.arange(length, dtype=jnp.int32)

    def block_scores(block_index):
        first_row = block_index * QBLOCK
        query_block = lax.dynamic_slice_in_dim(head_queries, first_row, QBLOCK, 0)
        block_docs = lax.dynamic_slice_in_dim(documents, first_row, QBLOCK, 0)
        scores = (
            jnp.einsum("qhd,khd->hqk", query_block, head_keys, preferred_element_type=f32) * factor
        )
        row_place = first_row + jnp.arange(QBLOCK, dtype=jnp.int32)
        allowed = (row_place[:, None] >= key_place[None, :]) & (
            block_docs[:, None] == documents[None, :]
        )
        return (query_block, jnp.where(allowed[None], scores, -1e30))

    def forward_block(block_index):
        _, scores = block_scores(block_index)
        top_score = jnp.max(scores, axis=-1, keepdims=True)
        weights = jnp.exp(scores - top_score)
        totals = jnp.sum(weights, axis=-1, keepdims=True)
        probability = (weights / totals).astype(bf16)
        mixture = jnp.einsum("hqk,khd->qhd", probability, head_values, preferred_element_type=f32)
        return (mixture.astype(bf16), (top_score + jnp.log(totals))[..., 0])

    mixed_blocks, log_totals = lax.map(forward_block, jnp.arange(block_count, dtype=jnp.int32))
    mixed_heads = mixed_blocks.reshape(length, local_heads, HEAD_DIM)
    mixed_rows = lax.all_to_all(
        mixed_heads, "seq", split_axis=0, concat_axis=1, tiled=True
    ).reshape(row_count, D)
    projected = jnp.dot(mixed_rows, weight_out, preferred_element_type=f32)
    hidden = inputs + projected
    normed_two, second_back = jax.vjp(norm_rows, hidden, gain_two.astype(f32))
    second = normed_two.astype(bf16)
    opening = jax.nn.sigmoid(jnp.dot(second, gate_vector, preferred_element_type=f32))
    whole_gate_up, whole_down = (
        lax.all_gather(shared_gate_up, "fsdp", axis=2, tiled=True),
        lax.all_gather(shared_down, "fsdp", axis=0, tiled=True),
    )
    shared_both = jnp.einsum("td,dcf->tcf", second, whole_gate_up, preferred_element_type=f32)
    shared_inner = (jax.nn.silu(shared_both[:, 0]) * shared_both[:, 1]).astype(bf16)
    branch = jnp.dot(shared_inner, whole_down, preferred_element_type=f32)
    expert_names = jnp.arange(EXPERTS, dtype=jnp.int32)
    picked = expert_ids[0]
    matches = picked[:, :, None] == expert_names[None, None, :]
    match_ints = matches.astype(jnp.int32)
    chosen = jnp.sum(match_ints, axis=1)
    earlier = jnp.cumsum(chosen, axis=0) - chosen
    offsets = prefix(jnp.sum(chosen, axis=0), "seq", add_counts, jnp.zeros((EXPERTS,), jnp.int32))
    retained = (chosen > 0) & (offsets[None, :] + earlier < capacity)
    portion = jnp.sum(
        jnp.where(matches, expert_gates[0][:, :, None], 0.0), axis=1
    ) * retained.astype(f32)
    slot_ids = jnp.arange(slot_count, dtype=jnp.int32)
    marks = (chosen.T[:, None, :] > 0) & (earlier.T[:, None, :] == slot_ids[None, :, None])
    mark_ints = marks.astype(jnp.int32)
    owners = jnp.sum(
        mark_ints * jnp.arange(row_count, dtype=jnp.int32)[None, None, :], axis=-1
    ) + row_count * (1 - jnp.sum(mark_ints, axis=-1))
    padded = jnp.concatenate([second, jnp.zeros((1, D), bf16)], axis=0)
    slotted = padded[owners]
    portion_pad = jnp.concatenate([portion, jnp.zeros((1, EXPERTS), f32)], axis=0)
    slot_share = portion_pad[owners, expert_names[:, None]]

    def expert_forward(counter, pieces):
        gate_up_piece, down_piece, expert_inputs = pieces
        whole_up, whole_down_e = expert_weights(gate_up_piece, down_piece)
        both_parts = jnp.dot(expert_inputs, whole_up, preferred_element_type=f32)
        inner_rows = (jax.nn.silu(both_parts[:, :FF_EXPERT]) * both_parts[:, FF_EXPERT:]).astype(
            bf16
        )
        results = jnp.dot(inner_rows, whole_down_e, preferred_element_type=f32)
        return (counter, (both_parts, inner_rows, results))

    _, (expert_both, expert_inner, expert_results) = lax.scan(
        expert_forward, jnp.zeros((), jnp.int32), (expert_gate_up, expert_down, slotted)
    )
    pick_place = jnp.sum(match_ints * earlier[:, None, :], axis=-1)
    flat_index = picked * slot_count + pick_place
    pick_share = jnp.sum(jnp.where(matches, portion[:, None, :], 0.0), axis=-1)
    routed = jnp.sum(
        expert_results.reshape(EXPERTS * slot_count, D)[flat_index] * pick_share[..., None], axis=1
    )
    output = (hidden + opening[:, None] * branch + routed).astype(bf16)
    upstream = cotangent[0].astype(f32)
    upstream_pad = jnp.concatenate([upstream, jnp.zeros((1, D), f32)], axis=0)
    grad_results = (slot_share[..., None] * upstream_pad[owners]).astype(bf16)

    def expert_backward(counter, pieces):
        gate_up_piece, down_piece, expert_inputs, both_parts, inner_rows, grad_rows = pieces
        whole_up, whole_down_e = expert_weights(gate_up_piece, down_piece)
        grad_inner = jnp.einsum("sd,fd->sf", grad_rows, whole_down_e, preferred_element_type=f32)
        grad_both = expert_swiglu_back(both_parts, grad_inner).astype(bf16)
        grad_inputs = jnp.einsum("sf,df->sd", grad_both, whole_up, preferred_element_type=f32)
        grad_up_full = jnp.einsum("sd,sf->df", expert_inputs, grad_both, preferred_element_type=f32)
        grad_down_full = jnp.einsum("sf,sd->fd", inner_rows, grad_rows, preferred_element_type=f32)
        grad_up_part, grad_down_part = (
            lax.psum_scatter(
                grad_up_full.astype(jnp.bfloat16), "fsdp", scatter_dimension=0, tiled=True
            ).astype(jnp.float32),
            lax.psum_scatter(
                grad_down_full.astype(jnp.bfloat16), "fsdp", scatter_dimension=0, tiled=True
            ).astype(jnp.float32),
        )
        return (counter, (grad_inputs, grad_up_part, grad_down_part))

    _, (expert_grad_inputs, grad_expert_gate_up, grad_expert_down) = lax.scan(
        expert_backward,
        jnp.zeros((), jnp.int32),
        (expert_gate_up, expert_down, slotted, expert_both, expert_inner, grad_results),
    )
    grad_second = jnp.sum(expert_grad_inputs.reshape(EXPERTS * slot_count, D)[flat_index], axis=1)
    grad_branch = (opening[:, None] * upstream).astype(bf16)
    grad_logit = jnp.sum(upstream * branch, axis=-1) * opening * (1.0 - opening)
    grad_second = grad_second + grad_logit[:, None] * gate_vector.astype(f32)[None, :]
    grad_gate_vector = jnp.dot(grad_logit, second.astype(f32), precision=lax.Precision.HIGHEST)
    grad_shared_inner = jnp.einsum("td,fd->tf", grad_branch, whole_down, preferred_element_type=f32)
    grad_shared_both = shared_swiglu_back(shared_both, grad_shared_inner).astype(bf16)
    grad_second = grad_second + jnp.einsum(
        "tcf,dcf->td", grad_shared_both, whole_gate_up, preferred_element_type=f32
    )
    full_gate_up = jnp.einsum("td,tcf->dcf", second, grad_shared_both, preferred_element_type=f32)
    full_down = jnp.einsum("tf,td->fd", shared_inner, grad_branch, preferred_element_type=f32)
    grad_shared_gate_up, grad_shared_down = (
        lax.psum_scatter(
            full_gate_up.astype(jnp.bfloat16), "fsdp", scatter_dimension=2, tiled=True
        ).astype(jnp.float32),
        lax.psum_scatter(
            full_down.astype(jnp.bfloat16), "fsdp", scatter_dimension=0, tiled=True
        ).astype(jnp.float32),
    )
    grad_hidden_part, grad_gain_two = second_back(grad_second)
    grad_hidden = upstream + grad_hidden_part
    grad_projected = grad_hidden.astype(bf16)
    grad_weight_out = jnp.einsum(
        "td,te->de", mixed_rows, grad_projected, preferred_element_type=f32
    )
    grad_mixture = jnp.einsum(
        "te,de->td", grad_projected, weight_out, preferred_element_type=f32
    ).astype(bf16)
    grad_heads = lax.all_to_all(
        grad_mixture.reshape(row_count, HEADS, HEAD_DIM),
        "seq",
        split_axis=1,
        concat_axis=0,
        tiled=True,
    )

    def backward_block(totals_kv, block_index):
        grad_keys, grad_values = totals_kv
        query_block, scores = block_scores(block_index)
        first_row = block_index * QBLOCK
        log_block = lax.dynamic_index_in_dim(log_totals, block_index, 0, keepdims=False)
        probability = jnp.exp(scores - log_block[..., None])
        grad_block = lax.dynamic_slice_in_dim(grad_heads, first_row, QBLOCK, 0)
        grad_values = grad_values + jnp.einsum(
            "hqk,qhd->khd", probability.astype(bf16), grad_block, preferred_element_type=f32
        )
        grad_probability = jnp.einsum(
            "qhd,khd->hqk", grad_block, head_values, preferred_element_type=f32
        )
        centre = jnp.sum(grad_probability * probability, axis=-1, keepdims=True)
        grad_scores = (probability * (grad_probability - centre)).astype(bf16)
        grad_queries = (
            jnp.einsum("hqk,khd->qhd", grad_scores, head_keys, preferred_element_type=f32) * factor
        )
        grad_keys = (
            grad_keys
            + jnp.einsum("hqk,qhd->khd", grad_scores, query_block, preferred_element_type=f32)
            * factor
        )
        return ((grad_keys, grad_values), grad_queries)

    zero_heads = jnp.zeros((length, local_heads, HEAD_DIM), f32)
    (grad_keys, grad_values), grad_query_blocks = lax.scan(
        backward_block, (zero_heads, zero_heads), jnp.arange(block_count, dtype=jnp.int32)
    )
    grad_queries = grad_query_blocks.reshape(length, local_heads, HEAD_DIM)
    back_queries, back_keys, back_values = (
        lax.all_to_all(grad_queries.astype(bf16), "seq", split_axis=0, concat_axis=1, tiled=True),
        lax.all_to_all(grad_keys.astype(bf16), "seq", split_axis=0, concat_axis=1, tiled=True),
        lax.all_to_all(grad_values.astype(bf16), "seq", split_axis=0, concat_axis=1, tiled=True),
    )

    def turn_heads(head_rows):
        return rotate(head_rows, cosine, sine_table)

    _, turn_back = jax.vjp(turn_heads, split_heads[:, 0])
    grad_joined = (
        jnp.stack(
            [
                turn_back(back_queries.astype(f32))[0],
                turn_back(back_keys.astype(f32))[0],
                back_values.astype(f32),
            ],
            axis=1,
        )
        .reshape(row_count, 3 * D)
        .astype(bf16)
    )
    grad_bias = jnp.sum(grad_joined.astype(f32), axis=0)
    grad_weight_qkv = jnp.einsum("td,te->de", normed_low, grad_joined, preferred_element_type=f32)
    grad_normed = jnp.einsum("te,de->td", grad_joined, weight_qkv, preferred_element_type=f32)
    grad_input_part, grad_gain_one = first_back(grad_normed)
    input_grad = (grad_hidden + grad_input_part).astype(bf16)
    shard_gain_one, shard_qkv, shard_bias, shard_out, shard_gain_two, shard_gate = (
        lax.psum_scatter(
            grad_gain_one.astype(jnp.bfloat16), "fsdp", scatter_dimension=0, tiled=True
        ).astype(jnp.float32),
        lax.psum_scatter(
            grad_weight_qkv.astype(jnp.bfloat16), "fsdp", scatter_dimension=0, tiled=True
        ).astype(jnp.float32),
        lax.psum_scatter(
            grad_bias.astype(jnp.bfloat16), "fsdp", scatter_dimension=0, tiled=True
        ).astype(jnp.float32),
        lax.psum_scatter(
            grad_weight_out.astype(jnp.bfloat16), "fsdp", scatter_dimension=0, tiled=True
        ).astype(jnp.float32),
        lax.psum_scatter(
            grad_gain_two.astype(jnp.bfloat16), "fsdp", scatter_dimension=0, tiled=True
        ).astype(jnp.float32),
        lax.psum_scatter(
            grad_gate_vector.astype(jnp.bfloat16), "fsdp", scatter_dimension=0, tiled=True
        ).astype(jnp.float32),
    )
    summed = (
        lax.psum(shard_gain_one.astype(jnp.bfloat16), "seq").astype(jnp.float32),
        lax.psum(shard_qkv.astype(jnp.bfloat16), "seq").astype(jnp.float32),
        lax.psum(shard_bias.astype(jnp.bfloat16), "seq").astype(jnp.float32),
        lax.psum(shard_out.astype(jnp.bfloat16), "seq").astype(jnp.float32),
        lax.psum(shard_gain_two.astype(jnp.bfloat16), "seq").astype(jnp.float32),
        lax.psum(grad_shared_gate_up.astype(jnp.bfloat16), "seq").astype(jnp.float32),
        lax.psum(grad_shared_down.astype(jnp.bfloat16), "seq").astype(jnp.float32),
        lax.psum(shard_gate.astype(jnp.bfloat16), "seq").astype(jnp.float32),
        lax.psum(grad_expert_gate_up.astype(jnp.bfloat16), "seq").astype(jnp.float32),
        lax.psum(grad_expert_down.astype(jnp.bfloat16), "seq").astype(jnp.float32),
    )
    return (
        output[None],
        input_grad[None],
        summed[0],
        summed[1],
        summed[2],
        summed[3],
        summed[4],
        summed[5],
        summed[6],
        summed[7],
        summed[8],
        summed[9],
    )


def solution(mesh):
    return jax.shard_map(
        on_device,
        mesh=mesh,
        in_specs=(
            P("fsdp", "seq", None),
            P("fsdp", None),
            P("fsdp", "seq", None),
            P("fsdp", "seq", None),
            P("fsdp"),
            P("fsdp", None),
            P("fsdp"),
            P("fsdp", None),
            P("fsdp"),
            P(None, None, "fsdp"),
            P("fsdp", None),
            P("fsdp"),
            P(None, "fsdp", None),
            P(None, "fsdp", None),
            P("fsdp", "seq", None),
        ),
        out_specs=(
            P("fsdp", "seq", None),
            P("fsdp", "seq", None),
            P("fsdp"),
            P("fsdp", None),
            P("fsdp"),
            P("fsdp", None),
            P("fsdp"),
            P(None, None, "fsdp"),
            P("fsdp", None),
            P("fsdp"),
            P(None, "fsdp", None),
            P(None, "fsdp", None),
        ),
        check_vma=False,
    )
```

profile of v0, /device:TPU:0, one launch (start us, length us, event | category | flops | bytes accessed | tf_op | source)
XLA Modules:
  0.0 5617.6 jit_solution(3809711536340188011)
XLA Ops:
  29.7 108.3 %all-gather.26.cloned.1.call-done = bf16[2048,6144]{1,0:T(8,128)(2,1)} async-done(((bf16[256,6144]{1,0:T(8,128)(2,1)}), bf16[2048,6144]{1,0:T(8,128)(2,1)}) %all-gather.26.cloned.1.call-update) | async-done | bytes 25165840 | tf_op jit(solution)/shard_map/all_gather | solution.py:108
  339.4 977.2 %while.70 = (s32[]{:T(128)}, f32[8,192,2816]{2,1,0:T(8,128)}, bf16[8,192,1408]{2,1,0:T(8,128)(2,1)}, f32[8,192,2048]{2,1,0:T(8,128)}, bf16[8,192,2048]{2,1,0:T(8...) while((s32[]{:T(128)}, f32[8,192,2816]{2,1,0:T(8,128)}, ...), condition=%wide.region_12.13_spmd, body=%wide.region_11.12_spmd.sunk | while | flops 3323510784 | bytes 90490040 | solution.py:203
  344.1 66.9 %all-gather.34.cloned.1.call-done = bf16[1,2048,2816]{2,1,0:T(8,128)(2,1)} async-done(((bf16[1,256,2816]{2,1,0:T(8,128)(2,1)}), bf16[1,2048,2816]{2,1,0:T(8,128)(2,1)}) %all-gather.34.cloned.1.call-update) | async-done | bytes 11534352 | tf_op jit(solution)/shard_map/while/body/eval_jaxpr/all_gather | solution.py:71
  466.8 66.2 %all-gather.34.cloned.1.call-done = bf16[1,2048,2816]{2,1,0:T(8,128)(2,1)} async-done(((bf16[1,256,2816]{2,1,0:T(8,128)(2,1)}), bf16[1,2048,2816]{2,1,0:T(8,128)(2,1)}) %all-gather.34.cloned.1.call-update) | async-done | bytes 11534352 | tf_op jit(solution)/shard_map/while/body/eval_jaxpr/all_gather | solution.py:71
  588.7 66.5 %all-gather.34.cloned.1.call-done = bf16[1,2048,2816]{2,1,0:T(8,128)(2,1)} async-done(((bf16[1,256,2816]{2,1,0:T(8,128)(2,1)}), bf16[1,2048,2816]{2,1,0:T(8,128)(2,1)}) %all-gather.34.cloned.1.call-update) | async-done | bytes 11534352 | tf_op jit(solution)/shard_map/while/body/eval_jaxpr/all_gather | solution.py:71
  711.0 66.5 %all-gather.34.cloned.1.call-done = bf16[1,2048,2816]{2,1,0:T(8,128)(2,1)} async-done(((bf16[1,256,2816]{2,1,0:T(8,128)(2,1)}), bf16[1,2048,2816]{2,1,0:T(8,128)(2,1)}) %all-gather.34.cloned.1.call-update) | async-done | bytes 11534352 | tf_op jit(solution)/shard_map/while/body/eval_jaxpr/all_gather | solution.py:71
  833.2 66.5 %all-gather.34.cloned.1.call-done = bf16[1,2048,2816]{2,1,0:T(8,128)(2,1)} async-done(((bf16[1,256,2816]{2,1,0:T(8,128)(2,1)}), bf16[1,2048,2816]{2,1,0:T(8,128)(2,1)}) %all-gather.34.cloned.1.call-update) | async-done | bytes 11534352 | tf_op jit(solution)/shard_map/while/body/eval_jaxpr/all_gather | solution.py:71
  955.4 66.5 %all-gather.34.cloned.1.call-done = bf16[1,2048,2816]{2,1,0:T(8,128)(2,1)} async-done(((bf16[1,256,2816]{2,1,0:T(8,128)(2,1)}), bf16[1,2048,2816]{2,1,0:T(8,128)(2,1)}) %all-gather.34.cloned.1.call-update) | async-done | bytes 11534352 | tf_op jit(solution)/shard_map/while/body/eval_jaxpr/all_gather | solution.py:71
  1199.4 66.2 %all-gather.34.cloned.1.call-done = bf16[1,2048,2816]{2,1,0:T(8,128)(2,1)} async-done(((bf16[1,256,2816]{2,1,0:T(8,128)(2,1)}), bf16[1,2048,2816]{2,1,0:T(8,128)(2,1)}) %all-gather.34.cloned.1.call-update) | async-done | bytes 11534352 | tf_op jit(solution)/shard_map/while/body/eval_jaxpr/all_gather | solution.py:71
  1322.7 2179.5 %while.71 = (s32[]{:T(128)}, f32[8,192,2048]{2,1,0:T(8,128)}, bf16[8,256,2816]{2,1,0:T(8,128)(2,1)}, bf16[8,176,2048]{2,1,0:T(8,128)(2,1)}, bf16[8,192,2048]{2,1...) while((s32[]{:T(128)}, f32[8,192,2048]{2,1,0:T(8,128)}, ...), condition=%wide.region_23.24_spmd, body=%wide.region_20.23_spmd.sunk | while | flops 6661619712 | bytes 176407824 | solution.py:235
  1434.7 67.6 %all-gather.38.cloned.1.call-done = bf16[1,2048,2816]{2,1,0:T(8,128)(2,1)} async-done(((bf16[1,256,2816]{2,1,0:T(8,128)(2,1)}), bf16[1,2048,2816]{2,1,0:T(8,128)(2,1)}) %all-gather.38.cloned.1.call-update) | async-done | bytes 11534352 | tf_op jit(solution)/shard_map/while/body/eval_jaxpr/all_gather | solution.py:71
  1511.6 81.6 %reduce-scatter.15.cloned.1.call-done = bf16[256,2816]{1,0:T(8,128)(2,1)} async-done(((bf16[2048,2816]{1,0:T(8,128)(2,1)}), bf16[256,2816]{1,0:T(8,128)(2,1)}) %reduce-scatter.15.cloned.1.call-update) | async-done | bytes 1441808 | tf_op jit(solution)/shard_map/while/body/eval_jaxpr/reduce_scatter | solution.py:226
  1707.3 67.6 %all-gather.38.cloned.1.call-done = bf16[1,2048,2816]{2,1,0:T(8,128)(2,1)} async-done(((bf16[1,256,2816]{2,1,0:T(8,128)(2,1)}), bf16[1,2048,2816]{2,1,0:T(8,128)(2,1)}) %all-gather.38.cloned.1.call-update) | async-done | bytes 11534352 | tf_op jit(solution)/shard_map/while/body/eval_jaxpr/all_gather | solution.py:71
  1784.2 81.4 %reduce-scatter.15.cloned.1.call-done = bf16[256,2816]{1,0:T(8,128)(2,1)} async-done(((bf16[2048,2816]{1,0:T(8,128)(2,1)}), bf16[256,2816]{1,0:T(8,128)(2,1)}) %reduce-scatter.15.cloned.1.call-update) | async-done | bytes 1441808 | tf_op jit(solution)/shard_map/while/body/eval_jaxpr/reduce_scatter | solution.py:226
  1979.6 67.6 %all-gather.38.cloned.1.call-done = bf16[1,2048,2816]{2,1,0:T(8,128)(2,1)} async-done(((bf16[1,256,2816]{2,1,0:T(8,128)(2,1)}), bf16[1,2048,2816]{2,1,0:T(8,128)(2,1)}) %all-gather.38.cloned.1.call-update) | async-done | bytes 11534352 | tf_op jit(solution)/shard_map/while/body/eval_jaxpr/all_gather | solution.py:71
  2056.5 81.5 %reduce-scatter.15.cloned.1.call-done = bf16[256,2816]{1,0:T(8,128)(2,1)} async-done(((bf16[2048,2816]{1,0:T(8,128)(2,1)}), bf16[256,2816]{1,0:T(8,128)(2,1)}) %reduce-scatter.15.cloned.1.call-update) | async-done | bytes 1441808 | tf_op jit(solution)/shard_map/while/body/eval_jaxpr/reduce_scatter | solution.py:226
  2252.2 67.4 %all-gather.38.cloned.1.call-done = bf16[1,2048,2816]{2,1,0:T(8,128)(2,1)} async-done(((bf16[1,256,2816]{2,1,0:T(8,128)(2,1)}), bf16[1,2048,2816]{2,1,0:T(8,128)(2,1)}) %all-gather.38.cloned.1.call-update) | async-done | bytes 11534352 | tf_op jit(solution)/shard_map/while/body/eval_jaxpr/all_gather | solution.py:71
  2328.9 81.6 %reduce-scatter.15.cloned.1.call-done = bf16[256,2816]{1,0:T(8,128)(2,1)} async-done(((bf16[2048,2816]{1,0:T(8,128)(2,1)}), bf16[256,2816]{1,0:T(8,128)(2,1)}) %reduce-scatter.15.cloned.1.call-update) | async-done | bytes 1441808 | tf_op jit(solution)/shard_map/while/body/eval_jaxpr/reduce_scatter | solution.py:226
  2524.7 67.4 %all-gather.38.cloned.1.call-done = bf16[1,2048,2816]{2,1,0:T(8,128)(2,1)} async-done(((bf16[1,256,2816]{2,1,0:T(8,128)(2,1)}), bf16[1,2048,2816]{2,1,0:T(8,128)(2,1)}) %all-gather.38.cloned.1.call-update) | async-done | bytes 11534352 | tf_op jit(solution)/shard_map/while/body/eval_jaxpr/all_gather | solution.py:71
  2601.4 81.5 %reduce-scatter.15.cloned.1.call-done = bf16[256,2816]{1,0:T(8,128)(2,1)} async-done(((bf16[2048,2816]{1,0:T(8,128)(2,1)}), bf16[256,2816]{1,0:T(8,128)(2,1)}) %reduce-scatter.15.cloned.1.call-update) | async-done | bytes 1441808 | tf_op jit(solution)/shard_map/while/body/eval_jaxpr/reduce_scatter | solution.py:226
  2797.0 67.6 %all-gather.38.cloned.1.call-done = bf16[1,2048,2816]{2,1,0:T(8,128)(2,1)} async-done(((bf16[1,256,2816]{2,1,0:T(8,128)(2,1)}), bf16[1,2048,2816]{2,1,0:T(8,128)(2,1)}) %all-gather.38.cloned.1.call-update) | async-done | bytes 11534352 | tf_op jit(solution)/shard_map/while/body/eval_jaxpr/all_gather | solution.py:71
  2873.8 81.6 %reduce-scatter.15.cloned.1.call-done = bf16[256,2816]{1,0:T(8,128)(2,1)} async-done(((bf16[2048,2816]{1,0:T(8,128)(2,1)}), bf16[256,2816]{1,0:T(8,128)(2,1)}) %reduce-scatter.15.cloned.1.call-update) | async-done | bytes 1441808 | tf_op jit(solution)/shard_map/while/body/eval_jaxpr/reduce_scatter | solution.py:226
  3069.4 67.4 %all-gather.38.cloned.1.call-done = bf16[1,2048,2816]{2,1,0:T(8,128)(2,1)} async-done(((bf16[1,256,2816]{2,1,0:T(8,128)(2,1)}), bf16[1,2048,2816]{2,1,0:T(8,128)(2,1)}) %all-gather.38.cloned.1.call-update) | async-done | bytes 11534352 | tf_op jit(solution)/shard_map/while/body/eval_jaxpr/all_gather | solution.py:71
  3146.1 81.5 %reduce-scatter.15.cloned.1.call-done = bf16[256,2816]{1,0:T(8,128)(2,1)} async-done(((bf16[2048,2816]{1,0:T(8,128)(2,1)}), bf16[256,2816]{1,0:T(8,128)(2,1)}) %reduce-scatter.15.cloned.1.call-update) | async-done | bytes 1441808 | tf_op jit(solution)/shard_map/while/body/eval_jaxpr/reduce_scatter | solution.py:226
  3341.4 67.4 %all-gather.38.cloned.1.call-done = bf16[1,2048,2816]{2,1,0:T(8,128)(2,1)} async-done(((bf16[1,256,2816]{2,1,0:T(8,128)(2,1)}), bf16[1,2048,2816]{2,1,0:T(8,128)(2,1)}) %all-gather.38.cloned.1.call-update) | async-done | bytes 11534352 | tf_op jit(solution)/shard_map/while/body/eval_jaxpr/all_gather | solution.py:71
  3418.1 81.6 %reduce-scatter.15.cloned.1.call-done = bf16[256,2816]{1,0:T(8,128)(2,1)} async-done(((bf16[2048,2816]{1,0:T(8,128)(2,1)}), bf16[256,2816]{1,0:T(8,128)(2,1)}) %reduce-scatter.15.cloned.1.call-update) | async-done | bytes 1441808 | tf_op jit(solution)/shard_map/while/body/eval_jaxpr/reduce_scatter | solution.py:226
  3584.1 134.7 %all-gather.30.cloned.1.call-done = bf16[2048,2,5632]{0,2,1:T(8,128)(2,1)} async-done(((bf16[2048,2,704]{0,2,1:T(8,128)(2,1)}), bf16[2048,2,5632]{0,2,1:T(8,128)(2,1)}) %all-gather.30.cloned.1.call-update) | async-done | bytes 46137360 | tf_op jit(solution)/shard_map/all_gather | solution.py:165
  3744.6 92.6 %all-gather.32.cloned.1.call-done = bf16[5632,2048]{1,0:T(8,128)(2,1)} async-done(((bf16[704,2048]{1,0:T(8,128)(2,1)}), bf16[5632,2048]{1,0:T(8,128)(2,1)}) %all-gather.32.cloned.1.call-update) | async-done | bytes 23068688 | tf_op jit(solution)/shard_map/all_gather | solution.py:166
  3959.7 70.6 %while.74 = (s32[]{:T(128)}, f32[1024,4,128]{0,2,1:T(8,128)S(1)}, f32[1024,4,128]{0,2,1:T(8,128)}, bf16[2,512,4,128]{3,1,0,2:T(8,128)(2,1)}, s32[2]{0:T(128)S(1)...) while((s32[]{:T(128)}, f32[1024,4,128]{0,2,1:T(8,128)S(1)}, ...), condition=%wide.region_29.30_spmd.clone, body=%wide.region_27.29_spmd.clone.sunk | while | flops 2720266752 | bytes 163650544 | solution.py:303
  4180.8 122.9 %reduce-scatter.7.cloned.1.call-done = bf16[256,6144]{1,0:T(8,128)(2,1)} async-done(((bf16[2048,6144]{1,0:T(8,128)(2,1)}), bf16[256,6144]{1,0:T(8,128)(2,1)}) %reduce-scatter.7.cloned.1.call-update) | async-done | bytes 3145744 | tf_op jit(solution)/shard_map/reduce_scatter | solution.py:338
  4303.8 268.4 %reduce-scatter.11.cloned.1.call-done = bf16[2048,2,704]{0,2,1:T(8,128)(2,1)} async-done(((bf16[2048,2,5632]{0,2,1:T(8,128)(2,1)}), bf16[2048,2,704]{0,2,1:T(8,128)(2,1)}) %reduce-scatter.11.cloned.1.call-update) | async-done | bytes 5767184 | tf_op jit(solution)/shard_map/reduce_scatter | solution.py:253
  4635.6 941.0 %all-reduce.17.cloned.1.call-done = (bf16[256,6144]{1,0:T(8,128)(2,1)}, bf16[256,2048]{1,0:T(8,128)(2,1)}, bf16[2048,2,704]{0,2,1:T(8,128)(2,1)}, bf16[704,2048]...) async-done(((bf16[256,6144]{1,0:T(8,128)(2,1)}, bf16[256,2048]{1,0:T(8,128)(2,1)}, bf16[2048,2,704]{0,2,1:T(8,128)(2,1)}, ...) | async-done | bytes 30146576 | tf_op jit(solution)/shard_map/psum | solution.py:356
  (613 shorter events, 2286.1 us)
Async XLA Ops:
  7.2 130.8 %all-gather.26.cloned.1.call-start = ((), (), s32[]{:S(2)}) async-start(), calls=%async_computation.14 | async-start | bytes 28311552 | tf_op jit(solution)/shard_map/all_gather | solution.py:108
  7.9 309.4 %all-gather.28.cloned.1.call-start = ((), (), s32[]{:S(2)}) async-start(), calls=%async_computation.15 | async-start | bytes 9437184 | tf_op jit(solution)/shard_map/all_gather | solution.py:110
  342.0 114.9 %all-gather.36.cloned.1.call-start = ((), (), s32[]{:S(2)}) async-start(), calls=%async_computation.24 | async-start | bytes 6488064 | tf_op jit(solution)/shard_map/while/body/eval_jaxpr/all_gather | solution.py:72
  464.7 114.1 %all-gather.36.cloned.1.call-start = ((), (), s32[]{:S(2)}) async-start(), calls=%async_computation.24 | async-start | bytes 6488064 | tf_op jit(solution)/shard_map/while/body/eval_jaxpr/all_gather | solution.py:72
  586.6 114.6 %all-gather.36.cloned.1.call-start = ((), (), s32[]{:S(2)}) async-start(), calls=%async_computation.24 | async-start | bytes 6488064 | tf_op jit(solution)/shard_map/while/body/eval_jaxpr/all_gather | solution.py:72
  708.9 114.4 %all-gather.36.cloned.1.call-start = ((), (), s32[]{:S(2)}) async-start(), calls=%async_computation.24 | async-start | bytes 6488064 | tf_op jit(solution)/shard_map/while/body/eval_jaxpr/all_gather | solution.py:72
  831.1 114.4 %all-gather.36.cloned.1.call-start = ((), (), s32[]{:S(2)}) async-start(), calls=%async_computation.24 | async-start | bytes 6488064 | tf_op jit(solution)/shard_map/while/body/eval_jaxpr/all_gather | solution.py:72
  953.2 114.4 %all-gather.36.cloned.1.call-start = ((), (), s32[]{:S(2)}) async-start(), calls=%async_computation.24 | async-start | bytes 6488064 | tf_op jit(solution)/shard_map/while/body/eval_jaxpr/all_gather | solution.py:72
  1197.3 114.1 %all-gather.36.cloned.1.call-start = ((), (), s32[]{:S(2)}) async-start(), calls=%async_computation.24 | async-start | bytes 6488064 | tf_op jit(solution)/shard_map/while/body/eval_jaxpr/all_gather | solution.py:72
  1330.8 171.5 %all-gather.38.cloned.1.call-start = ((), (), s32[]{:S(2)}) async-start(), calls=%async_computation.25 | async-start | bytes 12976128 | tf_op jit(solution)/shard_map/while/body/eval_jaxpr/all_gather | solution.py:71
  1333.5 259.7 %reduce-scatter.15.cloned.1.call-start = ((), (), s32[]{:S(2)}) async-start(), calls=%async_computation.27 | async-start | bytes 12976128 | tf_op jit(solution)/shard_map/while/body/eval_jaxpr/reduce_scatter | solution.py:226
  1603.4 171.5 %all-gather.38.cloned.1.call-start = ((), (), s32[]{:S(2)}) async-start(), calls=%async_computation.25 | async-start | bytes 12976128 | tf_op jit(solution)/shard_map/while/body/eval_jaxpr/all_gather | solution.py:71
  1606.1 259.6 %reduce-scatter.15.cloned.1.call-start = ((), (), s32[]{:S(2)}) async-start(), calls=%async_computation.27 | async-start | bytes 12976128 | tf_op jit(solution)/shard_map/while/body/eval_jaxpr/reduce_scatter | solution.py:226
  1875.8 171.4 %all-gather.38.cloned.1.call-start = ((), (), s32[]{:S(2)}) async-start(), calls=%async_computation.25 | async-start | bytes 12976128 | tf_op jit(solution)/shard_map/while/body/eval_jaxpr/all_gather | solution.py:71
  1878.5 259.4 %reduce-scatter.15.cloned.1.call-start = ((), (), s32[]{:S(2)}) async-start(), calls=%async_computation.27 | async-start | bytes 12976128 | tf_op jit(solution)/shard_map/while/body/eval_jaxpr/reduce_scatter | solution.py:226
  2148.1 171.5 %all-gather.38.cloned.1.call-start = ((), (), s32[]{:S(2)}) async-start(), calls=%async_computation.25 | async-start | bytes 12976128 | tf_op jit(solution)/shard_map/while/body/eval_jaxpr/all_gather | solution.py:71
  2150.8 259.7 %reduce-scatter.15.cloned.1.call-start = ((), (), s32[]{:S(2)}) async-start(), calls=%async_computation.27 | async-start | bytes 12976128 | tf_op jit(solution)/shard_map/while/body/eval_jaxpr/reduce_scatter | solution.py:226
  2420.7 171.4 %all-gather.38.cloned.1.call-start = ((), (), s32[]{:S(2)}) async-start(), calls=%async_computation.25 | async-start | bytes 12976128 | tf_op jit(solution)/shard_map/while/body/eval_jaxpr/all_gather | solution.py:71
  2423.4 259.6 %reduce-scatter.15.cloned.1.call-start = ((), (), s32[]{:S(2)}) async-start(), calls=%async_computation.27 | async-start | bytes 12976128 | tf_op jit(solution)/shard_map/while/body/eval_jaxpr/reduce_scatter | solution.py:226
  2693.2 171.4 %all-gather.38.cloned.1.call-start = ((), (), s32[]{:S(2)}) async-start(), calls=%async_computation.25 | async-start | bytes 12976128 | tf_op jit(solution)/shard_map/while/body/eval_jaxpr/all_gather | solution.py:71
  2695.9 259.6 %reduce-scatter.15.cloned.1.call-start = ((), (), s32[]{:S(2)}) async-start(), calls=%async_computation.27 | async-start | bytes 12976128 | tf_op jit(solution)/shard_map/while/body/eval_jaxpr/reduce_scatter | solution.py:226
  2965.6 171.2 %all-gather.38.cloned.1.call-start = ((), (), s32[]{:S(2)}) async-start(), calls=%async_computation.25 | async-start | bytes 12976128 | tf_op jit(solution)/shard_map/while/body/eval_jaxpr/all_gather | solution.py:71
  2968.3 259.2 %reduce-scatter.15.cloned.1.call-start = ((), (), s32[]{:S(2)}) async-start(), calls=%async_computation.27 | async-start | bytes 12976128 | tf_op jit(solution)/shard_map/while/body/eval_jaxpr/reduce_scatter | solution.py:226
  3237.7 171.1 %all-gather.38.cloned.1.call-start = ((), (), s32[]{:S(2)}) async-start(), calls=%async_computation.25 | async-start | bytes 12976128 | tf_op jit(solution)/shard_map/while/body/eval_jaxpr/all_gather | solution.py:71
  3240.4 259.2 %reduce-scatter.15.cloned.1.call-start = ((), (), s32[]{:S(2)}) async-start(), calls=%async_computation.27 | async-start | bytes 12976128 | tf_op jit(solution)/shard_map/while/body/eval_jaxpr/reduce_scatter | solution.py:226
  3502.3 216.6 %all-gather.30.cloned.1.call-start = ((), (), s32[]{:S(2)}) async-start(), calls=%async_computation.16 | async-start | bytes 51904512 | tf_op jit(solution)/shard_map/all_gather | solution.py:165
  3502.8 334.4 %all-gather.32.cloned.1.call-start = ((), (), s32[]{:S(2)}) async-start(), calls=%async_computation.17 | async-start | bytes 25952256 | tf_op jit(solution)/shard_map/all_gather | solution.py:166
  3503.6 677.2 %reduce-scatter.9.cloned.1.call-start = ((), (), s32[]{:S(2)}) async-start(), calls=%async_computation.19 | async-start | bytes 9437184 | tf_op jit(solution)/shard_map/reduce_scatter | solution.py:344
  3900.7 280.1 %reduce-scatter.13.cloned.1.call-start = ((), (), s32[]{:S(2)}) async-start(), calls=%async_computation.21 | async-start | bytes 25952256 | tf_op jit(solution)/shard_map/reduce_scatter | solution.py:256
  4096.3 207.5 %reduce-scatter.7.cloned.1.call-start = ((), (), s32[]{:S(2)}) async-start(), calls=%async_computation.18 | async-start | bytes 28311552 | tf_op jit(solution)/shard_map/reduce_scatter | solution.py:338
  4148.2 423.9 %reduce-scatter.11.cloned.1.call-start = ((), (), s32[]{:S(2)}) async-start(), calls=%async_computation.20 | async-start | bytes 51904512 | tf_op jit(solution)/shard_map/reduce_scatter | solution.py:253
  4180.5 1396.2 %all-reduce.17.cloned.1.call-start = ((), (), s32[]{:S(2)}) async-start(), calls=%async_computation.22 | async-start | bytes 60293120 | tf_op jit(solution)/shard_map/psum | solution.py:356
  (109 other events, 3792.6 us)
Sparse Core Ops, SparseCore 0:
  9.9 128.0 all-gather.25
  342.9 68.1 all-gather.33
  465.2 67.6 all-gather.33
  587.5 67.6 all-gather.33
  709.8 67.6 all-gather.33
  831.9 67.6 all-gather.33
  954.1 67.6 all-gather.33
  1076.0 67.6 all-gather.33
  1197.8 67.6 all-gather.33
  1434.6 67.6 all-gather.37
  1506.4 86.7 reduce-scatter.14
  1707.2 67.6 all-gather.37
  1778.8 86.8 reduce-scatter.14
  1979.5 67.6 all-gather.37
  2051.1 86.7 reduce-scatter.14
  2251.9 67.6 all-gather.37
  2323.7 86.7 reduce-scatter.14
  2524.4 67.6 all-gather.37
  2596.2 86.7 reduce-scatter.14
  2796.8 67.6 all-gather.37
  2868.6 86.7 reduce-scatter.14
  3069.1 67.6 all-gather.37
  3140.7 86.7 reduce-scatter.14
  3341.1 67.6 all-gather.37
  3412.9 86.7 reduce-scatter.14
  3504.7 214.0 all-gather.29
  3720.7 116.4 all-gather.31
  3900.8 71.2 reduce-scatter.8
  3976.8 145.9 reduce-scatter.12
  4148.4 155.3 reduce-scatter.6
  4307.8 264.3 reduce-scatter.10
  4576.6 999.9 all-reduce.16
  (25 shorter events, 1218.2 us)
where the time goes:
time: 5630 us; the launch traced here: 5620 us
  waiting for transfers between devices  4470 us (79%)
  matrix products  582 us (10%)
  local copies, waits for them, and re-layouts  227 us (4%)
  other arithmetic  148 us (3%)
  blocking collectives  130 us (2%)
    all_gather x16, waiting for transfers between devices, expert_weights(): lax.all_gather(gate_up_piece, 'fsdp', axis=0, tiled=True)  1070 us
    psum x1, waiting for transfers between devices, on_device(): lax.psum(shard_qkv.astype(jnp.bfloat16), 'seq').astype(jnp.float32)  941 us
    reduce_scatter x8, waiting for transfers between devices, expert_backward(): lax.psum_scatter(grad_up_full.astype(jnp.bfloat16), 'fsdp', scatter_dimen...  652 us
    all_gather x16, waiting for transfers between devices, expert_weights(): lax.all_gather(down_piece, 'fsdp', axis=0, tiled=True)  566 us
    reduce_scatter x8, waiting for transfers between devices, expert_backward(): lax.psum_scatter(grad_down_full.astype(jnp.bfloat16), 'fsdp', scatter_dim...  396 us
    reduce_scatter x1, waiting for transfers between devices, on_device(): lax.psum_scatter(full_gate_up.astype(jnp.bfloat16), 'fsdp', scatter_dimen...  268 us
    all_gather x1, waiting for transfers between devices, on_device(): lax.all_gather(shared_gate_up, 'fsdp', axis=2, tiled=True)  135 us
    reduce_scatter x1, waiting for transfers between devices, on_device(): lax.psum_scatter(grad_weight_qkv.astype(jnp.bfloat16), 'fsdp', scatter_di...  123 us
  transfers between devices with their start and end apart: 64, of which 59 were waited for; matrix products, arithmetic and copies ran while one was open for 13% of the time, Pallas kernels for 0%

commit v1 on v0

v1 whole, which is shorter than its diff:
```python
import math

import jax
import jax.numpy as jnp
from jax import lax
from jax.sharding import PartitionSpec as P

D = 2048
HEADS = 16
HEAD_DIM = 128
FF_EXPERT = 1408
TOP = 4
EXPERTS = 8
QBLOCK = 256
DOC_MOST = 512

EPSILON = 1e-06
THETA = 1000000.0

bf16 = jnp.bfloat16
f32 = jnp.float32


def dot(a, b, contract, kind=f32):
    return lax.dot_general(a, b, (contract, ((), ())), preferred_element_type=f32).astype(kind)


def rms_scale(values):
    return lax.rsqrt(jnp.mean(values * values, axis=-1, keepdims=True) + EPSILON)


def norm_back(values, scale, gain, grad):
    scaled = grad * gain
    centre = jnp.mean(scaled * values, axis=-1, keepdims=True)
    return scale * (scaled - values * (scale * scale) * centre)


def rope_tables(positions):
    steps_half = jnp.arange(HEAD_DIM // 2, dtype=jnp.int32).astype(f32)
    frequency = jnp.exp(steps_half * (-2.0 * math.log(THETA) / HEAD_DIM))
    angles = positions.astype(f32)[:, None] * frequency[None, :]
    angles = jnp.concatenate([angles, angles], axis=-1)
    return (jnp.cos(angles), jnp.sin(angles))


def rotate(rows, cosine, sine):
    middle = rows.shape[-1] // 2
    turned = jnp.concatenate([-rows[..., middle:], rows[..., :middle]], axis=-1)
    return rows * cosine[:, None, :] + turned * sine[:, None, :]


def rotate_back(rows, cosine, sine):
    middle = rows.shape[-1] // 2
    turned = rows * sine[:, None, :]
    turned = jnp.concatenate([turned[..., middle:], -turned[..., :middle]], axis=-1)
    return rows * cosine[:, None, :] + turned


def key_start(block):
    return max(0, block * QBLOCK - DOC_MOST)


def block_scores(block, queries, keys, documents, factor):
    first, start = block * QBLOCK, key_start(block)
    stop = first + QBLOCK
    scores = (
        jnp.einsum(
            "qhd,khd->hqk", queries[first:stop], keys[start:stop], preferred_element_type=f32
        )
        * factor
    )
    rows = first + jnp.arange(QBLOCK, dtype=jnp.int32)
    columns = start + jnp.arange(stop - start, dtype=jnp.int32)
    allowed = (rows[:, None] >= columns[None, :]) & (
        documents[first:stop, None] == documents[None, start:stop]
    )
    return jnp.where(allowed[None], scores, -1e30)


def attend(queries, keys, values, documents, factor):
    mixed, logs = [], []
    for block in range(queries.shape[0] // QBLOCK):
        start, stop = key_start(block), (block + 1) * QBLOCK
        scores = block_scores(block, queries, keys, documents, factor)
        top = jnp.max(scores, axis=-1, keepdims=True)
        weights = jnp.exp(scores - top)
        totals = jnp.sum(weights, axis=-1, keepdims=True)
        probability = (weights / totals).astype(bf16)
        mixed.append(
            jnp.einsum(
                "hqk,khd->qhd", probability, values[start:stop], preferred_element_type=f32
            ).astype(bf16)
        )
        logs.append(top + jnp.log(totals))
    return jnp.concatenate(mixed, axis=0), logs


def attend_back(queries, keys, values, documents, factor, logs, grads):
    length = queries.shape[0]
    grad_queries = []
    grad_keys = jnp.zeros(keys.shape, f32)
    grad_values = jnp.zeros(values.shape, f32)
    for block in range(length // QBLOCK):
        start, stop = key_start(block), (block + 1) * QBLOCK
        scores = block_scores(block, queries, keys, documents, factor)
        probability = jnp.exp(scores - logs[block])
        grad_block = grads[block * QBLOCK : stop]
        query_block = queries[block * QBLOCK : stop]
        grad_values = grad_values.at[start:stop].add(
            jnp.einsum(
                "hqk,qhd->khd", probability.astype(bf16), grad_block, preferred_element_type=f32
            )
        )
        grad_probability = jnp.einsum(
            "qhd,khd->hqk", grad_block, values[start:stop], preferred_element_type=f32
        )
        centre = jnp.sum(grad_probability * probability, axis=-1, keepdims=True)
        grad_scores = (probability * (grad_probability - centre)).astype(bf16)
        grad_queries.append(
            jnp.einsum("hqk,khd->qhd", grad_scores, keys[start:stop], preferred_element_type=f32)
            * factor
        )
        grad_keys = grad_keys.at[start:stop].add(
            jnp.einsum("hqk,qhd->khd", grad_scores, query_block, preferred_element_type=f32)
            * factor
        )
    return jnp.concatenate(grad_queries, axis=0), grad_keys, grad_values


def sum_seq(value):
    return lax.psum(value.astype(bf16), "seq").astype(f32)


def on_device(
    tokens,
    segments,
    expert_ids,
    expert_gates,
    attn_gain,
    qkv_weight,
    qkv_bias,
    out_weight,
    ffn_gain,
    shared_gate_up,
    shared_down,
    shared_gate,
    expert_gate_up,
    expert_down,
    cotangent,
):
    fsdp, seq = lax.axis_size("fsdp"), lax.axis_size("seq")
    me, place = lax.axis_index("fsdp"), lax.axis_index("seq")
    row_count, length = tokens.shape[1], segments.shape[1]
    heads = HEADS // seq
    copies = fsdp // EXPERTS
    width = D // fsdp
    hidden_own = FF_EXPERT // copies
    piece = hidden_own // fsdp
    factor = 1.0 / math.sqrt(HEAD_DIM)
    capacity = length * TOP // EXPERTS

    vectors = jnp.concatenate([attn_gain, ffn_gain, shared_gate, qkv_bias])
    vectors = lax.all_gather(vectors, "fsdp", axis=0)
    gain_one = vectors[:, :width].reshape(D).astype(f32)
    gain_two = vectors[:, width : 2 * width].reshape(D).astype(f32)
    gate_vector = vectors[:, 2 * width : 3 * width].reshape(D)
    bias = vectors[:, 3 * width :].reshape(3, seq, heads * HEAD_DIM)
    bias = lax.dynamic_index_in_dim(bias, place, 1, keepdims=False).reshape(-1).astype(f32)

    all_tokens = lax.all_gather(tokens[0], "seq", axis=0, tiled=True)
    weight_qkv = qkv_weight.reshape(width, 3, seq, heads * HEAD_DIM)
    weight_qkv = lax.dynamic_index_in_dim(weight_qkv, place, 2, keepdims=False)
    weight_qkv = lax.all_gather(
        weight_qkv.reshape(width, 3 * heads * HEAD_DIM), "fsdp", axis=0, tiled=True
    )
    weight_out = lax.all_gather(out_weight, "fsdp", axis=0, tiled=True)
    upstream_all = lax.all_gather(cotangent[0], "fsdp", axis=0, tiled=True)

    up_sent = expert_gate_up.reshape(EXPERTS, width, 2, fsdp, copies, piece)
    up_sent = up_sent.transpose(0, 4, 1, 2, 3, 5).reshape(fsdp, width, 2 * hidden_own)
    weight_up = lax.all_to_all(up_sent, "fsdp", 0, 0, tiled=True).reshape(D, 2 * hidden_own)
    down_sent = expert_down.reshape(fsdp, piece, D)
    weight_down = lax.all_to_all(down_sent, "fsdp", 0, 0, tiled=True).reshape(hidden_own, D)

    x_all = all_tokens.astype(f32)
    normed_unit = x_all * rms_scale(x_all)
    normed = (normed_unit * gain_one).astype(bf16)
    cosine, sine = rope_tables(jnp.arange(length, dtype=jnp.int32))
    joined = dot(normed, weight_qkv, ((1,), (0,))) + bias
    split = joined.reshape(length, 3, heads, HEAD_DIM)
    queries = rotate(split[:, 0], cosine, sine).astype(bf16)
    keys = rotate(split[:, 1], cosine, sine).astype(bf16)
    values = split[:, 2].astype(bf16)
    documents = segments[0]
    mixed, logs = attend(queries, keys, values, documents, factor)
    mixed_rows = lax.all_to_all(mixed, "seq", 0, 1, tiled=True).reshape(row_count, D)
    inputs = tokens[0].astype(f32)
    hidden = inputs + dot(mixed_rows, weight_out, ((1,), (0,)))
    scale_two = rms_scale(hidden)
    second = (hidden * scale_two * gain_two).astype(bf16)
    second_all = lax.all_gather(second, "fsdp", axis=0, tiled=True)

    names = jnp.arange(EXPERTS, dtype=jnp.int32)
    matches = expert_ids[0][:, :, None] == names[None, None, :]
    chosen = jnp.sum(matches.astype(jnp.int32), axis=1)
    earlier = jnp.cumsum(chosen, axis=0) - chosen
    tallies = lax.all_gather(jnp.sum(chosen, axis=0), "seq")
    before = jnp.arange(seq, dtype=jnp.int32)[:, None] < place
    offsets = jnp.sum(jnp.where(before, tallies, 0), axis=0)
    retained = (chosen > 0) & (offsets[None, :] + earlier < capacity)
    portion = jnp.sum(
        jnp.where(matches, expert_gates[0][:, :, None], 0.0), axis=1
    ) * retained.astype(f32)
    portion_all = lax.all_gather(portion, "fsdp", axis=0, tiled=True)
    own_expert = (names == me // copies).astype(f32)
    share = jnp.sum(portion_all * own_expert[None, :], axis=1, keepdims=True)

    def expert(weight_gate, weight_lift, weight_back, scale):
        gate = dot(second_all, weight_gate, ((1,), (0,)))
        lift = dot(second_all, weight_lift, ((1,), (0,)))
        raw = dot(upstream_all, weight_back, ((1,), (1,)))
        sigma = jax.nn.sigmoid(gate)
        silu = gate * sigma
        inner = silu * lift
        reach = jnp.sum(inner * raw, axis=1)
        inner = (inner * scale).astype(bf16)
        grad = raw * scale
        grad_gate = (grad * lift * sigma * (1.0 + gate * (1.0 - sigma))).astype(bf16)
        grad_lift = (grad * silu).astype(bf16)
        return inner, grad_gate, grad_lift, reach

    opening_all = jax.nn.sigmoid(dot(second_all, gate_vector, ((1,), (0,))))[:, None]
    s_gate, s_lift = shared_gate_up[:, 0], shared_gate_up[:, 1]
    inner_s, ga_s, gl_s, reach = expert(s_gate, s_lift, shared_down, opening_all)
    grad_s_down = dot(inner_s, upstream_all, ((0,), (0,)), bf16)
    grad_s_up = jnp.stack(
        [dot(second_all, ga_s, ((0,), (0,)), bf16), dot(second_all, gl_s, ((0,), (0,)), bf16)],
        axis=1,
    )
    e_gate, e_lift = weight_up[:, :hidden_own], weight_up[:, hidden_own:]
    inner_e, ga_e, gl_e, _ = expert(e_gate, e_lift, weight_down, share)

    grad_second_all = (
        dot(ga_s, s_gate, ((1,), (1,)))
        + dot(gl_s, s_lift, ((1,), (1,)))
        + dot(ga_e, e_gate, ((1,), (1,)))
        + dot(gl_e, e_lift, ((1,), (1,)))
    ).astype(bf16)
    grad_second = lax.psum_scatter(
        grad_second_all, "fsdp", scatter_dimension=0, tiled=True
    ).astype(f32)
    reach = lax.psum_scatter(reach, "fsdp", scatter_dimension=0, tiled=True)

    grad_e_down = dot(inner_e, upstream_all, ((0,), (0,)), bf16)
    grad_e_up = jnp.concatenate(
        [dot(second_all, ga_e, ((0,), (0,)), bf16), dot(second_all, gl_e, ((0,), (0,)), bf16)],
        axis=1,
    )
    grad_e_up = lax.all_to_all(
        grad_e_up.reshape(fsdp, width, 2 * hidden_own), "fsdp", 0, 0, tiled=True
    )
    grad_e_up = grad_e_up.reshape(EXPERTS, copies, width, 2, fsdp, piece)
    grad_e_up = grad_e_up.transpose(0, 2, 3, 4, 1, 5).reshape(EXPERTS, width, 2 * FF_EXPERT)
    grad_e_down = lax.all_to_all(
        grad_e_down.reshape(fsdp, piece, D), "fsdp", 0, 0, tiled=True
    ).reshape(EXPERTS, copies * piece, D)

    out_all = (
        dot(inner_s, shared_down, ((1,), (0,))) + dot(inner_e, weight_down, ((1,), (0,)))
    ).astype(bf16)
    out_part = lax.psum_scatter(out_all, "fsdp", scatter_dimension=0, tiled=True)
    output = (hidden + out_part.astype(f32)).astype(bf16)

    upstream = cotangent[0].astype(f32)
    opening = jax.nn.sigmoid(dot(second, gate_vector, ((1,), (0,))))
    grad_logit = reach * opening * (1.0 - opening)
    grad_second = grad_second + grad_logit[:, None] * gate_vector.astype(f32)[None, :]
    grad_gate_vector = jnp.sum(grad_logit[:, None] * second.astype(f32), axis=0)
    grad_hidden = upstream + norm_back(hidden, scale_two, gain_two, grad_second)
    grad_gain_two = jnp.sum(grad_second * hidden * scale_two, axis=0)
    grad_projected = grad_hidden.astype(bf16)
    grad_mixture = dot(grad_projected, weight_out, ((1,), (1,)), bf16)
    grad_heads = lax.all_to_all(
        grad_mixture.reshape(row_count, HEADS, HEAD_DIM), "seq", 1, 0, tiled=True
    )
    grad_out = dot(mixed_rows, grad_projected, ((0,), (0,)), bf16)
    grad_out = lax.psum_scatter(grad_out, "fsdp", scatter_dimension=0, tiled=True)

    grad_queries, grad_keys, grad_values = attend_back(
        queries, keys, values, documents, factor, logs, grad_heads
    )
    grad_joined = jnp.stack(
        [
            rotate_back(grad_queries.astype(bf16).astype(f32), cosine, sine),
            rotate_back(grad_keys.astype(bf16).astype(f32), cosine, sine),
            grad_values,
        ],
        axis=1,
    )
    grad_joined = grad_joined.reshape(length, 3 * heads * HEAD_DIM).astype(bf16)
    grad_normed_all = dot(grad_joined, weight_qkv, ((1,), (1,)))
    grad_gain_one = jnp.sum(grad_normed_all * normed_unit, axis=0)
    grad_normed = lax.psum_scatter(
        grad_normed_all.astype(bf16), "seq", scatter_dimension=0, tiled=True
    ).astype(f32)
    input_grad = (grad_hidden + norm_back(inputs, rms_scale(inputs), gain_one, grad_normed)).astype(
        bf16
    )

    grad_qkv = dot(normed, grad_joined, ((0,), (0,)), bf16)
    grad_qkv = lax.psum_scatter(grad_qkv, "fsdp", scatter_dimension=0, tiled=True)
    grad_qkv = lax.all_gather(grad_qkv.reshape(width, 3, heads * HEAD_DIM), "seq", axis=2)
    grad_qkv = grad_qkv.reshape(width, 3 * D).astype(f32)

    grad_bias = jnp.sum(grad_joined.astype(f32), axis=0).reshape(3, 1, heads * HEAD_DIM)
    own_heads = (jnp.arange(seq, dtype=jnp.int32) == place).astype(f32)
    grad_bias = (grad_bias * own_heads[None, :, None]).reshape(fsdp, 3 * D // fsdp)
    small = jnp.concatenate(
        [
            grad_gain_one.reshape(fsdp, width),
            grad_gain_two.reshape(fsdp, width),
            grad_gate_vector.reshape(fsdp, width),
            grad_bias,
        ],
        axis=1,
    )
    small = lax.psum(small, ("seq", "fsdp"))
    small = lax.dynamic_index_in_dim(small, me, 0, keepdims=False)

    return (
        output[None],
        input_grad[None],
        small[:width],
        grad_qkv,
        small[3 * width :],
        sum_seq(grad_out),
        small[width : 2 * width],
        sum_seq(grad_s_up),
        sum_seq(grad_s_down),
        small[2 * width : 3 * width],
        sum_seq(grad_e_up),
        sum_seq(grad_e_down),
    )


def solution(mesh):
    return jax.shard_map(
        on_device,
        mesh=mesh,
        in_specs=(
            P("fsdp", "seq", None),
            P("fsdp", None),
            P("fsdp", "seq", None),
            P("fsdp", "seq", None),
            P("fsdp"),
            P("fsdp", None),
            P("fsdp"),
            P("fsdp", None),
            P("fsdp"),
            P(None, None, "fsdp"),
            P("fsdp", None),
            P("fsdp"),
            P(None, "fsdp", None),
            P(None, "fsdp", None),
            P("fsdp", "seq", None),
        ),
        out_specs=(
            P("fsdp", "seq", None),
            P("fsdp", "seq", None),
            P("fsdp"),
            P("fsdp", None),
            P("fsdp"),
            P("fsdp", None),
            P("fsdp"),
            P(None, None, "fsdp"),
            P("fsdp", None),
            P("fsdp"),
            P(None, "fsdp", None),
            P(None, "fsdp", None),
        ),
        check_vma=False,
    )
```

time: 5630 us -> 2180 us (0.39)
  waiting for transfers between devices: 4470 us -> 1340 us
  matrix products: 582 us -> 371 us
  local copies, waits for them, and re-layouts: 227 us -> 79.4 us
  blocking collectives: 130 us -> 240 us
    all_gather x36 -> x6, waiting for transfers between devices: 1970 us -> 166 us  [the longest x1 60.8 us: on_device(): lax.all_gather(grad_qkv.reshape(width, 3, heads * HEAD_DIM), 'seq', axis=2)]
    reduce_scatter x20 -> x5, waiting for transfers between devices: 1440 us -> 102 us  [the longest x1 72.4 us: on_device(): lax.psum_scatter(out_all, 'fsdp', scatter_dimension=0, tiled=True)]
    dot_general x76 -> x50, matrix products: 582 us -> 371 us  [the longest x26 348 us: dot(): lax.dot_general(a, b, (contract, ((), ())), preferred_element_type=f32)]
    all_gather x4 -> x2, blocking collectives: 37.1 us -> 174 us  [the longest x1 163 us: on_device(): portion_all = lax.all_gather(portion, 'fsdp', axis=0, tiled=True)]
    dynamic_slice x40 -> x1, local copies, waits for them, and re-layouts: 76.9 us -> 2.1 us  [on_device(): weight_qkv = lax.dynamic_index_in_dim(weight_qkv, place, 2, keepdims=False)]
    gather x8 -> x0, local copies, waits for them, and re-layouts: 73.8 us -> none  [the longest x2 25.8 us: on_device(): expert_grad_inputs.reshape(EXPERTS * slot_count, D)[flat_index]]
    all_to_all x7 -> x6, waiting for transfers between devices: 116 us -> 184 us  [the longest x1 129 us: on_device(): lax.all_to_all(grad_e_up.reshape(fsdp, width, 2 * hidden_own), 'fsdp', 0,...]
    psum x1, waiting for transfers between devices: 941 us -> 883 us  [sum_seq(): return lax.psum(value.astype(bf16), 'seq').astype(f32)]
  transfers between devices with their start and end apart: 64 -> 18, of which waited for: 59 -> 11; matrix products, arithmetic and copies ran while one was open for 13% -> 17% of each run, Pallas kernels for 0% -> 0%
where the time goes in v1:
time: 2180 us; the launch traced here: 2170 us
  waiting for transfers between devices  1340 us (61%)
  matrix products  371 us (17%)
  blocking collectives  240 us (11%)
  other arithmetic  93.4 us (4%)
  local copies, waits for them, and re-layouts  79.4 us (4%)
  starting transfers between devices  29.9 us (1%)
    psum x1, waiting for transfers between devices, sum_seq(): return lax.psum(value.astype(bf16), 'seq').astype(f32)  883 us
    dot_general x26, matrix products, dot(): lax.dot_general(a, b, (contract, ((), ())), preferred_element_type=f32)  348 us
    all_gather x1, blocking collectives, on_device(): portion_all = lax.all_gather(portion, 'fsdp', axis=0, tiled=True)  163 us
    all_to_all x1, waiting for transfers between devices, on_device(): lax.all_to_all(grad_e_up.reshape(fsdp, width, 2 * hidden_own), 'fsdp', 0,...  129 us
    reduce_scatter x1, waiting for transfers between devices, on_device(): lax.psum_scatter(out_all, 'fsdp', scatter_dimension=0, tiled=True)  72.4 us
    all_gather x1, waiting for transfers between devices, on_device(): lax.all_gather(grad_qkv.reshape(width, 3, heads * HEAD_DIM), 'seq', axis=2)  60.8 us
    all_gather x1, waiting for transfers between devices, on_device(): all_tokens = lax.all_gather(tokens[0], 'seq', axis=0, tiled=True)  60.4 us
    psum x1, blocking collectives, on_device(): small = lax.psum(small, ('seq', 'fsdp'))  45.1 us
  transfers between devices with their start and end apart: 18, of which 11 were waited for; matrix products, arithmetic and copies ran while one was open for 17% of the time, Pallas kernels for 0%

profile of v1, /device:TPU:0, one launch (start us, length us, event | category | flops | bytes accessed | tf_op | source)
XLA Modules:
  0.0 2168.1 jit_solution(9530302432232517153)
XLA Ops:
  32.7 60.4 %all-gather.20.cloned.1.call-done = bf16[1,1024,2048]{2,1,0:T(8,128)(2,1)} async-done(((bf16[1,256,2048]{2,1,0:T(8,128)(2,1)}), bf16[1,1024,2048]{2,1,0:T(8,128)(2,1)}) %all-gather.20.cloned.1.call-update) | async-done | bytes 4194320 | tf_op jit(solution)/shard_map/all_gather | solution.py:170
  96.2 44.6 %all-gather.12.cloned.1.call-done = bf16[2048,1536]{0,1:T(8,128)(2,1)} async-done(((bf16[256,1536]{0,1:T(8,128)(2,1)}), bf16[2048,1536]{0,1:T(8,128)(2,1)}) %all-gather.12.cloned.1.call-update) | async-done | bytes 6291472 | tf_op jit(solution)/shard_map/all_gather | solution.py:173
  140.8 11.8 convolution_add_fusion
  190.8 26.1 %all-to-all-done = bf16[1024,4,128]{2,1,0:T(4,128)(2,1)} async-done(((bf16[1024,4,128]{2,1,0:T(4,128)(2,1)}), bf16[1024,4,128]{2,1,0:T(4,128)(2,1)}, u32[]{:S(2)}, u32[]{:S(2)}) %all-to-all-start) | async-done | bytes 1048608 | tf_op jit(solution)/shard_map/all_to_all | solution.py:196
  245.6 163.2 %all_gather.41 = f32[2048,8]{0,1:T(8,128)S(1)} all-gather(f32[256,8]{0,1:T(8,128)S(1)} %fusion.138), channel_id=1, replica_groups=mesh['seq'=4,'fsdp'=8] {'fsdp'}, dimensions={0}, use_global_device_ids=true | all-gather | bytes 73728 | tf_op jit(solution)/shard_map/all_gather | solution.py:214
  439.2 18.7 fusion.19
  457.9 15.8 multiply_reduce_fusion
  473.7 14.2 fusion.30
  487.9 12.5 fusion.34
  500.4 17.0 fusion.23
  517.4 26.3 %multiply_convert_fusion = (bf16[2048,1408]{1,0:T(8,128)(2,1)}, bf16[2048,1408]{1,0:T(8,128)(2,1)}, bf16[2048,1408]{1,0:T(8,128)(2,1)}) fusion(f32[2048]{0:T(1024)S(1)} %copy-done.69, f32[2048,1408]{1,0:T(8,128)} %fusion.23, f32[2048,1408]{1,0:T(8,128)} %fusion.19, bf16[1408,2048]{1,0:T(8,128)(2,1)} %bitcast.34, ...), kind=kOutput, calls=%fused_computation.3 | convolution fusion | flops 11860180992 | bytes 54534144 | tf_op jit(solution)/shard_map/dot_general | solution.py:25
  543.7 20.1 fusion.21
  563.7 26.1 %add_convert_fusion = bf16[2048,2048]{1,0:T(8,128)(2,1)} fusion(f32[2048,2048]{1,0:T(8,128)} %fusion.21, f32[2048,2048]{1,0:T(8,128)} %fusion.34, f32[2048,2048]{1,0:T(8,128)} %fusion.30, bf16[2048,1408]{1,0:T(8,128)(2,1)S(1)} %copy-done.85, bf16[2048,2816]{1,0:T(8,128)(2,1)} %bitcast.26), kind=kOutput, calls=%fused_computation | convolution fusion | flops 11827937280 | bytes 70254592 | tf_op jit(solution)/shard_map/dot_general | solution.py:25
  589.9 14.2 fusion.151
  604.0 21.6 add_convert_fusion.1
  629.2 15.0 all-reduce.3
  644.3 15.9 reduce-scatter.8.cloned.1.call-done
  663.6 72.4 %reduce-scatter.6.cloned.1.call-done = bf16[256,2048]{1,0:T(8,128)(2,1)} async-done(((bf16[2048,2048]{1,0:T(8,128)(2,1)}), bf16[256,2048]{1,0:T(8,128)(2,1)}) %reduce-scatter.6.cloned.1.call-update) | async-done | bytes 1048592 | tf_op jit(solution)/shard_map/reduce_scatter | solution.py:271
  752.4 25.6 %all-to-all-done.3 = bf16[256,16,128]{2,0,1:T(8,128)(2,1)S(1)} async-done(((bf16[256,16,128]{2,0,1:T(8,128)(2,1)}), bf16[256,16,128]{2,0,1:T(8,128)(2,1)S(1)}, u32[]{:S(2)}, u32[]{:S(2)}) %all-to-all-start.3) | async-done | bytes 1048608 | tf_op jit(solution)/shard_map/all_to_all | solution.py:283
  811.9 12.4 convolution_convert_fusion.1
  833.7 19.0 fusion.14
  857.6 12.4 fusion.4
  870.1 16.5 convolution_convert_fusion.2
  886.5 16.5 convolution_convert_fusion.3
  903.1 13.6 pad_maximum_fusion
  916.7 16.0 copy.326
  974.7 128.7 %all-to-all-done.4 = bf16[8,256,2816]{2,1,0:T(8,128)(2,1)} async-done(((bf16[8,256,2816]{2,1,0:T(8,128)(2,1)}), bf16[8,256,2816]{2,1,0:T(8,128)(2,1)}, u32[]{:S(2)}, u32[]{:S(2)}) %all-to-all-start.4) | async-done | bytes 11534368 | tf_op jit(solution)/shard_map/all_to_all | solution.py:259
  1104.2 45.1 %psum.42 = f32[8,1536]{1,0:T(8,128)S(1)} all-reduce(f32[8,1536]{1,0:T(8,128)S(1)} %pad_maximum_fusion.4), channel_id=1, replica_groups=mesh['seq'=4,'fsdp'=8] {'seq','fsdp'}, use_global_device_ids=true, to_apply=%region_33.34 | all-reduce | flops 12288 | bytes 98304 | tf_op jit(solution)/shard_map/psum | solution.py:327
  1150.7 13.7 reduce-scatter.10.cloned.1.call-done
  1169.8 60.8 %all-gather.18.cloned.1.call-done = bf16[256,3,4,512]{3,0,1,2:T(8,128)(2,1)} async-done(((bf16[256,3,1,512]{3,0,1,2:T(8,128)(2,1)}), bf16[256,3,4,512]{3,0,1,2:T(8,128)(2,1)}) %all-gather.18.cloned.1.call-update) | async-done | bytes 3145744 | tf_op jit(solution)/shard_map/all_gather | solution.py:312
  1247.5 882.8 %all-reduce.7.cloned.1.call-done = (bf16[256,2048]{1,0:T(8,128)(2,1)}, bf16[2048,2,704]{0,2,1:T(8,128)(2,1)}, bf16[704,2048]{1,0:T(8,128)(2,1)}, bf16[8,256,2816]{2,1,0:T(8,128)(2,1)}, bf16[8,176,2048]{2,1,0:T(8,128)(2,1)}) async-done(((bf16[256,2048]{1,0:T(8,128)(2,1)}, bf16[2048,2,704]{0,2,1:T(8,128)(2,1)}, bf16[704,2048]{1,0:T(8,128)(2,1)}, bf16[8,256,2816]{2,1,0:T(8,128)(2,1)}, ...) | async-done | bytes 27000848 | tf_op jit(solution)/shard_map/psum | solution.py:131
  2130.3 13.2 convert_element_type.364
  (374 shorter events, 278.6 us)
Async XLA Ops:
  7.2 450.7 %copy-start = (bf16[704,2048]{1,0:T(8,128)(2,1)S(1)}, bf16[704,2048]{1,0:T(8,128)(2,1)}, u32[]{:S(2)}) copy-start(bf16[704,2048]{1,0:T(8,128)(2,1)} %param.41) | copy-start | bytes 8650756
  7.2 85.9 %all-gather.20.cloned.1.call-start = ((), (), s32[]{:S(2)}) async-start(), calls=%async_computation.20 | async-start | bytes 5242880 | tf_op jit(solution)/shard_map/all_gather | solution.py:170
  7.9 132.8 %all-gather.12.cloned.1.call-start = ((), (), s32[]{:S(2)}) async-start(), calls=%async_computation.11 | async-start | bytes 7077888 | tf_op jit(solution)/shard_map/all_gather | solution.py:173
  14.8 207.1 %all-gather.14.cloned.1.call-start = ((), (), s32[]{:S(2)}) async-start(), calls=%async_computation.12 | async-start | bytes 9437184 | tf_op jit(solution)/shard_map/all_gather | solution.py:176
  27.6 113.2 %copy-start.37 = (f32[1,2,8,128]{3,1,2,0:T(2,128)}, f32[1,2,8,128]{3,1,2,0:T(2,128)S(1)}, u32[]{:S(2)}) copy-start(f32[1,2,8,128]{3,1,2,0:T(2,128)S(1)} %copy.331) | copy-start | bytes 24580
  30.6 140.5 %copy-start.21 = (f32[1024,128]{1,0:T(8,128)}, f32[1024,128]{1,0:T(8,128)S(1)}, u32[]{:S(2)}) copy-start(f32[1024,128]{1,0:T(8,128)S(1)} %get-tuple-element.197) | copy-start | bytes 1572868
  96.2 56.4 %copy-start.71 = (f32[1024]{0:T(1024)}, f32[1024]{0:T(1024)S(1)}, u32[]{:S(2)}) copy-start(f32[1024]{0:T(1024)S(1)} %add_rsqrt_fusion) | copy-start | bytes 12292
  186.2 30.7 %all-to-all-start = ((bf16[1024,4,128]{2,1,0:T(4,128)(2,1)}), bf16[1024,4,128]{2,1,0:T(4,128)(2,1)}, u32[]{:S(2)}, u32[]{:S(2)}) async-start(bf16[1024,4,128]{2,1,0:T(4,128)(2,1)} %copy.253), calls=%async_computation | async-start | bytes 2097152 | tf_op jit(solution)/shard_map/all_to_all | solution.py:196
  190.8 218.7 %all-gather.16.cloned.1.call-start = ((), (), s32[]{:S(2)}) async-start(), calls=%async_computation.13 | async-start | bytes 9437184 | tf_op jit(solution)/shard_map/all_gather | solution.py:201
  190.8 38.1 %copy-start.35 = (f32[1,2,8,128]{3,1,2,0:T(2,128)}, f32[1,2,8,128]{3,1,2,0:T(2,128)S(1)}, u32[]{:S(2)}) copy-start(f32[1,2,8,128]{3,1,2,0:T(2,128)S(1)} %copy.332) | copy-start | bytes 24580
  230.9 227.0 %all-gather.22.cloned.1.call-start = ((), (), s32[]{:S(2)}) async-start(), calls=%async_computation.21 | async-start | bytes 9437184 | tf_op jit(solution)/shard_map/all_gather | solution.py:177
  231.5 202.9 %all-to-all-start.1 = ((bf16[8,256,2816]{2,1,0:T(8,128)(2,1)}), bf16[8,256,2816]{2,1,0:T(8,128)(2,1)}, u32[]{:S(2)}, u32[]{:S(2)}) async-start(bf16[8,256,2816]{2,1,0:T(8,128)(2,1)} %param.43), calls=%async_computation.1 | async-start | bytes 23068672 | tf_op jit(solution)/shard_map/all_to_all | solution.py:181
  245.4 170.2 %copy-start.40 = (bf16[1,1,8,256]{3,1,2,0:T(2,128)(2,1)}, bf16[1,1,8,256]{3,1,2,0:T(2,128)(2,1)S(1)}, u32[]{:S(2)}) copy-start(bf16[1,1,8,256]{3,1,2,0:T(2,128)(2,1)S(1)} %copy.333) | copy-start | bytes 12292
  434.4 83.0 %all-to-all-start.2 = ((bf16[8,176,2048]{2,1,0:T(8,128)(2,1)}), bf16[8,176,2048]{2,1,0:T(8,128)(2,1)}, u32[]{:S(2)}, u32[]{:S(2)}) async-start(bf16[8,176,2048]{2,1,0:T(8,128)(2,1)} %param.44), calls=%async_computation.2 | async-start | bytes 11534336 | tf_op jit(solution)/shard_map/all_to_all | solution.py:183
  439.1 221.1 %reduce-scatter.8.cloned.1.call-start = ((), (), s32[]{:S(2)}) async-start(), calls=%async_computation.15 | async-start | bytes 9437184 | tf_op jit(solution)/shard_map/reduce_scatter | solution.py:249
  473.7 26.7 %slice-start = ((s8[8388608]{0:T(1024)(128)(4,1)}), s8[4194304]{0:T(1024)(128)(4,1)S(1)}, s32[]{:S(2)}) async-start(s8[8388608]{0:T(1024)(128)(4,1)} %bitcast.283), calls=%async_computation.23 | async-start | bytes 8388608
  589.8 146.2 %reduce-scatter.6.cloned.1.call-start = ((), (), s32[]{:S(2)}) async-start(), calls=%async_computation.14 | async-start | bytes 9437184 | tf_op jit(solution)/shard_map/reduce_scatter | solution.py:271
  625.6 34.6 %copy-start.9 = (f32[256,2048]{1,0:T(8,128)S(1)}, f32[256,2048]{1,0:T(8,128)}, u32[]{:S(2)}) copy-start(f32[256,2048]{1,0:T(8,128)} %copy-done.8) | copy-start | bytes 6291460
  625.7 34.6 %copy-start.36 = (f32[1,2,8,128]{3,1,2,0:T(2,128)S(1)}, f32[1,2,8,128]{3,1,2,0:T(2,128)}, u32[]{:S(2)}) copy-start(f32[1,2,8,128]{3,1,2,0:T(2,128)} %copy-done.35) | copy-start | bytes 24580
  625.7 34.6 %copy-start.68 = (f32[256]{0:T(256)S(1)}, f32[256]{0:T(256)}, u32[]{:S(2)}) copy-start(f32[256]{0:T(256)} %copy-done.67) | copy-start | bytes 3076
  625.7 110.3 %copy-start.74 = (f32[256]{0:T(256)S(1)}, f32[256]{0:T(256)}, u32[]{:S(2)}) copy-start(f32[256]{0:T(256)} %get-tuple-element.212) | copy-start | bytes 3076
  746.4 31.6 %copy-start.14 = (f32[4,256,256]{1,2,0:T(8,128)S(1)}, f32[4,256,256]{1,2,0:T(8,128)}, u32[]{:S(2)}) copy-start(f32[4,256,256]{1,2,0:T(8,128)} %copy-done.13) | copy-start | bytes 3145732
  747.7 30.3 %all-to-all-start.3 = ((bf16[256,16,128]{2,0,1:T(8,128)(2,1)}), bf16[256,16,128]{2,0,1:T(8,128)(2,1)S(1)}, u32[]{:S(2)}, u32[]{:S(2)}) async-start(bf16[256,16,128]{2,0,1:T(8,128)(2,1)} %bitcast.295), calls=%async_computation.5 | async-start | bytes 2097152 | tf_op jit(solution)/shard_map/all_to_all | solution.py:283
  752.3 189.7 %reduce-scatter.12.cloned.1.call-start = ((), (), s32[]{:S(2)}) async-start(), calls=%async_computation.17 | async-start | bytes 7077888 | tf_op jit(solution)/shard_map/reduce_scatter | solution.py:311
  824.3 279.0 %reduce-scatter.14.cloned.1.call-start = ((), (), s32[]{:S(2)}) async-start(), calls=%async_computation.19 | async-start | bytes 9437184 | tf_op jit(solution)/shard_map/reduce_scatter | solution.py:287
  852.7 83.9 %all-to-all-start.5 = ((bf16[8,176,2048]{2,1,0:T(8,128)(2,1)}), bf16[8,176,2048]{2,1,0:T(8,128)(2,1)}, u32[]{:S(2)}, u32[]{:S(2)}) async-start(bf16[8,176,2048]{2,1,0:T(8,128)(2,1)} %bitcast.293), calls=%async_computation.10 | async-start | bytes 11534336 | tf_op jit(solution)/shard_map/all_to_all | solution.py:264
  857.6 306.8 %reduce-scatter.10.cloned.1.call-start = ((), (), s32[]{:S(2)}) async-start(), calls=%async_computation.16 | async-start | bytes 5242880 | tf_op jit(solution)/shard_map/reduce_scatter | solution.py:303
  936.6 166.7 %all-to-all-start.4 = ((bf16[8,256,2816]{2,1,0:T(8,128)(2,1)}), bf16[8,256,2816]{2,1,0:T(8,128)(2,1)}, u32[]{:S(2)}, u32[]{:S(2)}) async-start(bf16[8,256,2816]{2,1,0:T(8,128)(2,1)} %bitcast.279), calls=%async_computation.9 | async-start | bytes 23068672 | tf_op jit(solution)/shard_map/all_to_all | solution.py:259
  941.9 288.7 %all-gather.18.cloned.1.call-start = ((), (), s32[]{:S(2)}) async-start(), calls=%async_computation.18 | async-start | bytes 3932160 | tf_op jit(solution)/shard_map/all_gather | solution.py:312
  944.7 1185.6 %all-reduce.7.cloned.1.call-start = ((), (), s32[]{:S(2)}) async-start(), calls=%async_computation.22 | async-start | bytes 54001664 | tf_op jit(solution)/shard_map/psum | solution.py:131
  1103.4 61.0 %copy-start.39 = (f32[1,2,8,128]{3,1,2,0:T(2,128)S(1)}, f32[1,2,8,128]{3,1,2,0:T(2,128)}, u32[]{:S(2)}) copy-start(f32[1,2,8,128]{3,1,2,0:T(2,128)} %copy-done.37) | copy-start | bytes 24580
  1103.4 63.1 %copy-start.12 = (f32[256,2048]{1,0:T(8,128)S(1)}, f32[256,2048]{1,0:T(8,128)}, u32[]{:S(2)}) copy-start(f32[256,2048]{1,0:T(8,128)} %copy-done.10) | copy-start | bytes 6291460
  (79 other events, 462.6 us)
Sparse Core Ops, SparseCore 0:
  9.6 83.4 all-gather.19
  95.5 45.1 all-gather.11
  142.7 54.3 all-gather.13
  231.0 129.8 all-gather.15
  362.6 76.5 all-gather.21
  589.9 70.2 reduce-scatter.7
  664.7 71.2 reduce-scatter.5
  824.4 91.0 reduce-scatter.11
  920.0 151.4 reduce-scatter.13
  1073.6 90.7 reduce-scatter.9
  1166.6 63.9 all-gather.17
  1234.5 895.7 all-reduce.6

commit v2 on v1

v2 whole, which is shorter than its diff:
```python
import functools
import math

import jax
import jax.numpy as jnp
from jax import lax
from jax.experimental import pallas as pl
from jax.experimental.pallas import tpu as pltpu
from jax.sharding import PartitionSpec as P

D = 2048
HEADS = 16
HEAD_DIM = 128
FF_EXPERT = 1408
TOP = 4
EXPERTS = 8
QBLOCK = 256
DOC_MOST = 512

EPSILON = 1e-06
THETA = 1000000.0

bf16 = jnp.bfloat16
f32 = jnp.float32


def dot(a, b, contract, kind=f32):
    return lax.dot_general(a, b, (contract, ((), ())), preferred_element_type=f32).astype(kind)


def rms_scale(values):
    return lax.rsqrt(jnp.mean(values * values, axis=-1, keepdims=True) + EPSILON)


def norm_back(values, scale, gain, grad):
    scaled = grad * gain
    centre = jnp.mean(scaled * values, axis=-1, keepdims=True)
    return scale * (scaled - values * (scale * scale) * centre)


def rope_tables(positions):
    steps_half = jnp.arange(HEAD_DIM // 2, dtype=jnp.int32).astype(f32)
    frequency = jnp.exp(steps_half * (-2.0 * math.log(THETA) / HEAD_DIM))
    angles = positions.astype(f32)[:, None] * frequency[None, :]
    angles = jnp.concatenate([angles, angles], axis=-1)
    return (jnp.cos(angles), jnp.sin(angles))


def rotate(rows, cosine, sine):
    middle = rows.shape[-1] // 2
    turned = jnp.concatenate([-rows[..., middle:], rows[..., :middle]], axis=-1)
    return rows * cosine[:, None, :] + turned * sine[:, None, :]


def rotate_back(rows, cosine, sine):
    middle = rows.shape[-1] // 2
    turned = rows * sine[:, None, :]
    turned = jnp.concatenate([turned[..., middle:], -turned[..., :middle]], axis=-1)
    return rows * cosine[:, None, :] + turned


def key_start(block):
    return max(0, block * QBLOCK - DOC_MOST)


def block_scores(block, queries, keys, documents, factor):
    first, start = block * QBLOCK, key_start(block)
    stop = first + QBLOCK
    scores = (
        jnp.einsum(
            "qhd,khd->hqk", queries[first:stop], keys[start:stop], preferred_element_type=f32
        )
        * factor
    )
    rows = first + jnp.arange(QBLOCK, dtype=jnp.int32)
    columns = start + jnp.arange(stop - start, dtype=jnp.int32)
    allowed = (rows[:, None] >= columns[None, :]) & (
        documents[first:stop, None] == documents[None, start:stop]
    )
    return jnp.where(allowed[None], scores, -1e30)


def attend(queries, keys, values, documents, factor):
    mixed, logs = [], []
    for block in range(queries.shape[0] // QBLOCK):
        start, stop = key_start(block), (block + 1) * QBLOCK
        scores = block_scores(block, queries, keys, documents, factor)
        top = jnp.max(scores, axis=-1, keepdims=True)
        weights = jnp.exp(scores - top)
        totals = jnp.sum(weights, axis=-1, keepdims=True)
        probability = (weights / totals).astype(bf16)
        mixed.append(
            jnp.einsum(
                "hqk,khd->qhd", probability, values[start:stop], preferred_element_type=f32
            ).astype(bf16)
        )
        logs.append(top + jnp.log(totals))
    return jnp.concatenate(mixed, axis=0), logs


def attend_back(queries, keys, values, documents, factor, logs, grads):
    length = queries.shape[0]
    grad_queries = []
    grad_keys = jnp.zeros(keys.shape, f32)
    grad_values = jnp.zeros(values.shape, f32)
    for block in range(length // QBLOCK):
        start, stop = key_start(block), (block + 1) * QBLOCK
        scores = block_scores(block, queries, keys, documents, factor)
        probability = jnp.exp(scores - logs[block])
        grad_block = grads[block * QBLOCK : stop]
        query_block = queries[block * QBLOCK : stop]
        grad_values = grad_values.at[start:stop].add(
            jnp.einsum(
                "hqk,qhd->khd", probability.astype(bf16), grad_block, preferred_element_type=f32
            )
        )
        grad_probability = jnp.einsum(
            "qhd,khd->hqk", grad_block, values[start:stop], preferred_element_type=f32
        )
        centre = jnp.sum(grad_probability * probability, axis=-1, keepdims=True)
        grad_scores = (probability * (grad_probability - centre)).astype(bf16)
        grad_queries.append(
            jnp.einsum("hqk,khd->qhd", grad_scores, keys[start:stop], preferred_element_type=f32)
            * factor
        )
        grad_keys = grad_keys.at[start:stop].add(
            jnp.einsum("hqk,qhd->khd", grad_scores, query_block, preferred_element_type=f32)
            * factor
        )
    return jnp.concatenate(grad_queries, axis=0), grad_keys, grad_values


def after(value, *earlier):
    return lax.optimization_barrier((value, earlier))[0]


def line_neighbours(place):
    middle = lax.rem(place + 1, 4) // 2
    low = 1 - place // 2
    partner = low * (1 - place) + (1 - low) * (5 - place)
    across = low * 2 + (1 - low) * 1
    return middle, partner, across


def flip(index, bits):
    result, step = 0, 1
    while step < 8:
        bit = lax.rem(index // step, 2)
        result = result + step * (1 - bit if bits & step else bit)
        step *= 2
    return result


SLOTS = 4
ORDER = (0, 1, 2, 4, 3, 5, 6, 7)
LEAVE = {2: ((2, 4), (3, 5)), 4: ((3, 5), (6, 7))}


def combine_kernel(plan, *refs):
    count = len(plan)
    sources, refs = refs[:count], refs[count:]
    results, refs = refs[:count], refs[count:]
    lands, refs = refs[:count], refs[count:]
    buffers, refs = refs[: 5 * count], refs[5 * count :]
    (land_send, land_recv, g_sem, a_send, a_recv, b_send, b_recv, c_send, c_recv) = refs[:9]
    out_sem, a_free, b_free = refs[9:]
    me, place = lax.axis_index("fsdp"), lax.axis_index("seq")
    middle, partner, across = line_neighbours(place)
    peers = [flip(me, k) for k in range(8)]

    barrier = pltpu.get_barrier_semaphore()
    swapping = any(swapped for swapped, _, _, _ in plan)
    if swapping:
        for k in range(1, 8):
            pl.semaphore_signal(
                barrier, device_id={"fsdp": peers[k]}, device_id_type=pl.DeviceIdType.MESH
            )
    pl.semaphore_signal(
        barrier, device_id={"seq": partner}, device_id_type=pl.DeviceIdType.MESH
    )

    @pl.when(middle == 1)
    def _():
        pl.semaphore_signal(
            barrier, device_id={"seq": across}, device_id_type=pl.DeviceIdType.MESH
        )

    pl.semaphore_wait(barrier, 1 + middle + (7 if swapping else 0))

    arrivals = {}
    for index, (swapped, rows, blocks, _) in enumerate(plan):
        if not swapped:
            continue
        here = pl.ds(pl.multiple_of(me * rows, 16), rows)
        for k in range(1, 8):
            there = pl.ds(pl.multiple_of(peers[k] * rows, 16), rows)
            copy = pltpu.make_async_remote_copy(
                src_ref=sources[index].at[there],
                dst_ref=lands[index].at[here],
                send_sem=land_send.at[index, k],
                recv_sem=land_recv.at[index, k],
                device_id={"fsdp": peers[k]},
                device_id_type=pl.DeviceIdType.MESH,
            )
            arrivals[index, k] = copy
            if k in (1, 2, 4):
                copy.start()

    chunks, starts = [], []
    for index, (swapped, rows, blocks, size) in enumerate(plan):
        starts.append(len(chunks))
        for block in range(blocks):
            base = (peers[ORDER[block]] if swapped else block) * rows
            for first in range(0, rows, size):
                chunks.append((index, block if first == 0 else None, base + first, size))
    total = len(chunks)

    def landed(c):
        index, block, _, _ = chunks[c]
        if not plan[index][0] or block is None:
            return
        if block > 0:
            arrivals[index, ORDER[block]].wait_recv()
        if block in LEAVE:
            left, leaving = LEAVE[block]
            for k in left:
                arrivals[index, k].wait_send()
            for k in leaving:
                arrivals[index, k].start()

    def place_of(c, ref_list):
        index, _, start, size = chunks[c]
        if isinstance(start, int):
            return ref_list[index].at[pl.ds(start, size)]
        return ref_list[index].at[pl.ds(pl.multiple_of(start, 16), size)]

    def held(c, which):
        return buffers[5 * chunks[c][0] + which].at[c % SLOTS]

    def given(c):
        index, _, _, size = chunks[c]
        away = plan[index][0] and size * (c - starts[index]) >= plan[index][1]
        return place_of(c, lands if away else sources)

    def inward(c):
        return pltpu.make_async_remote_copy(
            src_ref=given(c),
            dst_ref=held(c, 1),
            send_sem=a_send.at[c % SLOTS],
            recv_sem=a_recv.at[c % SLOTS],
            device_id={"seq": partner},
            device_id_type=pl.DeviceIdType.MESH,
        )

    def crossing(c):
        return pltpu.make_async_remote_copy(
            src_ref=held(c, 2),
            dst_ref=held(c, 3),
            send_sem=b_send.at[c % SLOTS],
            recv_sem=b_recv.at[c % SLOTS],
            device_id={"seq": across},
            device_id_type=pl.DeviceIdType.MESH,
        )

    def outward(c):
        return pltpu.make_async_remote_copy(
            src_ref=held(c, 4),
            dst_ref=place_of(c, results),
            send_sem=c_send.at[c % SLOTS],
            recv_sem=c_recv.at[c],
            device_id={"seq": partner},
            device_id_type=pl.DeviceIdType.MESH,
        )

    def fetch(c):
        return pltpu.make_async_copy(given(c), held(c, 0), g_sem.at[c % SLOTS])

    def keep(c):
        return pltpu.make_async_copy(held(c, 4), place_of(c, results), out_sem.at[c % SLOTS])

    @pl.when(middle == 0)
    def _():
        for c in range(total):
            landed(c)
            if c >= SLOTS:
                inward(c - SLOTS).wait_send()
                pl.semaphore_wait(a_free, 1)
            inward(c).start()
        for c in range(max(0, total - SLOTS), total):
            inward(c).wait_send()
        for c in range(total):
            outward(c).wait_recv()

    @pl.when(middle == 1)
    def _():
        for c in range(min(SLOTS, total)):
            landed(c)
            fetch(c).start()
        for i in range(total + 1):
            c = i
            if c < total:
                fetch(c).wait()
                inward(c).wait_recv()
                if c >= SLOTS:
                    crossing(c - SLOTS).wait_send()
                held(c, 2)[...] = (
                    held(c, 0)[...].astype(f32) + held(c, 1)[...].astype(f32)
                ).astype(bf16)
                if c + SLOTS < total:
                    pl.semaphore_signal(
                        a_free, device_id={"seq": partner}, device_id_type=pl.DeviceIdType.MESH
                    )
                if c >= SLOTS:
                    pl.semaphore_wait(b_free, 1)
                crossing(c).start()
                if c + SLOTS < total:
                    landed(c + SLOTS)
                    fetch(c + SLOTS).start()
            c = i - 1
            if c >= 0:
                crossing(c).wait_recv()
                if c >= SLOTS:
                    keep(c - SLOTS).wait()
                    outward(c - SLOTS).wait_send()
                held(c, 4)[...] = (
                    held(c, 2)[...].astype(f32) + held(c, 3)[...].astype(f32)
                ).astype(bf16)
                if c + SLOTS < total:
                    pl.semaphore_signal(
                        b_free, device_id={"seq": across}, device_id_type=pl.DeviceIdType.MESH
                    )
                outward(c).start()
                keep(c).start()
        for c in range(max(0, total - SLOTS), total):
            crossing(c).wait_send()
            keep(c).wait()
            outward(c).wait_send()

    for (_, k), copy in arrivals.items():
        if k in (1, 6, 7):
            copy.wait_send()


def combine(arrays, number):
    plan = []
    for value, swapped, size in arrays:
        rows = value.shape[0] // 8 if swapped else value.shape[0]
        plan.append((swapped, rows, 8 if swapped else 1, size))
    count = len(plan)
    total = sum(rows // size * blocks for _, rows, blocks, size in plan)
    shapes = [jax.ShapeDtypeStruct(value.shape, bf16) for value, _, _ in arrays]
    lands = [
        jax.ShapeDtypeStruct(value.shape if swapped else (16, 128), bf16)
        for value, swapped, _ in arrays
    ]
    buffers = [
        pltpu.VMEM((SLOTS, size, value.shape[1]), bf16)
        for value, _, size in arrays
        for _ in range(5)
    ]
    dma = pltpu.SemaphoreType.DMA
    moved = sum(value.size for value, _, _ in arrays)
    anywhere = pl.BlockSpec(memory_space=pl.ANY)
    return pl.pallas_call(
        functools.partial(combine_kernel, tuple(plan)),
        out_shape=shapes + lands,
        in_specs=[anywhere] * count,
        out_specs=[anywhere] * (2 * count),
        scratch_shapes=buffers
        + [
            dma((count, 8)),
            dma((count, 8)),
            dma((SLOTS,)),
            dma((SLOTS,)),
            dma((SLOTS,)),
            dma((SLOTS,)),
            dma((SLOTS,)),
            dma((SLOTS,)),
            dma((total,)),
            dma((SLOTS,)),
            pltpu.SemaphoreType.REGULAR,
            pltpu.SemaphoreType.REGULAR,
        ],
        compiler_params=pltpu.CompilerParams(
            collective_id=number, has_side_effects=True, vmem_limit_bytes=48 * 1024 * 1024
        ),
        cost_estimate=pl.CostEstimate(
            flops=2 * moved, bytes_accessed=200 * moved, transcendentals=0
        ),
        name="combine_%d" % number,
    )(*[value for value, _, _ in arrays])[:count]


def middle_kernel(joined, x, u, w_gate, w_lift, w_down, scale, inner, *outs):
    gate = jnp.dot(x[...], w_gate[...], preferred_element_type=f32)
    lift = jnp.dot(x[...], w_lift[...], preferred_element_type=f32)
    raw = lax.dot_general(
        u[...], w_down[...], (((1,), (1,)), ((), ())), preferred_element_type=f32
    )
    sigma = 1.0 / (1.0 + jnp.exp(-gate))
    silu = gate * sigma
    product = silu * lift
    outs[-1][...] = jnp.sum(product * raw, axis=1, keepdims=True)
    inner[...] = (product * scale[...]).astype(bf16)
    grad = raw * scale[...]
    grad_gate = (grad * lift * sigma * (1.0 + gate * (1.0 - sigma))).astype(bf16)
    grad_lift = (grad * silu).astype(bf16)
    if joined:
        width = grad_gate.shape[1]
        outs[0][:, :width] = grad_gate
        outs[0][:, width:] = grad_lift
    else:
        outs[0][...] = grad_gate
        outs[1][...] = grad_lift


def middle(x, u, w_gate, w_lift, w_down, scale):
    joined = w_lift is None
    rows, hidden = x.shape[0], w_down.shape[0]
    tile = 256
    whole = dict(pipeline_mode=pl.Buffered(1))
    grads = [hidden * 2] if joined else [hidden, hidden]
    return pl.pallas_call(
        functools.partial(middle_kernel, joined),
        grid=(rows // tile,),
        in_specs=[
            pl.BlockSpec((tile, D), lambda i: (i, 0)),
            pl.BlockSpec((tile, D), lambda i: (i, 0)),
            pl.BlockSpec((D, hidden), lambda i: (0, 0), **whole),
            pl.BlockSpec((D, hidden), lambda i: (0, 1 if joined else 0), **whole),
            pl.BlockSpec((hidden, D), lambda i: (0, 0), **whole),
            pl.BlockSpec((tile, 1), lambda i: (i, 0)),
        ],
        out_specs=[pl.BlockSpec((tile, w), lambda i: (i, 0)) for w in [hidden] + grads + [1]],
        out_shape=[jax.ShapeDtypeStruct((rows, w), bf16) for w in [hidden] + grads]
        + [jax.ShapeDtypeStruct((rows, 1), f32)],
        compiler_params=pltpu.CompilerParams(vmem_limit_bytes=52 * 1024 * 1024),
        cost_estimate=pl.CostEstimate(
            flops=6 * rows * D * hidden,
            bytes_accessed=2 * (2 * rows * D + 3 * hidden * D + 3 * rows * hidden),
            transcendentals=rows * hidden,
        ),
    )(x, u, w_gate, w_gate if joined else w_lift, w_down, scale)


def window(blocks, first, count, axis):
    size = blocks[0].shape[axis]
    return lax.dynamic_slice_in_dim(
        jnp.concatenate(blocks, axis=axis), first * size, count * size, axis
    )


def gather_seq(value):
    seq, place = lax.axis_size("seq"), lax.axis_index("seq")
    if seq != 4:
        return lax.all_gather(value, "seq", axis=0, tiled=True)
    lower, higher, up, down = [], [], value, value
    for hop in range(seq - 1):
        up = lax.ppermute(up, "seq", [(i, i + 1) for i in range(hop, seq - 1)])
        down = lax.ppermute(down, "seq", [(i + 1, i) for i in range(seq - 1 - hop)])
        lower.insert(0, up)
        higher.append(down)
    return window(lower + [value] + higher, seq - 1 - place, seq, 0)


def together(*values):
    return lax.optimization_barrier(values)


def exchange_seq(value, axis_out, axis_in):
    seq, place = lax.axis_size("seq"), lax.axis_index("seq")
    if seq != 4:
        return lax.all_to_all(value, "seq", axis_out, axis_in, tiled=True)
    size = value.shape[axis_out] // seq
    came = []
    for shift in range(seq):
        block = lax.dynamic_slice_in_dim(value, lax.rem(place + shift, seq) * size, size, axis_out)
        if shift:
            block = lax.ppermute(block, "seq", [(i, (i + shift) % seq) for i in range(seq)])
        came.append(block)
    order = [came[shift % seq] for shift in range(seq - 1, -seq, -1)]
    return window(order, seq - 1 - place, seq, axis_in)


def swap(value):
    return lax.all_to_all(value, "fsdp", 0, 0, tiled=True)


def scatter(value):
    size = lax.axis_size("fsdp")
    return jnp.sum(swap(value.reshape(size, -1, value.shape[-1])).astype(f32), axis=0)


def on_device(
    tokens,
    segments,
    expert_ids,
    expert_gates,
    attn_gain,
    qkv_weight,
    qkv_bias,
    out_weight,
    ffn_gain,
    shared_gate_up,
    shared_down,
    shared_gate,
    expert_gate_up,
    expert_down,
    cotangent,
):
    fsdp, seq = lax.axis_size("fsdp"), lax.axis_size("seq")
    me, place = lax.axis_index("fsdp"), lax.axis_index("seq")
    row_count, length = tokens.shape[1], segments.shape[1]
    heads = HEADS // seq
    group = heads * HEAD_DIM
    copies = fsdp // EXPERTS
    width = D // fsdp
    hidden_own = FF_EXPERT // copies
    piece = hidden_own // fsdp
    factor = 1.0 / math.sqrt(HEAD_DIM)
    capacity = length * TOP // EXPERTS

    all_tokens = gather_seq(tokens[0])
    own = [
        lax.dynamic_slice_in_dim(qkv_weight, part * D + place * group, group, 1)
        for part in range(3)
    ]
    vectors = jnp.concatenate([attn_gain, ffn_gain, shared_gate, qkv_bias])
    extra = -(-6 * width // (3 * group) // 16) * 16
    vectors = jnp.pad(vectors, (0, extra * 3 * group - 6 * width)).reshape(extra, 3 * group)
    gathered = lax.all_gather(
        jnp.concatenate([jnp.concatenate(own, axis=1), vectors], axis=0), "fsdp", axis=0
    )
    weight_qkv = gathered[:, :width].reshape(D, 3 * group)
    vectors = gathered[:, width:].reshape(fsdp, -1)
    gain_one = vectors[:, :width].reshape(D).astype(f32)
    gain_two = vectors[:, width : 2 * width].reshape(D).astype(f32)
    gate_vector = vectors[:, 2 * width : 3 * width].reshape(D)
    bias = vectors[:, 3 * width : 6 * width].reshape(3, seq, group)
    bias = lax.dynamic_index_in_dim(bias, place, 1, keepdims=False).reshape(-1).astype(f32)
    weight_out = lax.all_gather(out_weight, "fsdp", axis=0, tiled=True)
    upstream_all = lax.all_gather(cotangent[0], "fsdp", axis=0, tiled=True)

    up_sent = expert_gate_up.reshape(EXPERTS, width, 2, fsdp, copies, piece)
    up_sent = up_sent.transpose(0, 4, 1, 2, 3, 5).reshape(fsdp, width, 2 * hidden_own)
    down_sent = expert_down.reshape(fsdp, piece, D)
    if seq == 4:
        half = lax.rem(place, 2)
        fetched = swap(lax.dynamic_slice_in_dim(up_sent, half * (width // 2), width // 2, 1))
        given = lax.ppermute(fetched, "seq", [(0, 1), (1, 0), (2, 3), (3, 2)])
    else:
        fetched = given = swap(up_sent)

    x_all = all_tokens.astype(f32)
    normed_unit = x_all * rms_scale(x_all)
    normed = (normed_unit * gain_one).astype(bf16)
    cosine, sine = rope_tables(jnp.arange(length, dtype=jnp.int32))
    normed = after(normed, weight_qkv)
    joined = dot(normed, weight_qkv, ((1,), (0,))) + bias
    split = joined.reshape(length, 3, heads, HEAD_DIM)
    queries = rotate(split[:, 0], cosine, sine).astype(bf16)
    keys = rotate(split[:, 1], cosine, sine).astype(bf16)
    values = split[:, 2].astype(bf16)
    documents = segments[0]
    mixed, logs = attend(queries, keys, values, documents, factor)
    mixed_rows = exchange_seq(mixed.reshape(length, group), 0, 1)
    mixed_rows = after(mixed_rows, upstream_all)
    inputs = tokens[0].astype(f32)
    hidden = inputs + dot(mixed_rows, weight_out, ((1,), (0,)))
    scale_two = rms_scale(hidden)
    second = (hidden * scale_two * gain_two).astype(bf16)
    second_all = lax.all_gather(after(second, fetched), "fsdp", axis=0, tiled=True)

    names = jnp.arange(EXPERTS, dtype=jnp.int32)
    matches = expert_ids[0][None, :, :] == names[:, None, None]
    gates = jnp.sum(jnp.where(matches, expert_gates[0][None], 0.0), axis=-1)
    gates = jnp.where(jnp.any(matches, axis=-1), gates, -1.0)
    gates = lax.all_gather(after(gates.reshape(-1), second), ("seq", "fsdp"), axis=0)
    gates = gates.reshape(seq, fsdp, EXPERTS, row_count)
    gates = lax.dynamic_index_in_dim(gates, me // copies, 2, keepdims=False)
    gates = gates.transpose(1, 0, 2).reshape(fsdp, length)
    chosen = (gates >= 0.0).astype(jnp.int32)
    earlier = jnp.cumsum(chosen, axis=1) - chosen
    share = jnp.where((chosen > 0) & (earlier < capacity), gates, 0.0)
    share = lax.dynamic_slice_in_dim(share, place * row_count, row_count, 1).reshape(-1, 1)

    weight_down = swap(after(down_sent, second_all)).reshape(hidden_own, D)
    weight_up, fetched = after((given, fetched), second_all)
    if seq == 4:
        weight_up = jnp.concatenate(
            [jnp.where(half == 0, fetched, weight_up), jnp.where(half == 0, weight_up, fetched)],
            axis=1,
        )
    weight_up = weight_up.reshape(D, 2 * hidden_own)

    by_kernel = seq == 4 and fsdp == 8
    s_gate, s_lift = shared_gate_up[:, 0], shared_gate_up[:, 1]
    opening_all = jax.nn.sigmoid(dot(second_all, gate_vector, ((1,), (0,))))[:, None]
    inner_s, ga_s, gl_s, reach = middle(
        second_all, upstream_all, s_gate, s_lift, shared_down, opening_all
    )
    grad_s_down = dot(inner_s, upstream_all, ((0,), (0,)), bf16)
    grad_s_gate = dot(second_all, ga_s, ((0,), (0,)), bf16)
    grad_s_lift = dot(second_all, gl_s, ((0,), (0,)), bf16)

    held = after(second_all, grad_s_down, grad_s_gate, grad_s_lift)
    if hidden_own % 128 == 0:
        inner_e, grads_e, _ = middle(held, upstream_all, weight_up, None, weight_down, share)
    else:
        inner_e, ga_e, gl_e, _ = middle(
            held,
            upstream_all,
            weight_up[:, :hidden_own],
            weight_up[:, hidden_own:],
            weight_down,
            share,
        )
        grads_e = jnp.concatenate([ga_e, gl_e], axis=1)
    part = dot(inner_e, upstream_all, ((0,), (0,)), bf16)
    grad_e_down = part
    reach = jnp.sum(swap(after(reach.reshape(fsdp, row_count), part)), axis=0)

    grads_e, ga_s, gl_s = after((grads_e, ga_s, gl_s), part)
    grad_second_all = (
        dot(ga_s, s_gate, ((1,), (1,)))
        + dot(gl_s, s_lift, ((1,), (1,)))
        + dot(grads_e, weight_up, ((1,), (1,)))
    ).astype(bf16)
    grad_second = scatter(grad_second_all)

    grad_e_up = dot(second_all, after(grads_e, grad_second_all), ((0,), (0,)), bf16)

    inner_s, inner_e = after((inner_s, inner_e), grad_e_up)
    out_all = (
        dot(inner_s, shared_down, ((1,), (0,))) + dot(inner_e, weight_down, ((1,), (0,)))
    ).astype(bf16)

    if by_kernel:
        shared = after((grad_s_down, grad_s_gate, grad_s_lift), out_all)
        sum_s = combine([(shared[0], False, 64), (shared[1], False, 256), (shared[2], False, 256)], 2)
        out_all = after(out_all, *sum_s)
    else:
        sum_s = lax.psum((grad_s_down, grad_s_gate, grad_s_lift), "seq")

    grad_second, reach = after((grad_second, reach), out_all)
    upstream = cotangent[0].astype(f32)
    opening = jax.nn.sigmoid(dot(second, gate_vector, ((1,), (0,))))
    grad_logit = reach * opening * (1.0 - opening)
    grad_second = grad_second + grad_logit[:, None] * gate_vector.astype(f32)[None, :]
    grad_gate_vector = jnp.sum(grad_logit[:, None] * second.astype(f32), axis=0)
    grad_hidden = upstream + norm_back(hidden, scale_two, gain_two, grad_second)
    grad_gain_two = jnp.sum(grad_second * hidden * scale_two, axis=0)
    grad_projected = grad_hidden.astype(bf16)
    grad_mixture = dot(grad_projected, weight_out, ((1,), (1,)), bf16)
    grad_heads = exchange_seq(grad_mixture, 1, 0)
    grad_out = dot(mixed_rows, after(grad_projected, grad_mixture), ((0,), (0,)), bf16)

    grad_heads = after(grad_heads, grad_out)
    grad_queries, grad_keys, grad_values = attend_back(
        queries,
        keys,
        values,
        documents,
        factor,
        logs,
        grad_heads.reshape(length, heads, HEAD_DIM),
    )
    grad_joined = jnp.stack(
        [
            rotate_back(grad_queries.astype(bf16).astype(f32), cosine, sine),
            rotate_back(grad_keys.astype(bf16).astype(f32), cosine, sine),
            grad_values,
        ],
        axis=1,
    )
    grad_joined = grad_joined.reshape(length, 3 * group).astype(bf16)
    grad_normed_all = dot(grad_joined, weight_qkv, ((1,), (1,)))
    grad_gain_one = jnp.sum(grad_normed_all * normed_unit, axis=0)

    grad_qkv = dot(normed, grad_joined, ((0,), (0,)), bf16).reshape(fsdp, width, 3 * group)
    grad_bias = jnp.sum(grad_joined.astype(f32), axis=0).reshape(3, 1, group)
    own_heads = (jnp.arange(seq, dtype=jnp.int32) == place).astype(f32)
    grad_bias = (grad_bias * own_heads[None, :, None]).reshape(fsdp, 3 * width)
    rows = jnp.concatenate(
        [
            grad_gain_one.reshape(fsdp, width),
            grad_gain_two.reshape(fsdp, width),
            grad_gate_vector.reshape(fsdp, width),
            grad_bias,
        ],
        axis=1,
    ).astype(bf16)
    rows = jnp.pad(rows, ((0, 0), (0, extra * 3 * group - 6 * width)))
    rows = rows.reshape(fsdp, extra, 3 * group)
    grad_qkv = jnp.concatenate([grad_qkv, rows], axis=1)

    grad_out = scatter(grad_out).astype(bf16)
    grad_normed_all = grad_normed_all.astype(bf16)
    grad_e_up, grad_out, grad_qkv, grad_normed_all, out_all = together(
        grad_e_up, grad_out, grad_qkv, grad_normed_all, out_all
    )
    grad_qkv = lax.psum_scatter(
        grad_qkv.reshape(-1, 3 * group), "fsdp", scatter_dimension=0, tiled=True
    )
    grad_normed = lax.psum_scatter(grad_normed_all, "seq", scatter_dimension=0, tiled=True)
    out_part = lax.psum_scatter(out_all, "fsdp", scatter_dimension=0, tiled=True)
    if by_kernel:
        sum_e_up, sum_e_down, sum_out = combine(
            [(grad_e_up, True, 64), (grad_e_down, True, 176), (grad_out, False, 64)], 1
        )
        sum_e_up = sum_e_up.reshape(EXPERTS, width, 2 * FF_EXPERT)
        sum_e_down = sum_e_down.reshape(EXPERTS, piece, D)
    else:
        sum_e_up = swap(grad_e_up.reshape(fsdp, width, 2 * hidden_own))
        sum_e_down = swap(grad_e_down.reshape(fsdp, piece, D))
        sum_e_up, sum_e_down, sum_out = lax.psum((sum_e_up, sum_e_down, grad_out), "seq")
        sum_e_down = sum_e_down.reshape(EXPERTS, copies * piece, D)
        sum_e_up = sum_e_up.reshape(EXPERTS, copies, width, 2, fsdp, piece)
        sum_e_up = sum_e_up.transpose(0, 2, 3, 4, 1, 5).reshape(EXPERTS, width, 2 * FF_EXPERT)
    output = (hidden + out_part.astype(f32)).astype(bf16)
    grad_normed = grad_normed.astype(f32)
    grad_qkv = lax.all_gather(grad_qkv, "seq", axis=0)
    rows = jnp.sum(grad_qkv[:, width:].astype(f32), axis=0).reshape(-1)
    grad_qkv = jnp.concatenate(
        [
            grad_qkv[owner, :width, part * group : (part + 1) * group]
            for part in range(3)
            for owner in range(seq)
        ],
        axis=1,
    ).astype(f32)
    input_grad = (grad_hidden + norm_back(inputs, rms_scale(inputs), gain_one, grad_normed)).astype(
        bf16
    )
    sum_s_up = jnp.stack([sum_s[1], sum_s[2]], axis=1)

    return (
        output[None],
        input_grad[None],
        rows[:width],
        grad_qkv,
        rows[3 * width : 6 * width],
        sum_out.astype(f32),
        rows[width : 2 * width],
        sum_s_up.astype(f32),
        sum_s[0].astype(f32),
        rows[2 * width : 3 * width],
        sum_e_up.astype(f32),
        sum_e_down.astype(f32),
    )


def solution(mesh):
    return jax.shard_map(
        on_device,
        mesh=mesh,
        in_specs=(
            P("fsdp", "seq", None),
            P("fsdp", None),
            P("fsdp", "seq", None),
            P("fsdp", "seq", None),
            P("fsdp"),
            P("fsdp", None),
            P("fsdp"),
            P("fsdp", None),
            P("fsdp"),
            P(None, None, "fsdp"),
            P("fsdp", None),
            P("fsdp"),
            P(None, "fsdp", None),
            P(None, "fsdp", None),
            P("fsdp", "seq", None),
        ),
        out_specs=(
            P("fsdp", "seq", None),
            P("fsdp", "seq", None),
            P("fsdp"),
            P("fsdp", None),
            P("fsdp"),
            P("fsdp", None),
            P("fsdp"),
            P(None, None, "fsdp"),
            P("fsdp", None),
            P("fsdp"),
            P(None, "fsdp", None),
            P(None, "fsdp", None),
        ),
        check_vma=False,
    )
```

time: 2180 us -> 1730 us (0.79)
  waiting for transfers between devices: 1340 us -> 197 us
  Pallas kernels: 0 us -> 843 us
  matrix products: 371 us -> 250 us
  blocking collectives: 240 us -> 143 us
  local copies, waits for them, and re-layouts: 79.4 us -> 105 us
  other arithmetic: 93.4 us -> 118 us
    psum x1 -> x0, waiting for transfers between devices: 883 us -> none  [sum_seq(): return lax.psum(value.astype(bf16), 'seq').astype(f32)]
    pallas_call x0 -> x4, Pallas kernels: none -> 843 us  [the longest x2 761 us: combine(): pl.pallas_call(functools.partial(combine_kernel, tuple(plan)), out_shape=...]
    all_to_all x6 -> x5, waiting for transfers between devices: 184 us -> 13.4 us  [swap(): return lax.all_to_all(value, 'fsdp', 0, 0, tiled=True)]
    all_gather x4 -> x3, waiting for transfers between devices: 166 us -> 0.02 us  [the longest x1 0.02 us: on_device(): lax.all_gather(jnp.concatenate([jnp.concatenate(own, axis=1), vectors], a...]
    dot_general x26 -> x18, matrix products: 348 us -> 226 us  [dot(): lax.dot_general(a, b, (contract, ((), ())), preferred_element_type=f32)]
    ppermute x0 -> x13, waiting for transfers between devices: none -> 95.4 us  [the longest x3 48.1 us: gather_seq(): down = lax.ppermute(down, 'seq', [(i + 1, i) for i in range(seq - 1 - hop)])]
    reduce_scatter x1, waiting for transfers between devices: 72.4 us -> 0.01 us  [on_device(): lax.psum_scatter(out_all, 'fsdp', scatter_dimension=0, tiled=True)]
    psum x1 -> x0, blocking collectives: 45.1 us -> none  [on_device(): small = lax.psum(small, ('seq', 'fsdp'))]
  transfers between devices with their start and end apart: 18 -> 26, of which waited for: 11 -> 10; matrix products, arithmetic and copies ran while one was open for 17% -> 23% of each run, Pallas kernels for 0% -> 46%
where the time goes in v2:
time: 1730 us; the launch traced here: 1720 us
  Pallas kernels  843 us (49%)
  matrix products  250 us (14%)
  waiting for transfers between devices  197 us (11%)
  blocking collectives  143 us (8%)
  other arithmetic  118 us (7%)
  local copies, waits for them, and re-layouts  105 us (6%)
  starting transfers between devices  44.3 us (3%)
    pallas_call x2, Pallas kernels, combine(): pl.pallas_call(functools.partial(combine_kernel, tuple(plan)), out_shape=...  761 us
    dot_general x18, matrix products, dot(): lax.dot_general(a, b, (contract, ((), ())), preferred_element_type=f32)  226 us
    all_gather x1, blocking collectives, on_device(): lax.all_gather(after(gates.reshape(-1), second), ('seq', 'fsdp'), axis=0)  143 us
    pallas_call x2, Pallas kernels, middle(): pl.pallas_call(functools.partial(middle_kernel, joined), grid=(rows // ti...  81.9 us
    reduce_scatter x1, waiting for transfers between devices, on_device(): lax.psum_scatter(grad_qkv.reshape(-1, 3 * group), 'fsdp', scatter_dimensi...  60.1 us
    unnamed x184, local copies, waits for them, and re-layouts  51.7 us
    ppermute x3, waiting for transfers between devices, gather_seq(): down = lax.ppermute(down, 'seq', [(i + 1, i) for i in range(seq - 1 - hop)])  48.1 us
  transfers between devices with their start and end apart: 26, of which 10 were waited for; matrix products, arithmetic and copies ran while one was open for 23% of the time, Pallas kernels for 46%

profile of v2, /device:TPU:0, one launch (start us, length us, event | category | flops | bytes accessed | tf_op | source)
XLA Modules:
  0.0 1715.8 jit_solution(15316721003108609127)
XLA Ops:
  17.4 21.0 %collective-permute-done = bf16[256,2048]{1,0:T(8,128)(2,1)S(1)} collective-permute-done((bf16[256,2048]{1,0:T(8,128)(2,1)S(1)}, bf16[256,2048]{1,0:T(8,128)(2,1)S(1)}, u32[]{:S(2)}, u32[]{:S(2)}) %collective-permute-start) | collective-permute-done | bytes 1048608 | tf_op jit(solution)/shard_map/ppermute | solution.py:459
  58.1 24.4 %collective-permute-done.4 = bf16[256,2048]{1,0:T(8,128)(2,1)S(1)} collective-permute-done((bf16[256,2048]{1,0:T(8,128)(2,1)S(1)}, bf16[256,2048]{1,0:T(8,128)(2,1)S(1)}, u32[]{:S(2)}, u32[]{:S(2)}) %collective-permute-start.4) | collective-permute-done | bytes 1048608 | tf_op jit(solution)/shard_map/ppermute | solution.py:460
  85.7 23.7 %collective-permute-done.5 = bf16[256,2048]{1,0:T(8,128)(2,1)S(1)} collective-permute-done((bf16[256,2048]{1,0:T(8,128)(2,1)S(1)}, bf16[256,2048]{1,0:T(8,128)(2,1)S(1)}, u32[]{:S(2)}, u32[]{:S(2)}) %collective-permute-start.5) | collective-permute-done | bytes 1048608 | tf_op jit(solution)/shard_map/ppermute | solution.py:460
  126.6 8.5 convolution_add_fusion
  135.1 7.6 reshape.888
  142.7 6.7 copy.174
  175.1 15.4 collective-permute-done.7
  190.8 25.4 %all-gather.10.cloned.1.call-done = bf16[2048,2048]{1,0:T(8,128)(2,1)} async-done(((bf16[256,2048]{1,0:T(8,128)(2,1)}), bf16[2048,2048]{1,0:T(8,128)(2,1)}) %all-gather.10.cloned.1.call-update) | async-done | bytes 8388624 | tf_op jit(solution)/shard_map/all_gather | solution.py:541
  242.4 143.3 %all-gather.2 = f32[65536]{0:T(1024)S(1)} all-gather(f32[2048]{0:T(1024)S(1)} %bitcast.365), channel_id=4, replica_groups=mesh['seq'=4,'fsdp'=8] {'seq','fsdp'}, dimensions={0}, use_global_device_ids=true | all-gather | bytes 270336 | tf_op jit(solution)/shard_map/all_gather | solution.py:578
  404.2 29.3 %shard_map.238 = (bf16[2048,704]{1,0:T(8,128)(2,1)}, bf16[2048,704]{1,0:T(8,128)(2,1)}, bf16[2048,704]{1,0:T(8,128)(2,1)}, f32[2048,1]{1,0:T(8,128)S(1)}) custom-call(bf16[2048,2048]{1,0:T(8,128)(2,1)} %all-gather.12.cloned.1.call-done.x, bf16[2048,2048]{1,0:T(8,128)(2,1)} %bitcast.379, bf16[2048,704]{1,0:T(8,128)(2,1)} %bitcast.326, ...), custom_call_target="tpu_custom_call" | custom-call | flops 17716740096 | bytes 34078720 | tf_op jit(solution)/shard_map/pallas_call | solution.py:423
  433.8 11.5 convolution_convert_fusion.5.refs_1_
  445.3 8.8 convolution_convert_fusion.6.refs_0_
  454.2 10.7 convolution_convert_fusion.4.refs_2_
  464.9 9.5 broadcast_select_fusion.1
  474.4 10.0 pad_maximum_fusion
  484.4 52.7 %shard_map.239 = (bf16[2048,1408]{1,0:T(8,128)(2,1)}, bf16[2048,2816]{1,0:T(8,128)(2,1)}, f32[2048,1]{1,0:T(8,128)}) custom-call(bf16[2048,2048]{1,0:T(8,128)(2,1)} %all-gather.12.cloned.1.call-done.x, bf16[2048,2048]{1,0:T(8,128)(2,1)} %bitcast.380, bf16[2048,2816]{1,0:T(8,128)(2,1)} %bitcast.295, bf16[2048,2816]{1,0:T(8,128)(2,1)} %bitcast.296, ...), custom_call_target="tpu_custom_call" | custom-call | flops 35433480192 | bytes 51380224 | tf_op jit(solution)/shard_map/pallas_call | solution.py:423
  537.1 18.2 %convolution_convert_fusion.3.refs_1_ = bf16[1408,2048]{1,0:T(8,128)(2,1)} fusion(bf16[2048,1408]{1,0:T(8,128)(2,1)} %get-tuple-element.168, bf16[1,2048,2048]{2,1,0:T(8,128)(2,1)} %all-gather.16.cloned.1.call-done), kind=kOutput, calls=%fused_computation.14 | convolution fusion | flops 11814043648 | bytes 19922944 | tf_op jit(solution)/shard_map/dot_general | solution.py:28
  560.5 12.7 fusion.7
  573.2 11.4 fusion.5
  584.6 35.2 %add_convert_fusion.1 = bf16[2048,2048]{1,0:T(8,128)(2,1)} fusion(f32[2048,2048]{1,0:T(8,128)} %fusion.7, f32[2048,2048]{1,0:T(8,128)} %fusion.5, bf16[2048,2816]{1,0:T(8,128)(2,1)} %get-tuple-element.164, bf16[2048,2816]{1,0:T(8,128)(2,1)} %bitcast.297), kind=kOutput, calls=%fused_computation.2 | convolution fusion | flops 23634903040 | bytes 65011712 | tf_op jit(solution)/shard_map/dot_general | solution.py:28
  624.9 31.5 %convolution_convert_fusion.refs_0_ = bf16[2048,2816]{1,0:T(8,128)(2,1)} fusion(bf16[2048,2048]{1,0:T(8,128)(2,1)} %all-gather.12.cloned.1.call-done.x, bf16[2048,2816]{1,0:T(8,128)(2,1)} %get-tuple-element.164), kind=kOutput, calls=%fused_computation.4 | convolution fusion | flops 23628087296 | bytes 31457280 | tf_op jit(solution)/shard_map/dot_general | solution.py:28
  656.5 9.6 fusion.148
  666.1 21.5 %add_convert_fusion = bf16[2048,2048]{1,0:T(8,128)(2,1)} fusion(f32[2048,2048]{1,0:T(8,128)} %fusion.148, bf16[2048,1408]{1,0:T(8,128)(2,1)} %get-tuple-element.168, bf16[1408,2048]{1,0:T(8,128)(2,1)} %bitcast.25.w_down), kind=kOutput, calls=%fused_computation | convolution fusion | flops 11819548672 | bytes 36700160 | tf_op jit(solution)/shard_map/dot_general | solution.py:28
  687.7 219.2 %combine_2.1 = (bf16[704,2048]{1,0:T(8,128)(2,1)S(1)}, bf16[2048,704]{1,0:T(8,128)(2,1)}, bf16[2048,704]{1,0:T(8,128)(2,1)}, bf16[16,128]{1,0:T(8,128)(2,1)}, bf...) custom-call(bf16[704,2048]{1,0:T(8,128)(2,1)S(1)} %convolution_convert_fusion.6.refs_0_, ...), custom_call_target="tpu_custom_call" | custom-call | flops 8650752 | bytes 865075200 | tf_op jit(solution)/shard_map/combine_2/pallas_call | solution.py:364
  985.7 13.1 fusion.135
  998.9 11.5 convolution_convert_fusion.1
  1010.4 6.2 pad_maximum_fusion.1
  1016.7 13.4 all-to-all-done.4
  1036.7 60.1 %reduce-scatter.8.cloned.1.call-done = bf16[272,1536]{1,0:T(8,128)(2,1)} async-done(((bf16[2176,1536]{1,0:T(8,128)(2,1)}), bf16[272,1536]{1,0:T(8,128)(2,1)}) %reduce-scatter.8.cloned.1.call-update) | async-done | bytes 835600 | tf_op jit(solution)/shard_map/reduce_scatter | solution.py:702
  1108.0 12.2 copy.222
  1120.1 541.4 %combine_1.1 = (bf16[2048,2816]{1,0:T(8,128)(2,1)}, bf16[1408,2048]{1,0:T(8,128)(2,1)}, bf16[256,2048]{1,0:T(8,128)(2,1)S(1)}, bf16[2048,2816]{1,0:T(8,128)(2,1)...) custom-call(bf16[2048,2816]{1,0:T(8,128)(2,1)} %convolution_convert_fusion.refs_0_, ...), custom_call_target="tpu_custom_call" | custom-call | flops 18350080 | bytes 1835008000 | tf_op jit(solution)/shard_map/combine_1/pallas_call | solution.py:364
  1663.1 14.7 convert.60
  (385 shorter events, 259.3 us)
Async XLA Ops:
  7.2 106.1 %all-gather.14.cloned.1.call-start = ((), (), s32[]{:S(2)}) async-start(), calls=%async_computation.13 | async-start | bytes 7520256 | tf_op jit(solution)/shard_map/all_gather | solution.py:531
  10.3 180.5 %all-gather.16.cloned.1.call-start = ((), (), s32[]{:S(2)}) async-start(), calls=%async_computation.14 | async-start | bytes 9437184 | tf_op jit(solution)/shard_map/all_gather | solution.py:542
  11.1 27.3 %collective-permute-start = (bf16[256,2048]{1,0:T(8,128)(2,1)S(1)}, bf16[256,2048]{1,0:T(8,128)(2,1)S(1)}, u32[]{:S(2)}, u32[]{:S(2)}) collective-permute-start(bf16[256,2048]{1,0:T(8,128)(2,1)S(1)} %bitcast.291), channel_id=1, source_target_pairs={{0,8},{8,16},{16,24},{1,9},{9,17},{17,25},{2,10},{10,18},{18,26},{... | collective-permute-start | bytes 3145736 | tf_op jit(solution)/shard_map/ppermute | solution.py:459
  16.1 35.5 %collective-permute-start.3 = (bf16[256,2048]{1,0:T(8,128)(2,1)S(1)}, bf16[256,2048]{1,0:T(8,128)(2,1)S(1)}, u32[]{:S(2)}, u32[]{:S(2)}) collective-permute-start(bf16[256,2048]{1,0:T(8,128)(2,1)S(1)} %bitcast.292), channel_id=1, source_target_pairs={{8,0},{16,8},{24,16},{9,1},{17,9},{25,17},{10,2},{18,10},{26,18},{... | collective-permute-start | bytes 3145736 | tf_op jit(solution)/shard_map/ppermute | solution.py:460
  38.4 14.6 collective-permute-start.1
  45.6 179.0 %all-to-all-start = ((bf16[8,128,2816]{2,1,0:T(8,128)(2,1)}), bf16[8,128,2816]{2,1,0:T(8,128)(2,1)}, u32[]{:S(2)}, u32[]{:S(2)}) async-start(bf16[8,128,2816]{2,1,0:T(8,128)(2,1)} %constant_dynamic-slice_fusion.5), calls=%async_computation | async-start | bytes 11534336 | tf_op jit(solution)/shard_map/all_to_all | solution.py:486
  50.4 165.8 %all-gather.10.cloned.1.call-start = ((), (), s32[]{:S(2)}) async-start(), calls=%async_computation.8 | async-start | bytes 9437184 | tf_op jit(solution)/shard_map/all_gather | solution.py:541
  51.1 341.2 %all-gather.12.cloned.1.call-start = ((), (), s32[]{:S(2)}) async-start(), calls=%async_computation.9 | async-start | bytes 9437184 | tf_op jit(solution)/shard_map/all_gather | solution.py:572
  51.5 33.7 %copy-start.33 = (bf16[256,2048]{1,0:T(8,128)(2,1)S(1)}, bf16[256,2048]{1,0:T(8,128)(2,1)}, u32[]{:S(2)}) copy-start(bf16[256,2048]{1,0:T(8,128)(2,1)} %copy-done.32) | copy-start | bytes 3145732
  51.5 31.0 %collective-permute-start.4 = (bf16[256,2048]{1,0:T(8,128)(2,1)S(1)}, bf16[256,2048]{1,0:T(8,128)(2,1)S(1)}, u32[]{:S(2)}, u32[]{:S(2)}) collective-permute-start(bf16[256,2048]{1,0:T(8,128)(2,1)S(1)} %collective-permute-done.3), channel_id=1, source_target_pairs={{8,0},{16,8},{9,1},{17,9},{10,2},{18,10},{11,3},{19,11},{12,4},{20... | collective-permute-start | bytes 3145736 | tf_op jit(solution)/shard_map/ppermute | solution.py:460
  53.0 30.9 %collective-permute-start.2 = (bf16[256,2048]{1,0:T(8,128)(2,1)}, bf16[256,2048]{1,0:T(8,128)(2,1)S(1)}, u32[]{:S(2)}, u32[]{:S(2)}) collective-permute-start(bf16[256,2048]{1,0:T(8,128)(2,1)} %collective-permute-done.1), channel_id=1, source_target_pairs={{16,24},{17,25},{18,26},{19,27},{20,28},{21,29},{22,30},{23,31}} | collective-permute-start | bytes 3145736 | tf_op jit(solution)/shard_map/ppermute | solution.py:459
  55.9 97.7 %copy-start.19 = (f32[1024,128]{1,0:T(8,128)}, f32[1024,128]{1,0:T(8,128)S(1)}, u32[]{:S(2)}) copy-start(f32[1024,128]{1,0:T(8,128)S(1)} %get-tuple-element.280) | copy-start | bytes 1572868
  55.9 97.7 %copy-start.22 = (f32[1024,128]{1,0:T(8,128)}, f32[1024,128]{1,0:T(8,128)S(1)}, u32[]{:S(2)}) copy-start(f32[1024,128]{1,0:T(8,128)S(1)} %get-tuple-element.281) | copy-start | bytes 1572868
  82.5 26.8 %collective-permute-start.5 = (bf16[256,2048]{1,0:T(8,128)(2,1)S(1)}, bf16[256,2048]{1,0:T(8,128)(2,1)S(1)}, u32[]{:S(2)}, u32[]{:S(2)}) collective-permute-start(bf16[256,2048]{1,0:T(8,128)(2,1)S(1)} %collective-permute-done.4), channel_id=1, source_target_pairs={{8,0},{9,1},{10,2},{11,3},{12,4},{13,5},{14,6},{15,7}} | collective-permute-start | bytes 3145736 | tf_op jit(solution)/shard_map/ppermute | solution.py:460
  167.0 8.1 collective-permute-start.6
  167.0 23.5 %collective-permute-start.7 = (bf16[256,512]{0,1:T(8,128)(2,1)S(1)}, bf16[256,512]{0,1:T(8,128)(2,1)S(1)}, u32[]{:S(2)}, u32[]{:S(2)}) collective-permute-start(bf16[256,512]{0,1:T(8,128)(2,1)S(1)} %get-tuple-element.274), channel_id=1, source_target_pairs={{0,16},{8,24},{16,0},{24,8},{1,17},{9,25},{17,1},{25,9},{2,18},{10... | collective-permute-start | bytes 786440 | tf_op jit(solution)/shard_map/ppermute | solution.py:479
  168.2 22.3 %collective-permute-start.8 = (bf16[256,512]{0,1:T(8,128)(2,1)S(1)}, bf16[256,512]{0,1:T(8,128)(2,1)S(1)}, u32[]{:S(2)}, u32[]{:S(2)}) collective-permute-start(bf16[256,512]{0,1:T(8,128)(2,1)S(1)} %get-tuple-element.273), channel_id=1, source_target_pairs={{0,8},{8,16},{16,24},{24,0},{1,9},{9,17},{17,25},{25,1},{2,10},{10... | collective-permute-start | bytes 786440 | tf_op jit(solution)/shard_map/ppermute | solution.py:479
  169.4 53.2 %copy-start.38 = (f32[1,2,8,128]{3,1,2,0:T(2,128)}, f32[1,2,8,128]{3,1,2,0:T(2,128)S(1)}, u32[]{:S(2)}) copy-start(f32[1,2,8,128]{3,1,2,0:T(2,128)S(1)} %copy.264) | copy-start | bytes 24580
  224.6 167.7 %collective-permute-start.9 = (bf16[8,128,2816]{2,1,0:T(8,128)(2,1)}, bf16[8,128,2816]{2,1,0:T(8,128)(2,1)}, u32[]{:S(2)}, u32[]{:S(2)}) collective-permute-start(bf16[8,128,2816]{2,1,0:T(8,128)(2,1)} %all-to-all-done), channel_id=1, source_target_pairs={{0,8},{8,0},{16,24},{24,16},{1,9},{9,1},{17,25},{25,17},{2,10},{10... | collective-permute-start | bytes 17301512 | tf_op jit(solution)/shard_map/ppermute | solution.py:550
  398.0 86.4 %all-to-all-start.1 = ((bf16[8,176,2048]{2,1,0:T(8,128)(2,1)}), bf16[8,176,2048]{2,1,0:T(8,128)(2,1)}, u32[]{:S(2)}, u32[]{:S(2)}) async-start(bf16[8,176,2048]{2,1,0:T(8,128)(2,1)} %param.44), calls=%async_computation.1 | async-start | bytes 11534336 | tf_op jit(solution)/shard_map/all_to_all | solution.py:486
  555.8 63.9 %all-to-all-start.3 = ((f32[8,1,256]{2,1,0:T(1,128)}), f32[8,1,256]{2,1,0:T(1,128)S(1)}, u32[]{:S(2)}, u32[]{:S(2)}) async-start(f32[8,1,256]{2,1,0:T(1,128)} %copy.185), calls=%async_computation.3 | async-start | bytes 16384 | tf_op jit(solution)/shard_map/all_to_all | solution.py:486
  619.8 288.7 %all-to-all-start.2 = ((bf16[8,256,2048]{2,1,0:T(8,128)(2,1)}), bf16[8,256,2048]{2,1,0:T(8,128)(2,1)}, u32[]{:S(2)}, u32[]{:S(2)}) async-start(bf16[8,256,2048]{2,1,0:T(8,128)(2,1)} %bitcast.299), calls=%async_computation.2 | async-start | bytes 16777216 | tf_op jit(solution)/shard_map/all_to_all | solution.py:486
  624.9 31.6 %copy-start.60 = (bf16[704,2048]{1,0:T(8,128)(2,1)S(1)}, bf16[704,2048]{1,0:T(8,128)(2,1)}, u32[]{:S(2)}) copy-start(bf16[704,2048]{1,0:T(8,128)(2,1)} %w_down.1) | copy-start | bytes 8650756
  624.9 31.5 %copy-start.62 = (bf16[2048,704]{1,0:T(8,128)(2,1)S(1)}, bf16[2048,704]{1,0:T(8,128)(2,1)}, u32[]{:S(2)}) copy-start(bf16[2048,704]{1,0:T(8,128)(2,1)} %get-tuple-element.167) | copy-start | bytes 8650756
  921.2 22.1 %collective-permute-start.12 = (bf16[256,512]{1,0:T(8,128)(2,1)}, bf16[256,512]{1,0:T(8,128)(2,1)S(1)}, u32[]{:S(2)}, u32[]{:S(2)}) collective-permute-start(bf16[256,512]{1,0:T(8,128)(2,1)} %get-tuple-element.270), channel_id=1, source_target_pairs={{0,8},{8,16},{16,24},{24,0},{1,9},{9,17},{17,25},{25,1},{2,10},{10... | collective-permute-start | bytes 786440 | tf_op jit(solution)/shard_map/ppermute | solution.py:479
  921.2 21.1 %collective-permute-start.11 = (bf16[256,512]{1,0:T(8,128)(2,1)}, bf16[256,512]{1,0:T(8,128)(2,1)}, u32[]{:S(2)}, u32[]{:S(2)}) collective-permute-start(bf16[256,512]{1,0:T(8,128)(2,1)} %get-tuple-element.271), channel_id=1, source_target_pairs={{0,16},{8,24},{16,0},{24,8},{1,17},{9,25},{17,1},{25,9},{2,18},{10... | collective-permute-start | bytes 786440 | tf_op jit(solution)/shard_map/ppermute | solution.py:479
  924.9 13.3 collective-permute-start.10
  931.0 99.0 %all-to-all-start.4 = ((bf16[8,256,2048]{2,1,0:T(8,128)(2,1)}), bf16[8,256,2048]{2,1,0:T(8,128)(2,1)}, u32[]{:S(2)}, u32[]{:S(2)}) async-start(bf16[8,256,2048]{2,1,0:T(8,128)(2,1)} %bitcast.288), calls=%async_computation.4 | async-start | bytes 16777216 | tf_op jit(solution)/shard_map/all_to_all | solution.py:486
  936.0 160.8 %reduce-scatter.8.cloned.1.call-start = ((), (), s32[]{:S(2)}) async-start(), calls=%async_computation.12 | async-start | bytes 7520256 | tf_op jit(solution)/shard_map/reduce_scatter | solution.py:702
  1035.3 648.6 %reduce-scatter.6.cloned.1.call-start = ((), (), s32[]{:S(2)}) async-start(), calls=%async_computation.11 | async-start | bytes 5242880 | tf_op jit(solution)/shard_map/reduce_scatter | solution.py:705
  1035.9 653.0 %reduce-scatter.4.cloned.1.call-start = ((), (), s32[]{:S(2)}) async-start(), calls=%async_computation.10 | async-start | bytes 9437184 | tf_op jit(solution)/shard_map/reduce_scatter | solution.py:706
  1036.6 654.7 %all-gather.18.cloned.1.call-start = ((), (), s32[]{:S(2)}) async-start(), calls=%async_computation.15 | async-start | bytes 4177920 | tf_op jit(solution)/shard_map/all_gather | solution.py:722
  (64 other events, 334.7 us)
Sparse Core Ops, SparseCore 0:
  10.5 54.9 all-gather.13
  67.4 92.4 all-gather.15
  161.7 54.3 all-gather.9
  224.7 54.5 all-gather.11
  1035.4 61.2 reduce-scatter.7
  1098.9 124.4 reduce-scatter.5
  1227.3 133.6 reduce-scatter.3
  1362.5 116.2 all-gather.17

commit v3 on v2

--- a/solution.py
+++ b/solution.py
@@ -391,6 +391,298 @@
     )(*[value for value, _, _ in arrays])[:count]
 
 
+HOST_BLOCKS = 8
+
+
+def feed_forward_kernel(*refs):
+    sources, refs = refs[:3], refs[3:]
+    tiles_in, refs = refs[:5], refs[5:]
+    weights, refs = refs[:5], refs[5:]
+    share, refs = refs[0], refs[1:]
+    results, refs = refs[:3], refs[3:]
+    tiles_out, refs = refs[:4], refs[4:]
+    zg, za, zs, zb, zt = refs[:5]
+    refs = refs[5:]
+    held, refs = refs[:5], refs[5:]
+    v_up, v_down, v_sg, v_sl, v_sd = held
+    loaded, refs = refs[:5], refs[5:]
+    v_x, v_u, v_ga, v_gl, v_in = loaded
+    stored, refs = refs[:4], refs[4:]
+    t_in, t_grads, t_second, t_out = stored
+    (w_sem, l_sem, s_sem, g_sem, a_send, a_recv, b_send, b_recv, c_send, c_recv) = refs[:10]
+    out_sem, a_free, b_free = refs[10:]
+    place = lax.axis_index("seq")
+    middle, partner, across = line_neighbours(place)
+    tile = v_x.shape[1]
+    hidden = v_down.shape[0]
+    last = HOST_BLOCKS - 1
+
+    for index in range(5):
+        pltpu.make_async_copy(weights[index], held[index], w_sem.at[index]).start()
+
+    barrier = pltpu.get_barrier_semaphore()
+    pl.semaphore_signal(
+        barrier, device_id={"seq": partner}, device_id_type=pl.DeviceIdType.MESH
+    )
+
+    @pl.when(middle == 1)
+    def _():
+        pl.semaphore_signal(
+            barrier, device_id={"seq": across}, device_id_type=pl.DeviceIdType.MESH
+        )
+
+    pl.semaphore_wait(barrier, 1 + middle)
+
+    def rows(o):
+        return pl.ds(o * tile if isinstance(o, int) else pl.multiple_of(o * tile, tile), tile)
+
+    def slot(o):
+        return o % 2 if isinstance(o, int) else lax.rem(o, 2)
+
+    def remote(source, target, sent, received, where):
+        return pltpu.make_async_remote_copy(
+            src_ref=source,
+            dst_ref=target,
+            send_sem=sent,
+            recv_sem=received,
+            device_id={"seq": where},
+            device_id_type=pl.DeviceIdType.MESH,
+        )
+
+    def inward(o, a):
+        i = slot(o)
+        return remote(
+            sources[a].at[rows(o)], za.at[i, a], a_send.at[i, a], a_recv.at[i, a], partner
+        )
+
+    def crossing(o, a):
+        i = slot(o)
+        return remote(zs.at[i, a], zb.at[i, a], b_send.at[i, a], b_recv.at[i, a], across)
+
+    def outward(o, a):
+        i = slot(o)
+        return remote(
+            zt.at[i, a], results[a].at[rows(o)], c_send.at[i, a], c_recv.at[o, a], partner
+        )
+
+    def fetch(o, a):
+        i = slot(o)
+        return pltpu.make_async_copy(sources[a].at[rows(o)], zg.at[i, a], g_sem.at[i, a])
+
+    def keep(o, a):
+        i = slot(o)
+        return pltpu.make_async_copy(zt.at[i, a], results[a].at[rows(o)], out_sem.at[i, a])
+
+    def load(o, index):
+        i = slot(o)
+        return pltpu.make_async_copy(
+            tiles_in[index].at[rows(o)], loaded[index].at[i], l_sem.at[i, index]
+        )
+
+    def store(o, index):
+        return pltpu.make_async_copy(stored[index], tiles_out[index].at[rows(o)], s_sem.at[index])
+
+    for index in range(5):
+        load(0, index).start()
+
+    @pl.when(middle == 0)
+    def _():
+        for o in (0, 1):
+            for a in range(3):
+                inward(o, a).start()
+
+    @pl.when(middle == 1)
+    def _():
+        for o in (0, 1):
+            for a in range(3):
+                fetch(o, a).start()
+
+    for index in range(5):
+        pltpu.make_async_copy(weights[index], held[index], w_sem.at[index]).wait()
+
+    def add(left, right):
+        return (left.astype(f32) + right.astype(f32)).astype(bf16)
+
+    def end_step(o):
+        @pl.when((o >= 1) & (o < last))
+        def _():
+            for a in range(3):
+                inward(o - 1, a).wait_send()
+                pl.semaphore_wait(a_free, 1)
+                inward(o + 1, a).start()
+
+    def middle_step(o):
+        @pl.when(o <= last)
+        def _():
+            i = slot(o)
+            for a in range(3):
+                fetch(o, a).wait()
+                inward(o, a).wait_recv()
+
+                @pl.when(o >= 2)
+                def _():
+                    crossing(o - 2, a).wait_send()
+                    pl.semaphore_wait(b_free, 1)
+
+                zs[i, a] = add(zg[i, a], za[i, a])
+                crossing(o, a).start()
+
+                @pl.when(o + 2 <= last)
+                def _():
+                    pl.semaphore_signal(
+                        a_free, device_id={"seq": partner}, device_id_type=pl.DeviceIdType.MESH
+                    )
+                    fetch(o + 2, a).start()
+
+        @pl.when(o >= 1)
+        def _():
+            p = o - 1
+            i = slot(p)
+            for a in range(3):
+                crossing(p, a).wait_recv()
+
+                @pl.when(p >= 2)
+                def _():
+                    keep(p - 2, a).wait()
+                    outward(p - 2, a).wait_send()
+
+                zt[i, a] = add(zs[i, a], zb[i, a])
+
+                @pl.when(p + 2 <= last)
+                def _():
+                    pl.semaphore_signal(
+                        b_free, device_id={"seq": across}, device_id_type=pl.DeviceIdType.MESH
+                    )
+
+                outward(p, a).start()
+                keep(p, a).start()
+
+    def across_rows(left, right):
+        return lax.dot_general(left, right, (((1,), (1,)), ((), ())), preferred_element_type=f32)
+
+    def host(o):
+        i = slot(o)
+        for index in range(5):
+            load(o, index).wait()
+
+        @pl.when(o < last)
+        def _():
+            for index in range(5):
+                load(o + 1, index).start()
+
+        @pl.when(o >= 1)
+        def _():
+            for index in range(4):
+                store(o - 1, index).wait()
+
+        scale = share[rows(o), :]
+        cut = hidden // 256 * 128
+        for first, end in ((0, cut), (cut, hidden)):
+            gate = jnp.dot(v_x[i], v_up[:, first:end], preferred_element_type=f32)
+            lift = jnp.dot(
+                v_x[i], v_up[:, hidden + first : hidden + end], preferred_element_type=f32
+            )
+            grad = across_rows(v_u[i], v_down[first:end, :]) * scale
+            sigma = 1.0 / (1.0 + jnp.exp(-gate))
+            silu = gate * sigma
+            t_in[:, first:end] = (silu * lift * scale).astype(bf16)
+            t_grads[:, first:end] = (
+                grad * lift * sigma * (1.0 + gate * (1.0 - sigma))
+            ).astype(bf16)
+            t_grads[:, hidden + first : hidden + end] = (grad * silu).astype(bf16)
+        for first in range(0, D, 512):
+            end = first + 512
+            t_second[:, first:end] = (
+                across_rows(t_grads[...], v_up[first:end, :])
+                + across_rows(v_ga[i], v_sg[first:end, :])
+                + across_rows(v_gl[i], v_sl[first:end, :])
+            ).astype(bf16)
+            t_out[:, first:end] = (
+                jnp.dot(t_in[...], v_down[:, first:end], preferred_element_type=f32)
+                + jnp.dot(v_in[i], v_sd[:, first:end], preferred_element_type=f32)
+            ).astype(bf16)
+        for index in range(4):
+            store(o, index).start()
+
+    def step(o, carry):
+        @pl.when(middle == 0)
+        def _():
+            end_step(o)
+
+        @pl.when(middle == 1)
+        def _():
+            middle_step(o)
+
+        @pl.when(o <= last)
+        def _():
+            host(o)
+
+        return carry
+
+    lax.fori_loop(0, HOST_BLOCKS + 1, step, 0)
+    for index in range(4):
+        store(last, index).wait()
+
+    @pl.when(middle == 0)
+    def _():
+        for a in range(3):
+            for o in (last - 1, last):
+                inward(o, a).wait_send()
+            for o in range(HOST_BLOCKS):
+                outward(o, a).wait_recv()
+
+    @pl.when(middle == 1)
+    def _():
+        for a in range(3):
+            for o in (last - 1, last):
+                crossing(o, a).wait_send()
+                keep(o, a).wait()
+                outward(o, a).wait_send()
+
+
+def feed_forward(sums, tiles, weights, share, number):
+    rows, cut = sums[0].shape
+    tile = rows // HOST_BLOCKS
+    hidden = weights[1].shape[0]
+    dma = pltpu.SemaphoreType.DMA
+    anywhere = pl.BlockSpec(memory_space=pl.ANY)
+    outs = [hidden, 2 * hidden, D, D]
+    return pl.pallas_call(
+        feed_forward_kernel,
+        out_shape=[jax.ShapeDtypeStruct((rows, cut), bf16)] * 3
+        + [jax.ShapeDtypeStruct((rows, w), bf16) for w in outs],
+        in_specs=[anywhere] * 13 + [pl.BlockSpec(memory_space=pltpu.VMEM)],
+        out_specs=[anywhere] * 7,
+        scratch_shapes=[pltpu.VMEM((2, 3, tile, cut), bf16)] * 5
+        + [pltpu.VMEM(w.shape, bf16) for w in weights]
+        + [pltpu.VMEM((2, tile, t.shape[1]), bf16) for t in tiles]
+        + [pltpu.VMEM((tile, w), bf16) for w in outs]
+        + [
+            dma((5,)),
+            dma((2, 5)),
+            dma((4,)),
+            dma((2, 3)),
+            dma((2, 3)),
+            dma((2, 3)),
+            dma((2, 3)),
+            dma((2, 3)),
+            dma((2, 3)),
+            dma((HOST_BLOCKS, 3)),
+            dma((2, 3)),
+            pltpu.SemaphoreType.REGULAR,
+            pltpu.SemaphoreType.REGULAR,
+        ],
+        compiler_params=pltpu.CompilerParams(
+            collective_id=number, has_side_effects=True, vmem_limit_bytes=60 * 1024 * 1024
+        ),
+        cost_estimate=pl.CostEstimate(
+            flops=2 * rows * D * (6 * hidden + 3 * cut),
+            bytes_accessed=800 * 1024 * 1024,
+            transcendentals=rows * hidden,
+        ),
+    )(*sums, *tiles, *weights, share)
+
+
 def middle_kernel(joined, x, u, w_gate, w_lift, w_down, scale, inner, *outs):
     gate = jnp.dot(x[...], w_gate[...], preferred_element_type=f32)
     lift = jnp.dot(x[...], w_lift[...], preferred_element_type=f32)
@@ -520,7 +812,20 @@
     factor = 1.0 / math.sqrt(HEAD_DIM)
     capacity = length * TOP // EXPERTS
 
-    all_tokens = gather_seq(tokens[0])
+    names = jnp.arange(EXPERTS, dtype=jnp.int32)
+    matches = expert_ids[0][None, :, :] == names[:, None, None]
+    gates = jnp.sum(jnp.where(matches, expert_gates[0][None], 0.0), axis=-1)
+    gates = jnp.where(jnp.any(matches, axis=-1), gates, -1.0)
+    chosen = (gates >= 0.0).astype(jnp.int32)
+    tallies = lax.all_gather(jnp.sum(chosen, axis=1), "seq")
+    before = jnp.arange(seq, dtype=jnp.int32)[:, None] < place
+    offsets = jnp.sum(jnp.where(before, tallies, 0), axis=0)
+    earlier = offsets[:, None] + jnp.cumsum(chosen, axis=1) - chosen
+    gates = jnp.where((chosen > 0) & (earlier < capacity), gates, 0.0)
+    gates = lax.all_gather(gates, "fsdp", axis=0)
+    share = lax.dynamic_index_in_dim(gates, me // copies, 1, keepdims=False).reshape(-1, 1)
+
+    all_tokens = gather_seq(after(tokens[0], gates))
     own = [
         lax.dynamic_slice_in_dim(qkv_weight, part * D + place * group, group, 1)
         for part in range(3)
@@ -529,7 +834,9 @@
     extra = -(-6 * width // (3 * group) // 16) * 16
     vectors = jnp.pad(vectors, (0, extra * 3 * group - 6 * width)).reshape(extra, 3 * group)
     gathered = lax.all_gather(
-        jnp.concatenate([jnp.concatenate(own, axis=1), vectors], axis=0), "fsdp", axis=0
+        after(jnp.concatenate([jnp.concatenate(own, axis=1), vectors], axis=0), gates),
+        "fsdp",
+        axis=0,
     )
     weight_qkv = gathered[:, :width].reshape(D, 3 * group)
     vectors = gathered[:, width:].reshape(fsdp, -1)
@@ -571,75 +878,69 @@
     second = (hidden * scale_two * gain_two).astype(bf16)
     second_all = lax.all_gather(after(second, fetched), "fsdp", axis=0, tiled=True)
 
-    names = jnp.arange(EXPERTS, dtype=jnp.int32)
-    matches = expert_ids[0][None, :, :] == names[:, None, None]
-    gates = jnp.sum(jnp.where(matches, expert_gates[0][None], 0.0), axis=-1)
-    gates = jnp.where(jnp.any(matches, axis=-1), gates, -1.0)
-    gates = lax.all_gather(after(gates.reshape(-1), second), ("seq", "fsdp"), axis=0)
-    gates = gates.reshape(seq, fsdp, EXPERTS, row_count)
-    gates = lax.dynamic_index_in_dim(gates, me // copies, 2, keepdims=False)
-    gates = gates.transpose(1, 0, 2).reshape(fsdp, length)
-    chosen = (gates >= 0.0).astype(jnp.int32)
-    earlier = jnp.cumsum(chosen, axis=1) - chosen
-    share = jnp.where((chosen > 0) & (earlier < capacity), gates, 0.0)
-    share = lax.dynamic_slice_in_dim(share, place * row_count, row_count, 1).reshape(-1, 1)
-
     weight_down = swap(after(down_sent, second_all)).reshape(hidden_own, D)
-    weight_up, fetched = after((given, fetched), second_all)
-    if seq == 4:
-        weight_up = jnp.concatenate(
-            [jnp.where(half == 0, fetched, weight_up), jnp.where(half == 0, weight_up, fetched)],
-            axis=1,
-        )
-    weight_up = weight_up.reshape(D, 2 * hidden_own)
-
     by_kernel = seq == 4 and fsdp == 8
     s_gate, s_lift = shared_gate_up[:, 0], shared_gate_up[:, 1]
     opening_all = jax.nn.sigmoid(dot(second_all, gate_vector, ((1,), (0,))))[:, None]
     inner_s, ga_s, gl_s, reach = middle(
         second_all, upstream_all, s_gate, s_lift, shared_down, opening_all
     )
-    grad_s_down = dot(inner_s, upstream_all, ((0,), (0,)), bf16)
+    grad_s_down = dot(upstream_all, inner_s, ((0,), (0,)), bf16)
     grad_s_gate = dot(second_all, ga_s, ((0,), (0,)), bf16)
     grad_s_lift = dot(second_all, gl_s, ((0,), (0,)), bf16)
 
-    held = after(second_all, grad_s_down, grad_s_gate, grad_s_lift)
-    if hidden_own % 128 == 0:
-        inner_e, grads_e, _ = middle(held, upstream_all, weight_up, None, weight_down, share)
+    weight_up, fetched = after((given, fetched), grad_s_down, grad_s_gate, grad_s_lift)
+    if seq == 4:
+        weight_up = jnp.concatenate(
+            [jnp.where(half == 0, fetched, weight_up), jnp.where(half == 0, weight_up, fetched)],
+            axis=1,
+        )
+    weight_up = weight_up.reshape(D, 2 * hidden_own)
+    if by_kernel:
+        *sum_s, inner_e, grads_e, grad_second_all, out_all = feed_forward(
+            (grad_s_down, grad_s_gate, grad_s_lift),
+            (second_all, upstream_all, ga_s, gl_s, inner_s),
+            (weight_up, weight_down, s_gate, s_lift, shared_down),
+            share,
+            2,
+        )
+        grad_second = scatter(grad_second_all)
+        grad_e_down = dot(inner_e, upstream_all, ((0,), (0,)), bf16)
+        grad_e_up = dot(second_all, after(grads_e, grad_e_down), ((0,), (0,)), bf16)
+        reach = jnp.sum(swap(after(reach.reshape(fsdp, row_count), inner_e)), axis=0)
+        out_all = after(out_all, grad_e_up)
     else:
-        inner_e, ga_e, gl_e, _ = middle(
-            held,
-            upstream_all,
-            weight_up[:, :hidden_own],
-            weight_up[:, hidden_own:],
-            weight_down,
-            share,
-        )
-        grads_e = jnp.concatenate([ga_e, gl_e], axis=1)
-    part = dot(inner_e, upstream_all, ((0,), (0,)), bf16)
-    grad_e_down = part
-    reach = jnp.sum(swap(after(reach.reshape(fsdp, row_count), part)), axis=0)
-
-    grads_e, ga_s, gl_s = after((grads_e, ga_s, gl_s), part)
-    grad_second_all = (
-        dot(ga_s, s_gate, ((1,), (1,)))
-        + dot(gl_s, s_lift, ((1,), (1,)))
-        + dot(grads_e, weight_up, ((1,), (1,)))
-    ).astype(bf16)
-    grad_second = scatter(grad_second_all)
-
-    grad_e_up = dot(second_all, after(grads_e, grad_second_all), ((0,), (0,)), bf16)
-
-    inner_s, inner_e = after((inner_s, inner_e), grad_e_up)
-    out_all = (
-        dot(inner_s, shared_down, ((1,), (0,))) + dot(inner_e, weight_down, ((1,), (0,)))
-    ).astype(bf16)
-
-    if by_kernel:
-        shared = after((grad_s_down, grad_s_gate, grad_s_lift), out_all)
-        sum_s = combine([(shared[0], False, 64), (shared[1], False, 256), (shared[2], False, 256)], 2)
-        out_all = after(out_all, *sum_s)
-    else:
+        held = after(second_all, grad_s_down, grad_s_gate, grad_s_lift)
+        if hidden_own % 128 == 0:
+            inner_e, grads_e, _ = middle(held, upstream_all, weight_up, None, weight_down, share)
+        else:
+            inner_e, ga_e, gl_e, _ = middle(
+                held,
+                upstream_all,
+                weight_up[:, :hidden_own],
+                weight_up[:, hidden_own:],
+                weight_down,
+                share,
+            )
+            grads_e = jnp.concatenate([ga_e, gl_e], axis=1)
+        part = dot(inner_e, upstream_all, ((0,), (0,)), bf16)
+        grad_e_down = part
+        reach = jnp.sum(swap(after(reach.reshape(fsdp, row_count), part)), axis=0)
+
+        grads_e, ga_s, gl_s = after((grads_e, ga_s, gl_s), part)
+        grad_second_all = (
+            dot(ga_s, s_gate, ((1,), (1,)))
+            + dot(gl_s, s_lift, ((1,), (1,)))
+            + dot(grads_e, weight_up, ((1,), (1,)))
+        ).astype(bf16)
+        grad_second = scatter(grad_second_all)
+
+        grad_e_up = dot(second_all, after(grads_e, grad_second_all), ((0,), (0,)), bf16)
+
+        inner_s, inner_e = after((inner_s, inner_e), grad_e_up)
+        out_all = (
+            dot(inner_s, shared_down, ((1,), (0,))) + dot(inner_e, weight_down, ((1,), (0,)))
+        ).astype(bf16)
         sum_s = lax.psum((grad_s_down, grad_s_gate, grad_s_lift), "seq")
 
     grad_second, reach = after((grad_second, reach), out_all)
@@ -719,7 +1020,7 @@
         sum_e_up = sum_e_up.transpose(0, 2, 3, 4, 1, 5).reshape(EXPERTS, width, 2 * FF_EXPERT)
     output = (hidden + out_part.astype(f32)).astype(bf16)
     grad_normed = grad_normed.astype(f32)
-    grad_qkv = lax.all_gather(grad_qkv, "seq", axis=0)
+    grad_qkv = lax.all_gather(after(grad_qkv, sum_out), "seq", axis=0)
     rows = jnp.sum(grad_qkv[:, width:].astype(f32), axis=0).reshape(-1)
     grad_qkv = jnp.concatenate(
         [
@@ -743,7 +1044,7 @@
         sum_out.astype(f32),
         rows[width : 2 * width],
         sum_s_up.astype(f32),
-        sum_s[0].astype(f32),
+        sum_s[0].T.astype(f32),
         rows[2 * width : 3 * width],
         sum_e_up.astype(f32),
         sum_e_down.astype(f32),

time: 1730 us -> 1510 us (0.87)
  blocking collectives: 143 us -> 20.1 us
  matrix products: 250 us -> 161 us
  Pallas kernels: 843 us -> 784 us
  waiting for transfers between devices: 197 us -> 250 us
    pallas_call x2 -> x1, Pallas kernels: 761 us -> 497 us  [combine(): pl.pallas_call(functools.partial(combine_kernel, tuple(plan)), out_shape=...]
    pallas_call x0 -> x1, Pallas kernels: none -> 258 us  [feed_forward(): pl.pallas_call(feed_forward_kernel, out_shape=[jax.ShapeDtypeStruct((rows...]
    all_gather x1, blocking collectives: 143 us -> 10.2 us  [on_device(): gates = lax.all_gather(gates, 'fsdp', axis=0)]
    dot_general x18 -> x13, matrix products: 226 us -> 137 us  [dot(): lax.dot_general(a, b, (contract, ((), ())), preferred_element_type=f32)]
    all_to_all x5, waiting for transfers between devices: 13.4 us -> 83.6 us  [swap(): return lax.all_to_all(value, 'fsdp', 0, 0, tiled=True)]
    reduce_scatter x1, waiting for transfers between devices: 60.1 us -> 0.02 us  [on_device(): lax.psum_scatter(grad_qkv.reshape(-1, 3 * group), 'fsdp', scatter_dimensi...]
    pallas_call x2 -> x1, Pallas kernels: 81.9 us -> 29.3 us  [middle(): pl.pallas_call(functools.partial(middle_kernel, joined), grid=(rows // ti...]
    all_gather x1, waiting for transfers between devices: 0.01 us -> 32.5 us  [on_device(): lax.all_gather(after(second, fetched), 'fsdp', axis=0, tiled=True)]
  transfers between devices with their start and end apart: 26 -> 26, of which waited for: 10 -> 13; matrix products, arithmetic and copies ran while one was open for 23% -> 22% of each run, Pallas kernels for 46% -> 35%
where the time goes in v3:
time: 1510 us; the launch traced here: 1500 us
  Pallas kernels  784 us (52%)
  waiting for transfers between devices  250 us (17%)
  matrix products  161 us (11%)
  other arithmetic  120 us (8%)
  local copies, waits for them, and re-layouts  109 us (7%)
  starting transfers between devices  41.3 us (3%)
  blocking collectives  20.1 us (1%)
  between operations  16.7 us (1%)
    pallas_call x1, Pallas kernels, combine(): pl.pallas_call(functools.partial(combine_kernel, tuple(plan)), out_shape=...  497 us
    pallas_call x1, Pallas kernels, feed_forward(): pl.pallas_call(feed_forward_kernel, out_shape=[jax.ShapeDtypeStruct((rows...  258 us
    dot_general x13, matrix products, dot(): lax.dot_general(a, b, (contract, ((), ())), preferred_element_type=f32)  137 us
    all_to_all x5, waiting for transfers between devices, swap(): return lax.all_to_all(value, 'fsdp', 0, 0, tiled=True)  83.6 us
    unnamed x169, local copies, waits for them, and re-layouts  53 us
    ppermute x3, waiting for transfers between devices, gather_seq(): down = lax.ppermute(down, 'seq', [(i + 1, i) for i in range(seq - 1 - hop)])  46.7 us
    all_gather x1, waiting for transfers between devices, on_device(): lax.all_gather(after(second, fetched), 'fsdp', axis=0, tiled=True)  32.5 us
  transfers between devices with their start and end apart: 26, of which 13 were waited for; matrix products, arithmetic and copies ran while one was open for 22% of the time, Pallas kernels for 35%

profile of v3, /device:TPU:0, one launch (start us, length us, event | category | flops | bytes accessed | tf_op | source)
XLA Modules:
  0.0 1502.0 jit_solution(44854802508399629)
XLA Ops:
  11.0 9.9 all-reduce.4
  22.8 10.2 all_gather.33
  40.8 21.5 %collective-permute-done = bf16[256,2048]{1,0:T(8,128)(2,1)S(1)} collective-permute-done((bf16[256,2048]{1,0:T(8,128)(2,1)S(1)}, bf16[256,2048]{1,0:T(8,128)(2,1)S(1)}, u32[]{:S(2)}, u32[]{:S(2)}) %collective-permute-start) | collective-permute-done | bytes 1048608 | tf_op jit(solution)/shard_map/ppermute | solution.py:751
  82.1 23.2 %collective-permute-done.4 = bf16[256,2048]{1,0:T(8,128)(2,1)S(1)} collective-permute-done((bf16[256,2048]{1,0:T(8,128)(2,1)S(1)}, bf16[256,2048]{1,0:T(8,128)(2,1)S(1)}, u32[]{:S(2)}, u32[]{:S(2)}) %collective-permute-start.4) | collective-permute-done | bytes 1048608 | tf_op jit(solution)/shard_map/ppermute | solution.py:752
  108.5 23.6 %collective-permute-done.5 = bf16[256,2048]{1,0:T(8,128)(2,1)S(1)} collective-permute-done((bf16[256,2048]{1,0:T(8,128)(2,1)S(1)}, bf16[256,2048]{1,0:T(8,128)(2,1)S(1)}, u32[]{:S(2)}, u32[]{:S(2)}) %collective-permute-start.5) | collective-permute-done | bytes 1048608 | tf_op jit(solution)/shard_map/ppermute | solution.py:752
  149.4 8.5 convolution_add_fusion
  157.9 7.7 reshape.960
  165.5 7.0 copy.228
  197.9 16.0 %collective-permute-done.7 = bf16[256,512]{0,1:T(8,128)(2,1)S(1)} collective-permute-done((bf16[256,512]{0,1:T(8,128)(2,1)S(1)}, bf16[256,512]{0,1:T(8,128)(2,1)S(1)}, u32[]{:S(2)}, u32[]{:S(2)}) %collective-permute-start.7) | collective-permute-done | bytes 262176 | tf_op jit(solution)/shard_map/ppermute | solution.py:771
  214.3 22.3 %all-gather.10.cloned.1.call-done = bf16[2048,2048]{1,0:T(8,128)(2,1)} async-done(((bf16[256,2048]{1,0:T(8,128)(2,1)}), bf16[2048,2048]{1,0:T(8,128)(2,1)}) %all-gather.10.cloned.1.call-update) | async-done | bytes 8388624 | tf_op jit(solution)/shard_map/all_gather | solution.py:848
  267.0 32.5 %all-gather.12.cloned.1.call-done.x.refs_3_ = bf16[2048,2048]{1,0:T(8,128)(2,1)} async-done(((bf16[256,2048]{1,0:T(8,128)(2,1)}), bf16[2048,2048]{1,0:T(8,128)(2,1)}) %all-gather.12.cloned.1.call-update) | async-done | bytes 8388624 | tf_op jit(solution)/shard_map/all_gather | solution.py:879
  311.2 29.3 %shard_map.238 = (bf16[2048,704]{1,0:T(8,128)(2,1)}, bf16[2048,704]{1,0:T(8,128)(2,1)}, bf16[2048,704]{1,0:T(8,128)(2,1)}, f32[2048,1]{1,0:T(8,128)S(1)}) custom-call(bf16[2048,2048]{1,0:T(8,128)(2,1)} %all-gather.12.cloned.1.call-done.x.refs_3_, bf16[2048,2048]{1,0:T(8,128)(2,1)} %bitcast.357, bf16[2048,704]{1,0:T(8,128)(2,1)} %bitcast.308, ...), custom_call_target="tpu_custom_call" | custom-call | flops 17716740096 | bytes 34078720 | tf_op jit(solution)/shard_map/pallas_call | solution.py:715
  340.9 9.6 convolution_convert_fusion.6
  353.3 11.5 convolution_convert_fusion.5.refs_1_
  364.8 10.9 convolution_convert_fusion.4.refs_2_
  375.7 11.3 collective-permute-done.9
  387.0 9.5 broadcast_select_fusion.1
  396.5 10.0 pad_maximum_fusion
  406.5 258.2 %shard_map.239 = (bf16[2048,704]{1,0:T(8,128)(2,1)}, bf16[2048,704]{1,0:T(8,128)(2,1)}, bf16[2048,704]{1,0:T(8,128)(2,1)}, bf16[2048,1408]{1,0:T(8,128)(2,1)}, b...) custom-call(bf16[2048,704]{1,0:T(8,128)(2,1)} %bitcast.310, ...), custom_call_target="tpu_custom_call" | custom-call | flops 88583700480 | bytes 838860800 | tf_op jit(solution)/shard_map/pallas_call | solution.py:650
  668.8 17.9 %convolution_convert_fusion.3.refs_1_ = bf16[1408,2048]{1,0:T(8,128)(2,1)} fusion(bf16[2048,1408]{1,0:T(8,128)(2,1)} %get-tuple-element.155, bf16[1,2048,2048]{2,1,0:T(8,128)(2,1)} %all-gather.16.cloned.1.call-done), kind=kOutput, calls=%fused_computation.12 | convolution fusion | flops 11814043648 | bytes 19922944 | tf_op jit(solution)/shard_map/dot_general | solution.py:28
  691.7 31.6 %convolution_convert_fusion.refs_0_ = bf16[2048,2816]{1,0:T(8,128)(2,1)} fusion(bf16[2048,2048]{1,0:T(8,128)(2,1)} %all-gather.12.cloned.1.call-done.x.refs_3_, bf16[2048,2816]{1,0:T(8,128)(2,1)} %get-tuple-element.156), kind=kOutput, calls=%fused_computation.2 | convolution fusion | flops 23628087296 | bytes 31457280 | tf_op jit(solution)/shard_map/dot_general | solution.py:28
  723.4 62.4 %all-to-all-done.2 = bf16[8,256,2048]{2,1,0:T(8,128)(2,1)} async-done(((bf16[8,256,2048]{2,1,0:T(8,128)(2,1)}), bf16[8,256,2048]{2,1,0:T(8,128)(2,1)}, u32[]{:S(2)}, u32[]{:S(2)}) %all-to-all-start.2) | async-done | bytes 8388640 | tf_op jit(solution)/shard_map/all_to_all | solution.py:778
  853.3 14.5 fusion.126
  868.0 11.0 convolution_convert_fusion.1
  879.0 6.2 pad_maximum_fusion.1
  885.2 21.2 %all-to-all-done.4 = bf16[8,256,2048]{2,1,0:T(8,128)(2,1)} async-done(((bf16[8,256,2048]{2,1,0:T(8,128)(2,1)}), bf16[8,256,2048]{2,1,0:T(8,128)(2,1)}, u32[]{:S(2)}, u32[]{:S(2)}) %all-to-all-start.4) | async-done | bytes 8388640 | tf_op jit(solution)/shard_map/all_to_all | solution.py:778
  913.0 497.0 %combine_1.1 = (bf16[2048,2816]{1,0:T(8,128)(2,1)}, bf16[1408,2048]{1,0:T(8,128)(2,1)}, bf16[256,2048]{1,0:T(8,128)(2,1)S(1)}, bf16[2048,2816]{1,0:T(8,128)(2,1)...) custom-call(bf16[2048,2816]{1,0:T(8,128)(2,1)} %convolution_convert_fusion.refs_0_, ...), custom_call_target="tpu_custom_call" | custom-call | flops 18350080 | bytes 1835008000 | tf_op jit(solution)/shard_map/combine_1/pallas_call | solution.py:364
  1415.1 6.5 copy.277
  1421.6 8.6 maximum_convert_fusion.1
  1430.2 12.2 copy.276
  1444.0 8.7 convert.62
  1452.6 13.0 convert.61
  (367 shorter events, 242.0 us)
Async XLA Ops:
  7.2 128.9 %all-gather.14.cloned.1.call-start = ((), (), s32[]{:S(2)}) async-start(), calls=%async_computation.13 | async-start | bytes 7520256 | tf_op jit(solution)/shard_map/all_gather | solution.py:836
  35.1 179.1 %all-gather.16.cloned.1.call-start = ((), (), s32[]{:S(2)}) async-start(), calls=%async_computation.14 | async-start | bytes 9437184 | tf_op jit(solution)/shard_map/all_gather | solution.py:849
  35.9 26.4 %collective-permute-start = (bf16[256,2048]{1,0:T(8,128)(2,1)S(1)}, bf16[256,2048]{1,0:T(8,128)(2,1)S(1)}, u32[]{:S(2)}, u32[]{:S(2)}) collective-permute-start(bf16[256,2048]{1,0:T(8,128)(2,1)S(1)} %bitcast.275), channel_id=1, source_target_pairs={{0,8},{8,16},{16,24},{1,9},{9,17},{17,25},{2,10},{10,18},{18,26},{... | collective-permute-start | bytes 3145736 | tf_op jit(solution)/shard_map/ppermute | solution.py:751
  39.5 36.0 %collective-permute-start.3 = (bf16[256,2048]{1,0:T(8,128)(2,1)S(1)}, bf16[256,2048]{1,0:T(8,128)(2,1)S(1)}, u32[]{:S(2)}, u32[]{:S(2)}) collective-permute-start(bf16[256,2048]{1,0:T(8,128)(2,1)S(1)} %bitcast.276), channel_id=1, source_target_pairs={{8,0},{16,8},{24,16},{9,1},{17,9},{25,17},{10,2},{18,10},{26,18},{... | collective-permute-start | bytes 3145736 | tf_op jit(solution)/shard_map/ppermute | solution.py:752
  62.3 14.7 collective-permute-start.1
  69.5 175.5 %all-to-all-start = ((bf16[8,128,2816]{2,1,0:T(8,128)(2,1)}), bf16[8,128,2816]{2,1,0:T(8,128)(2,1)}, u32[]{:S(2)}, u32[]{:S(2)}) async-start(bf16[8,128,2816]{2,1,0:T(8,128)(2,1)} %constant_dynamic-slice_fusion.5), calls=%async_computation | async-start | bytes 11534336 | tf_op jit(solution)/shard_map/all_to_all | solution.py:778
  74.4 162.1 %all-gather.10.cloned.1.call-start = ((), (), s32[]{:S(2)}) async-start(), calls=%async_computation.8 | async-start | bytes 9437184 | tf_op jit(solution)/shard_map/all_gather | solution.py:848
  75.1 224.4 %all-gather.12.cloned.1.call-start = ((), (), s32[]{:S(2)}) async-start(), calls=%async_computation.9 | async-start | bytes 9437184 | tf_op jit(solution)/shard_map/all_gather | solution.py:879
  75.5 29.7 %collective-permute-start.4 = (bf16[256,2048]{1,0:T(8,128)(2,1)S(1)}, bf16[256,2048]{1,0:T(8,128)(2,1)S(1)}, u32[]{:S(2)}, u32[]{:S(2)}) collective-permute-start(bf16[256,2048]{1,0:T(8,128)(2,1)S(1)} %collective-permute-done.3), channel_id=1, source_target_pairs={{8,0},{16,8},{9,1},{17,9},{10,2},{18,10},{11,3},{19,11},{12,4},{20... | collective-permute-start | bytes 3145736 | tf_op jit(solution)/shard_map/ppermute | solution.py:752
  76.9 29.6 %collective-permute-start.2 = (bf16[256,2048]{1,0:T(8,128)(2,1)}, bf16[256,2048]{1,0:T(8,128)(2,1)S(1)}, u32[]{:S(2)}, u32[]{:S(2)}) collective-permute-start(bf16[256,2048]{1,0:T(8,128)(2,1)} %collective-permute-done.1), channel_id=1, source_target_pairs={{16,24},{17,25},{18,26},{19,27},{20,28},{21,29},{22,30},{23,31}} | collective-permute-start | bytes 3145736 | tf_op jit(solution)/shard_map/ppermute | solution.py:751
  79.9 96.9 %copy-start.19 = (f32[1024,128]{1,0:T(8,128)}, f32[1024,128]{1,0:T(8,128)S(1)}, u32[]{:S(2)}) copy-start(f32[1024,128]{1,0:T(8,128)S(1)} %get-tuple-element.284) | copy-start | bytes 1572868
  79.9 96.9 %copy-start.22 = (f32[1024,128]{1,0:T(8,128)}, f32[1024,128]{1,0:T(8,128)S(1)}, u32[]{:S(2)}) copy-start(f32[1024,128]{1,0:T(8,128)S(1)} %get-tuple-element.285) | copy-start | bytes 1572868
  105.2 26.8 %collective-permute-start.5 = (bf16[256,2048]{1,0:T(8,128)(2,1)S(1)}, bf16[256,2048]{1,0:T(8,128)(2,1)S(1)}, u32[]{:S(2)}, u32[]{:S(2)}) collective-permute-start(bf16[256,2048]{1,0:T(8,128)(2,1)S(1)} %collective-permute-done.4), channel_id=1, source_target_pairs={{8,0},{9,1},{10,2},{11,3},{12,4},{13,5},{14,6},{15,7}} | collective-permute-start | bytes 3145736 | tf_op jit(solution)/shard_map/ppermute | solution.py:752
  190.2 7.7 collective-permute-start.6
  190.2 23.8 %collective-permute-start.7 = (bf16[256,512]{0,1:T(8,128)(2,1)S(1)}, bf16[256,512]{0,1:T(8,128)(2,1)S(1)}, u32[]{:S(2)}, u32[]{:S(2)}) collective-permute-start(bf16[256,512]{0,1:T(8,128)(2,1)S(1)} %get-tuple-element.278), channel_id=1, source_target_pairs={{0,16},{8,24},{16,0},{24,8},{1,17},{9,25},{17,1},{25,9},{2,18},{10... | collective-permute-start | bytes 786440 | tf_op jit(solution)/shard_map/ppermute | solution.py:771
  191.1 22.9 %collective-permute-start.8 = (bf16[256,512]{0,1:T(8,128)(2,1)S(1)}, bf16[256,512]{0,1:T(8,128)(2,1)S(1)}, u32[]{:S(2)}, u32[]{:S(2)}) collective-permute-start(bf16[256,512]{0,1:T(8,128)(2,1)S(1)} %get-tuple-element.277), channel_id=1, source_target_pairs={{0,8},{8,16},{16,24},{24,0},{1,9},{9,17},{17,25},{25,1},{2,10},{10... | collective-permute-start | bytes 786440 | tf_op jit(solution)/shard_map/ppermute | solution.py:771
  260.2 126.8 %collective-permute-start.9 = (bf16[8,128,2816]{2,1,0:T(8,128)(2,1)}, bf16[8,128,2816]{2,1,0:T(8,128)(2,1)}, u32[]{:S(2)}, u32[]{:S(2)}) collective-permute-start(bf16[8,128,2816]{2,1,0:T(8,128)(2,1)} %all-to-all-done), channel_id=1, source_target_pairs={{0,8},{8,0},{16,24},{24,16},{1,9},{9,1},{17,25},{25,17},{2,10},{10... | collective-permute-start | bytes 17301512 | tf_op jit(solution)/shard_map/ppermute | solution.py:857
  305.2 101.3 %all-to-all-start.1 = ((bf16[8,176,2048]{2,1,0:T(8,128)(2,1)}), bf16[8,176,2048]{2,1,0:T(8,128)(2,1)}, u32[]{:S(2)}, u32[]{:S(2)}) async-start(bf16[8,176,2048]{2,1,0:T(8,128)(2,1)} %param.44), calls=%async_computation.1 | async-start | bytes 11534336 | tf_op jit(solution)/shard_map/all_to_all | solution.py:778
  665.3 21.4 %all-to-all-start.3 = ((f32[8,1,256]{2,1,0:T(1,128)}), f32[8,1,256]{2,1,0:T(1,128)S(1)}, u32[]{:S(2)}, u32[]{:S(2)}) async-start(f32[8,1,256]{2,1,0:T(1,128)} %copy.239), calls=%async_computation.3 | async-start | bytes 16384 | tf_op jit(solution)/shard_map/all_to_all | solution.py:778
  686.7 99.0 %all-to-all-start.2 = ((bf16[8,256,2048]{2,1,0:T(8,128)(2,1)}), bf16[8,256,2048]{2,1,0:T(8,128)(2,1)}, u32[]{:S(2)}, u32[]{:S(2)}) async-start(bf16[8,256,2048]{2,1,0:T(8,128)(2,1)} %bitcast.282), calls=%async_computation.2 | async-start | bytes 16777216 | tf_op jit(solution)/shard_map/all_to_all | solution.py:778
  723.3 68.1 %copy-start.1 = (f32[256,2048]{1,0:T(8,128)S(1)}, f32[256,2048]{1,0:T(8,128)}, u32[]{:S(2)}) copy-start(f32[256,2048]{1,0:T(8,128)} %copy-done) | copy-start | bytes 6291460
  723.3 68.1 %copy-start.40 = (f32[1,2,8,128]{3,1,2,0:T(2,128)S(1)}, f32[1,2,8,128]{3,1,2,0:T(2,128)}, u32[]{:S(2)}) copy-start(f32[1,2,8,128]{3,1,2,0:T(2,128)} %copy-done.39) | copy-start | bytes 24580
  723.3 68.1 %copy-start.41 = (f32[2048]{0:T(1024)S(1)}, f32[2048]{0:T(1024)}, u32[]{:S(2)}) copy-start(f32[2048]{0:T(1024)} %convert_element_type.332) | copy-start | bytes 24580
  723.4 68.1 %copy-start.55 = (f32[256]{0:T(256)S(1)}, f32[256]{0:T(256)}, u32[]{:S(2)}) copy-start(f32[256]{0:T(256)} %copy-done.54) | copy-start | bytes 3076
  797.7 18.4 %collective-permute-start.12 = (bf16[256,512]{1,0:T(8,128)(2,1)S(1)}, bf16[256,512]{1,0:T(8,128)(2,1)S(1)}, u32[]{:S(2)}, u32[]{:S(2)}) collective-permute-start(bf16[256,512]{1,0:T(8,128)(2,1)S(1)} %get-tuple-element.274), channel_id=1, source_target_pairs={{0,8},{8,16},{16,24},{24,0},{1,9},{9,17},{17,25},{25,1},{2,10},{10... | collective-permute-start | bytes 786440 | tf_op jit(solution)/shard_map/ppermute | solution.py:771
  797.8 18.3 %collective-permute-start.11 = (bf16[256,512]{1,0:T(8,128)(2,1)S(1)}, bf16[256,512]{1,0:T(8,128)(2,1)S(1)}, u32[]{:S(2)}, u32[]{:S(2)}) collective-permute-start(bf16[256,512]{1,0:T(8,128)(2,1)S(1)} %get-tuple-element.275), channel_id=1, source_target_pairs={{0,16},{8,24},{16,0},{24,8},{1,17},{9,25},{17,1},{25,9},{2,18},{10... | collective-permute-start | bytes 786440 | tf_op jit(solution)/shard_map/ppermute | solution.py:771
  800.7 12.4 collective-permute-start.10
  807.4 99.1 %all-to-all-start.4 = ((bf16[8,256,2048]{2,1,0:T(8,128)(2,1)}), bf16[8,256,2048]{2,1,0:T(8,128)(2,1)}, u32[]{:S(2)}, u32[]{:S(2)}) async-start(bf16[8,256,2048]{2,1,0:T(8,128)(2,1)} %bitcast.272), calls=%async_computation.4 | async-start | bytes 16777216 | tf_op jit(solution)/shard_map/all_to_all | solution.py:778
  812.3 597.7 %reduce-scatter.8.cloned.1.call-start = ((), (), s32[]{:S(2)}) async-start(), calls=%async_computation.12 | async-start | bytes 7520256 | tf_op jit(solution)/shard_map/reduce_scatter | solution.py:1003
  911.7 554.0 %reduce-scatter.6.cloned.1.call-start = ((), (), s32[]{:S(2)}) async-start(), calls=%async_computation.11 | async-start | bytes 5242880 | tf_op jit(solution)/shard_map/reduce_scatter | solution.py:1006
  912.2 558.5 %reduce-scatter.4.cloned.1.call-start = ((), (), s32[]{:S(2)}) async-start(), calls=%async_computation.10 | async-start | bytes 9437184 | tf_op jit(solution)/shard_map/reduce_scatter | solution.py:1007
  913.0 564.6 %all-gather.18.cloned.1.call-start = ((), (), s32[]{:S(2)}) async-start(), calls=%async_computation.15 | async-start | bytes 4177920 | tf_op jit(solution)/shard_map/all_gather | solution.py:1023
  (57 other events, 442.1 us)
Sparse Core Ops, SparseCore 0:
  35.3 46.9 all-gather.13
  84.1 96.0 all-gather.15
  182.1 54.3 all-gather.9
  245.1 54.3 all-gather.11
  911.8 88.6 reduce-scatter.7
  1002.6 142.1 reduce-scatter.5
  1148.6 75.5 reduce-scatter.3
  1410.2 67.3 all-gather.17

commit v4 on v3

--- a/solution.py
+++ b/solution.py
@@ -392,13 +392,14 @@
 
 
 HOST_BLOCKS = 8
+SUM_BLOCKS = 16
 
 
 def feed_forward_kernel(*refs):
     sources, refs = refs[:3], refs[3:]
     tiles_in, refs = refs[:5], refs[5:]
-    weights, refs = refs[:5], refs[5:]
-    share, refs = refs[0], refs[1:]
+    near, far, *weights = refs[:6]
+    share, refs = refs[6], refs[7:]
     results, refs = refs[:3], refs[3:]
     tiles_out, refs = refs[:4], refs[4:]
     zg, za, zs, zb, zt = refs[:5]
@@ -415,10 +416,29 @@
     middle, partner, across = line_neighbours(place)
     tile = v_x.shape[1]
     hidden = v_down.shape[0]
-    last = HOST_BLOCKS - 1
-
-    for index in range(5):
-        pltpu.make_async_copy(weights[index], held[index], w_sem.at[index]).start()
+    last = SUM_BLOCKS - 1
+    pace = SUM_BLOCKS // HOST_BLOCKS
+    block = za.shape[2]
+
+    half = lax.rem(place, 2)
+    cut_rows = v_up.shape[0] // 16
+    copies = [
+        pltpu.make_async_copy(weights[index], held[index + 1], w_sem.at[index])
+        for index in range(4)
+    ]
+    for owner in range(8):
+        source = pl.ds(owner * cut_rows, cut_rows)
+        for which, (ref, side) in enumerate(((near, half), (far, 1 - half))):
+            first = pl.multiple_of((2 * owner + side) * cut_rows, cut_rows)
+            copies.append(
+                pltpu.make_async_copy(
+                    ref.at[source],
+                    v_up.at[pl.ds(first, cut_rows)],
+                    w_sem.at[4 + 2 * owner + which],
+                )
+            )
+    for copy in copies:
+        copy.start()
 
     barrier = pltpu.get_barrier_semaphore()
     pl.semaphore_signal(
@@ -433,8 +453,8 @@
 
     pl.semaphore_wait(barrier, 1 + middle)
 
-    def rows(o):
-        return pl.ds(o * tile if isinstance(o, int) else pl.multiple_of(o * tile, tile), tile)
+    def rows(o, size=block):
+        return pl.ds(o * size if isinstance(o, int) else pl.multiple_of(o * size, size), size)
 
     def slot(o):
         return o % 2 if isinstance(o, int) else lax.rem(o, 2)
@@ -476,11 +496,11 @@
     def load(o, index):
         i = slot(o)
         return pltpu.make_async_copy(
-            tiles_in[index].at[rows(o)], loaded[index].at[i], l_sem.at[i, index]
+            tiles_in[index].at[rows(o, tile)], loaded[index].at[i], l_sem.at[i, index]
         )
 
     def store(o, index):
-        return pltpu.make_async_copy(stored[index], tiles_out[index].at[rows(o)], s_sem.at[index])
+        return pltpu.make_async_copy(stored[index], tiles_out[index].at[rows(o, tile)], s_sem.at[index])
 
     for index in range(5):
         load(0, index).start()
@@ -497,8 +517,8 @@
             for a in range(3):
                 fetch(o, a).start()
 
-    for index in range(5):
-        pltpu.make_async_copy(weights[index], held[index], w_sem.at[index]).wait()
+    for copy in copies:
+        copy.wait()
 
     def add(left, right):
         return (left.astype(f32) + right.astype(f32)).astype(bf16)
@@ -565,7 +585,7 @@
         for index in range(5):
             load(o, index).wait()
 
-        @pl.when(o < last)
+        @pl.when(o < HOST_BLOCKS - 1)
         def _():
             for index in range(5):
                 load(o + 1, index).start()
@@ -575,7 +595,7 @@
             for index in range(4):
                 store(o - 1, index).wait()
 
-        scale = share[rows(o), :]
+        scale = share[rows(o, tile), :]
         cut = hidden // 256 * 128
         for first, end in ((0, cut), (cut, hidden)):
             gate = jnp.dot(v_x[i], v_up[:, first:end], preferred_element_type=f32)
@@ -613,22 +633,22 @@
         def _():
             middle_step(o)
 
-        @pl.when(o <= last)
+        @pl.when((o <= last) & (lax.rem(o, pace) == 0))
         def _():
-            host(o)
+            host(o // pace)
 
         return carry
 
-    lax.fori_loop(0, HOST_BLOCKS + 1, step, 0)
+    lax.fori_loop(0, SUM_BLOCKS + 1, step, 0)
     for index in range(4):
-        store(last, index).wait()
+        store(HOST_BLOCKS - 1, index).wait()
 
     @pl.when(middle == 0)
     def _():
         for a in range(3):
             for o in (last - 1, last):
                 inward(o, a).wait_send()
-            for o in range(HOST_BLOCKS):
+            for o in range(SUM_BLOCKS):
                 outward(o, a).wait_recv()
 
     @pl.when(middle == 1)
@@ -643,7 +663,7 @@
 def feed_forward(sums, tiles, weights, share, number):
     rows, cut = sums[0].shape
     tile = rows // HOST_BLOCKS
-    hidden = weights[1].shape[0]
+    hidden = weights[2].shape[0]
     dma = pltpu.SemaphoreType.DMA
     anywhere = pl.BlockSpec(memory_space=pl.ANY)
     outs = [hidden, 2 * hidden, D, D]
@@ -651,14 +671,15 @@
         feed_forward_kernel,
         out_shape=[jax.ShapeDtypeStruct((rows, cut), bf16)] * 3
         + [jax.ShapeDtypeStruct((rows, w), bf16) for w in outs],
-        in_specs=[anywhere] * 13 + [pl.BlockSpec(memory_space=pltpu.VMEM)],
+        in_specs=[anywhere] * 14 + [pl.BlockSpec(memory_space=pltpu.VMEM)],
         out_specs=[anywhere] * 7,
-        scratch_shapes=[pltpu.VMEM((2, 3, tile, cut), bf16)] * 5
-        + [pltpu.VMEM(w.shape, bf16) for w in weights]
+        scratch_shapes=[pltpu.VMEM((2, 3, rows // SUM_BLOCKS, cut), bf16)] * 5
+        + [pltpu.VMEM((D, 2 * hidden), bf16)]
+        + [pltpu.VMEM(w.shape, bf16) for w in weights[2:]]
         + [pltpu.VMEM((2, tile, t.shape[1]), bf16) for t in tiles]
         + [pltpu.VMEM((tile, w), bf16) for w in outs]
         + [
-            dma((5,)),
+            dma((20,)),
             dma((2, 5)),
             dma((4,)),
             dma((2, 3)),
@@ -667,7 +688,7 @@
             dma((2, 3)),
             dma((2, 3)),
             dma((2, 3)),
-            dma((HOST_BLOCKS, 3)),
+            dma((SUM_BLOCKS, 3)),
             dma((2, 3)),
             pltpu.SemaphoreType.REGULAR,
             pltpu.SemaphoreType.REGULAR,
@@ -778,9 +799,8 @@
     return lax.all_to_all(value, "fsdp", 0, 0, tiled=True)
 
 
-def scatter(value):
-    size = lax.axis_size("fsdp")
-    return jnp.sum(swap(value.reshape(size, -1, value.shape[-1])).astype(f32), axis=0)
+def sum_fsdp(value):
+    return lax.psum_scatter(value, "fsdp", scatter_dimension=0, tiled=True)
 
 
 def on_device(
@@ -825,7 +845,7 @@
     gates = lax.all_gather(gates, "fsdp", axis=0)
     share = lax.dynamic_index_in_dim(gates, me // copies, 1, keepdims=False).reshape(-1, 1)
 
-    all_tokens = gather_seq(after(tokens[0], gates))
+    all_tokens = gather_seq(tokens[0])
     own = [
         lax.dynamic_slice_in_dim(qkv_weight, part * D + place * group, group, 1)
         for part in range(3)
@@ -889,27 +909,35 @@
     grad_s_gate = dot(second_all, ga_s, ((0,), (0,)), bf16)
     grad_s_lift = dot(second_all, gl_s, ((0,), (0,)), bf16)
 
-    weight_up, fetched = after((given, fetched), grad_s_down, grad_s_gate, grad_s_lift)
-    if seq == 4:
-        weight_up = jnp.concatenate(
-            [jnp.where(half == 0, fetched, weight_up), jnp.where(half == 0, weight_up, fetched)],
-            axis=1,
-        )
-    weight_up = weight_up.reshape(D, 2 * hidden_own)
+    given, fetched = after((given, fetched), grad_s_down, grad_s_gate, grad_s_lift)
     if by_kernel:
         *sum_s, inner_e, grads_e, grad_second_all, out_all = feed_forward(
             (grad_s_down, grad_s_gate, grad_s_lift),
             (second_all, upstream_all, ga_s, gl_s, inner_s),
-            (weight_up, weight_down, s_gate, s_lift, shared_down),
+            (
+                fetched.reshape(D // 2, -1),
+                given.reshape(D // 2, -1),
+                weight_down,
+                s_gate,
+                s_lift,
+                shared_down,
+            ),
             share,
             2,
         )
-        grad_second = scatter(grad_second_all)
+        grad_second = sum_fsdp(grad_second_all)
         grad_e_down = dot(inner_e, upstream_all, ((0,), (0,)), bf16)
         grad_e_up = dot(second_all, after(grads_e, grad_e_down), ((0,), (0,)), bf16)
         reach = jnp.sum(swap(after(reach.reshape(fsdp, row_count), inner_e)), axis=0)
         out_all = after(out_all, grad_e_up)
     else:
+        weight_up = given
+        if seq == 4:
+            weight_up = jnp.concatenate(
+                [jnp.where(half == 0, fetched, given), jnp.where(half == 0, given, fetched)],
+                axis=1,
+            )
+        weight_up = weight_up.reshape(D, 2 * hidden_own)
         held = after(second_all, grad_s_down, grad_s_gate, grad_s_lift)
         if hidden_own % 128 == 0:
             inner_e, grads_e, _ = middle(held, upstream_all, weight_up, None, weight_down, share)
@@ -933,7 +961,7 @@
             + dot(gl_s, s_lift, ((1,), (1,)))
             + dot(grads_e, weight_up, ((1,), (1,)))
         ).astype(bf16)
-        grad_second = scatter(grad_second_all)
+        grad_second = sum_fsdp(grad_second_all)
 
         grad_e_up = dot(second_all, after(grads_e, grad_second_all), ((0,), (0,)), bf16)
 
@@ -947,7 +975,7 @@
     upstream = cotangent[0].astype(f32)
     opening = jax.nn.sigmoid(dot(second, gate_vector, ((1,), (0,))))
     grad_logit = reach * opening * (1.0 - opening)
-    grad_second = grad_second + grad_logit[:, None] * gate_vector.astype(f32)[None, :]
+    grad_second = grad_second.astype(f32) + grad_logit[:, None] * gate_vector.astype(f32)[None, :]
     grad_gate_vector = jnp.sum(grad_logit[:, None] * second.astype(f32), axis=0)
     grad_hidden = upstream + norm_back(hidden, scale_two, gain_two, grad_second)
     grad_gain_two = jnp.sum(grad_second * hidden * scale_two, axis=0)
@@ -995,7 +1023,7 @@
     rows = rows.reshape(fsdp, extra, 3 * group)
     grad_qkv = jnp.concatenate([grad_qkv, rows], axis=1)
 
-    grad_out = scatter(grad_out).astype(bf16)
+    grad_out = sum_fsdp(grad_out)
     grad_normed_all = grad_normed_all.astype(bf16)
     grad_e_up, grad_out, grad_qkv, grad_normed_all, out_all = together(
         grad_e_up, grad_out, grad_qkv, grad_normed_all, out_all

time: 1510 us -> 1400 us (0.927)
  waiting for transfers between devices: 250 us -> 174 us
  other arithmetic: 120 us -> 88.2 us
    all_to_all x5 -> x3, waiting for transfers between devices: 83.6 us -> 0.01 us  [swap(): return lax.all_to_all(value, 'fsdp', 0, 0, tiled=True)]
    pallas_call x1, Pallas kernels: 258 us -> 236 us  [feed_forward(): pl.pallas_call(feed_forward_kernel, out_shape=[jax.ShapeDtypeStruct((rows...]
    unnamed x169 -> x185, local copies, waits for them, and re-layouts: 53 us -> 55.2 us
  transfers between devices with their start and end apart: 26 -> 26, of which waited for: 13 -> 11; matrix products, arithmetic and copies ran while one was open for 22% -> 23% of each run, Pallas kernels for 35% -> 38%
where the time goes in v4:
time: 1400 us; the launch traced here: 1390 us
  Pallas kernels  769 us (55%)
  waiting for transfers between devices  174 us (12%)
  matrix products  164 us (12%)
  local copies, waits for them, and re-layouts  113 us (8%)
  other arithmetic  88.2 us (6%)
  starting transfers between devices  45.1 us (3%)
  blocking collectives  20.1 us (1%)
  between operations  17.1 us (1%)
    pallas_call x1, Pallas kernels, combine(): pl.pallas_call(functools.partial(combine_kernel, tuple(plan)), out_shape=...  503 us
    pallas_call x1, Pallas kernels, feed_forward(): pl.pallas_call(feed_forward_kernel, out_shape=[jax.ShapeDtypeStruct((rows...  236 us
    dot_general x13, matrix products, dot(): lax.dot_general(a, b, (contract, ((), ())), preferred_element_type=f32)  141 us
    unnamed x185, local copies, waits for them, and re-layouts  55.2 us
    ppermute x3, waiting for transfers between devices, gather_seq(): down = lax.ppermute(down, 'seq', [(i + 1, i) for i in range(seq - 1 - hop)])  46.7 us
    all_gather x1, waiting for transfers between devices, on_device(): lax.all_gather(after(second, fetched), 'fsdp', axis=0, tiled=True)  37.2 us
    pallas_call x1, Pallas kernels, middle(): pl.pallas_call(functools.partial(middle_kernel, joined), grid=(rows // ti...  29.3 us
  transfers between devices with their start and end apart: 26, of which 11 were waited for; matrix products, arithmetic and copies ran while one was open for 23% of the time, Pallas kernels for 38%

profile of v4, /device:TPU:0, one launch (start us, length us, event | category | flops | bytes accessed | tf_op | source)
XLA Modules:
  0.0 1390.9 jit_solution(1711331549206766551)
XLA Ops:
  11.0 9.9 all-reduce.4
  22.8 10.2 all_gather.33
  40.8 21.5 %collective-permute-done = bf16[256,2048]{1,0:T(8,128)(2,1)S(1)} collective-permute-done((bf16[256,2048]{1,0:T(8,128)(2,1)S(1)}, bf16[256,2048]{1,0:T(8,128)(2,1)S(1)}, u32[]{:S(2)}, u32[]{:S(2)}) %collective-permute-start) | collective-permute-done | bytes 1048608 | tf_op jit(solution)/shard_map/ppermute | solution.py:772
  82.0 23.2 %collective-permute-done.4 = bf16[256,2048]{1,0:T(8,128)(2,1)S(1)} collective-permute-done((bf16[256,2048]{1,0:T(8,128)(2,1)S(1)}, bf16[256,2048]{1,0:T(8,128)(2,1)S(1)}, u32[]{:S(2)}, u32[]{:S(2)}) %collective-permute-start.4) | collective-permute-done | bytes 1048608 | tf_op jit(solution)/shard_map/ppermute | solution.py:773
  108.4 23.6 %collective-permute-done.5 = bf16[256,2048]{1,0:T(8,128)(2,1)S(1)} collective-permute-done((bf16[256,2048]{1,0:T(8,128)(2,1)S(1)}, bf16[256,2048]{1,0:T(8,128)(2,1)S(1)}, u32[]{:S(2)}, u32[]{:S(2)}) %collective-permute-start.5) | collective-permute-done | bytes 1048608 | tf_op jit(solution)/shard_map/ppermute | solution.py:773
  136.1 5.9 slice.518
  148.7 8.5 convolution_add_fusion
  157.3 7.7 reshape.957
  164.9 6.7 copy.228
  190.8 13.1 collective-permute-start.8
  203.9 8.8 collective-permute-done.7
  213.1 23.4 %all-gather.10.cloned.1.call-done = bf16[2048,2048]{1,0:T(8,128)(2,1)} async-done(((bf16[256,2048]{1,0:T(8,128)(2,1)}), bf16[2048,2048]{1,0:T(8,128)(2,1)}) %all-gather.10.cloned.1.call-update) | async-done | bytes 8388624 | tf_op jit(solution)/shard_map/all_gather | solution.py:868
  262.3 37.2 %all-gather.12.cloned.1.call-done.x.refs_3_ = bf16[2048,2048]{1,0:T(8,128)(2,1)} async-done(((bf16[256,2048]{1,0:T(8,128)(2,1)}), bf16[2048,2048]{1,0:T(8,128)(2,1)}) %all-gather.12.cloned.1.call-update) | async-done | bytes 8388624 | tf_op jit(solution)/shard_map/all_gather | solution.py:899
  311.3 29.3 %shard_map.238 = (bf16[2048,704]{1,0:T(8,128)(2,1)}, bf16[2048,704]{1,0:T(8,128)(2,1)}, bf16[2048,704]{1,0:T(8,128)(2,1)}, f32[2048,1]{1,0:T(8,128)S(1)}) custom-call(bf16[2048,2048]{1,0:T(8,128)(2,1)} %all-gather.12.cloned.1.call-done.x.refs_3_, bf16[2048,2048]{1,0:T(8,128)(2,1)} %bitcast.351, bf16[2048,704]{1,0:T(8,128)(2,1)} %bitcast.302, ...), custom_call_target="tpu_custom_call" | custom-call | flops 17716740096 | bytes 34078720 | tf_op jit(solution)/shard_map/pallas_call | solution.py:736
  340.5 10.7 convolution_convert_fusion.6
  355.9 11.5 convolution_convert_fusion.5.refs_1_
  367.4 10.5 convolution_convert_fusion.4.refs_2_
  377.9 9.0 collective-permute-done.9
  386.9 236.5 %shard_map.239 = (bf16[2048,704]{1,0:T(8,128)(2,1)}, bf16[2048,704]{1,0:T(8,128)(2,1)}, bf16[2048,704]{1,0:T(8,128)(2,1)}, bf16[2048,1408]{1,0:T(8,128)(2,1)}, b...) custom-call(bf16[2048,704]{1,0:T(8,128)(2,1)} %bitcast.304, ...), custom_call_target="tpu_custom_call" | custom-call | flops 88583700480 | bytes 838860800 | tf_op jit(solution)/shard_map/pallas_call | solution.py:670
  625.5 19.3 %convolution_convert_fusion.3.refs_1_ = bf16[1408,2048]{1,0:T(8,128)(2,1)} fusion(bf16[2048,1408]{1,0:T(8,128)(2,1)} %get-tuple-element.153, bf16[1,2048,2048]{2,1,0:T(8,128)(2,1)} %all-gather.16.cloned.1.call-done), kind=kOutput, calls=%fused_computation.10 | convolution fusion | flops 11814043648 | bytes 19922944 | tf_op jit(solution)/shard_map/dot_general | solution.py:28
  648.8 31.6 %convolution_convert_fusion.refs_0_ = bf16[2048,2816]{1,0:T(8,128)(2,1)} fusion(bf16[2048,2048]{1,0:T(8,128)(2,1)} %all-gather.12.cloned.1.call-done.x.refs_3_, bf16[2048,2816]{1,0:T(8,128)(2,1)} %get-tuple-element.154), kind=kOutput, calls=%fused_computation | convolution fusion | flops 23628087296 | bytes 31457280 | tf_op jit(solution)/shard_map/dot_general | solution.py:28
  680.4 12.7 reduce-scatter.6.cloned.1.call-done
  715.8 6.8 collective-permute-done.10
  763.9 14.3 %fusion.127 = (bf16[1024,2048]{1,0:T(8,128)(2,1)}, bf16[2048]{0:T(1024)(128)(2,1)S(1)}) fusion(f32[1024]{0:T(1024)S(1)} %copy-done.66, bf16[1792,2048]{1,0:T(8,128)(2,1)} %copy-done.16, s32[]{:T(128)S(6)} %select_n.107, bf16[1024,1536]{0,1:T(8,128)(2,1)} %bitcast.305, bf16[2048,1536]{1,0:T(8,128)(2,1)} %bitcast.279), kind=kOutput, calls=%fused_computation.302 | convolution fusion | flops 6452934656 | bytes 17833988 | tf_op jit(solution)/shard_map/dot_general | solution.py:28
  778.3 11.1 convolution_convert_fusion.1
  789.4 6.2 pad_maximum_fusion
  797.6 503.4 %combine_1.1 = (bf16[2048,2816]{1,0:T(8,128)(2,1)}, bf16[1408,2048]{1,0:T(8,128)(2,1)}, bf16[256,2048]{1,0:T(8,128)(2,1)S(1)}, bf16[2048,2816]{1,0:T(8,128)(2,1)...) custom-call(bf16[2048,2816]{1,0:T(8,128)(2,1)} %convolution_convert_fusion.refs_0_, ...), custom_call_target="tpu_custom_call" | custom-call | flops 18350080 | bytes 1835008000 | tf_op jit(solution)/shard_map/combine_1/pallas_call | solution.py:364
  1306.2 6.6 copy.277
  1312.8 8.6 maximum_convert_fusion.1
  1321.4 12.2 copy.276
  1335.2 8.7 convert.61
  1343.9 13.0 convert.60
  (380 shorter events, 212.1 us)
Async XLA Ops:
  7.2 128.9 %all-gather.14.cloned.1.call-start = ((), (), s32[]{:S(2)}) async-start(), calls=%async_computation.15 | async-start | bytes 7520256 | tf_op jit(solution)/shard_map/all_gather | solution.py:856
  35.1 178.0 %all-gather.16.cloned.1.call-start = ((), (), s32[]{:S(2)}) async-start(), calls=%async_computation.16 | async-start | bytes 9437184 | tf_op jit(solution)/shard_map/all_gather | solution.py:869
  35.9 26.4 %collective-permute-start = (bf16[256,2048]{1,0:T(8,128)(2,1)S(1)}, bf16[256,2048]{1,0:T(8,128)(2,1)S(1)}, u32[]{:S(2)}, u32[]{:S(2)}) collective-permute-start(bf16[256,2048]{1,0:T(8,128)(2,1)S(1)} %bitcast.274), channel_id=1, source_target_pairs={{0,8},{8,16},{16,24},{1,9},{9,17},{17,25},{2,10},{10,18},{18,26},{... | collective-permute-start | bytes 3145736 | tf_op jit(solution)/shard_map/ppermute | solution.py:772
  39.5 36.0 %collective-permute-start.3 = (bf16[256,2048]{1,0:T(8,128)(2,1)S(1)}, bf16[256,2048]{1,0:T(8,128)(2,1)S(1)}, u32[]{:S(2)}, u32[]{:S(2)}) collective-permute-start(bf16[256,2048]{1,0:T(8,128)(2,1)S(1)} %bitcast.275), channel_id=1, source_target_pairs={{8,0},{16,8},{24,16},{9,1},{17,9},{25,17},{10,2},{18,10},{26,18},{... | collective-permute-start | bytes 3145736 | tf_op jit(solution)/shard_map/ppermute | solution.py:773
  62.3 14.6 %collective-permute-start.1 = (bf16[256,2048]{1,0:T(8,128)(2,1)S(1)}, bf16[256,2048]{1,0:T(8,128)(2,1)}, u32[]{:S(2)}, u32[]{:S(2)}) collective-permute-start(bf16[256,2048]{1,0:T(8,128)(2,1)S(1)} %collective-permute-done), channel_id=1, source_target_pairs={{8,16},{16,24},{9,17},{17,25},{10,18},{18,26},{11,19},{19,27},{12,... | collective-permute-start | bytes 3145736 | tf_op jit(solution)/shard_map/ppermute | solution.py:772
  69.5 175.4 %all-to-all-start = ((bf16[8,128,2816]{2,1,0:T(8,128)(2,1)}), bf16[8,128,2816]{2,1,0:T(8,128)(2,1)}, u32[]{:S(2)}, u32[]{:S(2)}) async-start(bf16[8,128,2816]{2,1,0:T(8,128)(2,1)} %constant_dynamic-slice_fusion.5), calls=%async_computation | async-start | bytes 11534336 | tf_op jit(solution)/shard_map/all_to_all | solution.py:799
  74.3 162.2 %all-gather.10.cloned.1.call-start = ((), (), s32[]{:S(2)}) async-start(), calls=%async_computation.8 | async-start | bytes 9437184 | tf_op jit(solution)/shard_map/all_gather | solution.py:868
  75.0 224.4 %all-gather.12.cloned.1.call-start = ((), (), s32[]{:S(2)}) async-start(), calls=%async_computation.9 | async-start | bytes 9437184 | tf_op jit(solution)/shard_map/all_gather | solution.py:899
  75.4 29.7 %collective-permute-start.4 = (bf16[256,2048]{1,0:T(8,128)(2,1)S(1)}, bf16[256,2048]{1,0:T(8,128)(2,1)S(1)}, u32[]{:S(2)}, u32[]{:S(2)}) collective-permute-start(bf16[256,2048]{1,0:T(8,128)(2,1)S(1)} %collective-permute-done.3), channel_id=1, source_target_pairs={{8,0},{16,8},{9,1},{17,9},{10,2},{18,10},{11,3},{19,11},{12,4},{20... | collective-permute-start | bytes 3145736 | tf_op jit(solution)/shard_map/ppermute | solution.py:773
  76.9 29.6 %collective-permute-start.2 = (bf16[256,2048]{1,0:T(8,128)(2,1)}, bf16[256,2048]{1,0:T(8,128)(2,1)S(1)}, u32[]{:S(2)}, u32[]{:S(2)}) collective-permute-start(bf16[256,2048]{1,0:T(8,128)(2,1)} %collective-permute-done.1), channel_id=1, source_target_pairs={{16,24},{17,25},{18,26},{19,27},{20,28},{21,29},{22,30},{23,31}} | collective-permute-start | bytes 3145736 | tf_op jit(solution)/shard_map/ppermute | solution.py:772
  79.8 96.0 %copy-start.21 = (f32[1024,128]{1,0:T(8,128)}, f32[1024,128]{1,0:T(8,128)S(1)}, u32[]{:S(2)}) copy-start(f32[1024,128]{1,0:T(8,128)S(1)} %get-tuple-element.280) | copy-start | bytes 1572868
  79.9 96.0 %copy-start.24 = (f32[1024,128]{1,0:T(8,128)}, f32[1024,128]{1,0:T(8,128)S(1)}, u32[]{:S(2)}) copy-start(f32[1024,128]{1,0:T(8,128)S(1)} %get-tuple-element.281) | copy-start | bytes 1572868
  105.2 26.8 %collective-permute-start.5 = (bf16[256,2048]{1,0:T(8,128)(2,1)S(1)}, bf16[256,2048]{1,0:T(8,128)(2,1)S(1)}, u32[]{:S(2)}, u32[]{:S(2)}) collective-permute-start(bf16[256,2048]{1,0:T(8,128)(2,1)S(1)} %collective-permute-done.4), channel_id=1, source_target_pairs={{8,0},{9,1},{10,2},{11,3},{12,4},{13,5},{14,6},{15,7}} | collective-permute-start | bytes 3145736 | tf_op jit(solution)/shard_map/ppermute | solution.py:773
  189.3 14.6 %collective-permute-start.6 = (bf16[256,512]{0,1:T(8,128)(2,1)}, bf16[256,512]{0,1:T(8,128)(2,1)S(1)}, u32[]{:S(2)}, u32[]{:S(2)}) collective-permute-start(bf16[256,512]{0,1:T(8,128)(2,1)} %get-tuple-element.275), channel_id=1, source_target_pairs={{0,24},{8,0},{16,8},{24,16},{1,25},{9,1},{17,9},{25,17},{2,26},{10... | collective-permute-start | bytes 786440 | tf_op jit(solution)/shard_map/ppermute | solution.py:792
  189.3 23.5 %collective-permute-start.7 = (bf16[256,512]{0,1:T(8,128)(2,1)S(1)}, bf16[256,512]{0,1:T(8,128)(2,1)S(1)}, u32[]{:S(2)}, u32[]{:S(2)}) collective-permute-start(bf16[256,512]{0,1:T(8,128)(2,1)S(1)} %get-tuple-element.274), channel_id=1, source_target_pairs={{0,16},{8,24},{16,0},{24,8},{1,17},{9,25},{17,1},{25,9},{2,18},{10... | collective-permute-start | bytes 786440 | tf_op jit(solution)/shard_map/ppermute | solution.py:792
  190.8 22.1 %collective-permute-start.8 = (bf16[256,512]{0,1:T(8,128)(2,1)S(1)}, bf16[256,512]{0,1:T(8,128)(2,1)S(1)}, u32[]{:S(2)}, u32[]{:S(2)}) collective-permute-start(bf16[256,512]{0,1:T(8,128)(2,1)S(1)} %get-tuple-element.273), channel_id=1, source_target_pairs={{0,8},{8,16},{16,24},{24,0},{1,9},{9,17},{17,25},{25,1},{2,10},{10... | collective-permute-start | bytes 786440 | tf_op jit(solution)/shard_map/ppermute | solution.py:792
  260.2 126.8 %collective-permute-start.9 = (bf16[8,128,2816]{2,1,0:T(8,128)(2,1)}, bf16[8,128,2816]{2,1,0:T(8,128)(2,1)}, u32[]{:S(2)}, u32[]{:S(2)}) collective-permute-start(bf16[8,128,2816]{2,1,0:T(8,128)(2,1)} %all-to-all-done), channel_id=1, source_target_pairs={{0,8},{8,0},{16,24},{24,16},{1,9},{9,1},{17,25},{25,17},{2,10},{10... | collective-permute-start | bytes 17301512 | tf_op jit(solution)/shard_map/ppermute | solution.py:877
  305.2 81.8 %all-to-all-start.1 = ((bf16[8,176,2048]{2,1,0:T(8,128)(2,1)}), bf16[8,176,2048]{2,1,0:T(8,128)(2,1)}, u32[]{:S(2)}, u32[]{:S(2)}) async-start(bf16[8,176,2048]{2,1,0:T(8,128)(2,1)} %param.44), calls=%async_computation.1 | async-start | bytes 11534336 | tf_op jit(solution)/shard_map/all_to_all | solution.py:799
  309.9 383.3 %reduce-scatter.6.cloned.1.call-start = ((), (), s32[]{:S(2)}) async-start(), calls=%async_computation.10 | async-start | bytes 9437184 | tf_op jit(solution)/shard_map/reduce_scatter | solution.py:803
  645.3 35.0 %all-to-all-start.2 = ((f32[8,1,256]{2,1,0:T(1,128)}), f32[8,1,256]{2,1,0:T(1,128)S(1)}, u32[]{:S(2)}, u32[]{:S(2)}) async-start(f32[8,1,256]{2,1,0:T(1,128)} %copy.239), calls=%async_computation.3 | async-start | bytes 16384 | tf_op jit(solution)/shard_map/all_to_all | solution.py:799
  648.7 44.5 %copy-start.2 = (f32[256,2048]{1,0:T(8,128)S(1)}, f32[256,2048]{1,0:T(8,128)}, u32[]{:S(2)}) copy-start(f32[256,2048]{1,0:T(8,128)} %copy-done.1) | copy-start | bytes 6291460
  648.7 44.5 %copy-start.42 = (f32[1,2,8,128]{3,1,2,0:T(2,128)S(1)}, f32[1,2,8,128]{3,1,2,0:T(2,128)}, u32[]{:S(2)}) copy-start(f32[1,2,8,128]{3,1,2,0:T(2,128)} %copy-done.41) | copy-start | bytes 24580
  648.7 44.5 %copy-start.44 = (f32[2048]{0:T(1024)S(1)}, f32[2048]{0:T(1024)}, u32[]{:S(2)}) copy-start(f32[2048]{0:T(1024)} %convert_element_type.330) | copy-start | bytes 24580
  648.7 44.5 %copy-start.48 = (f32[256]{0:T(256)S(1)}, f32[256]{0:T(256)}, u32[]{:S(2)}) copy-start(f32[256]{0:T(256)} %copy-done.47) | copy-start | bytes 3076
  648.7 146.9 %reduce-scatter.8.cloned.1.call-start = ((), (), s32[]{:S(2)}) async-start(), calls=%async_computation.11 | async-start | bytes 9437184 | tf_op jit(solution)/shard_map/reduce_scatter | solution.py:803
  704.2 21.3 %collective-permute-start.12 = (bf16[256,512]{1,0:T(8,128)(2,1)S(1)}, bf16[256,512]{1,0:T(8,128)(2,1)S(1)}, u32[]{:S(2)}, u32[]{:S(2)}) collective-permute-start(bf16[256,512]{1,0:T(8,128)(2,1)S(1)} %get-tuple-element.270), channel_id=1, source_target_pairs={{0,8},{8,16},{16,24},{24,0},{1,9},{9,17},{17,25},{25,1},{2,10},{10... | collective-permute-start | bytes 786440 | tf_op jit(solution)/shard_map/ppermute | solution.py:792
  705.7 19.7 %collective-permute-start.11 = (bf16[256,512]{1,0:T(8,128)(2,1)S(1)}, bf16[256,512]{1,0:T(8,128)(2,1)S(1)}, u32[]{:S(2)}, u32[]{:S(2)}) collective-permute-start(bf16[256,512]{1,0:T(8,128)(2,1)S(1)} %get-tuple-element.271), channel_id=1, source_target_pairs={{0,16},{8,24},{16,0},{24,8},{1,17},{9,25},{17,1},{25,9},{2,18},{10... | collective-permute-start | bytes 786440 | tf_op jit(solution)/shard_map/ppermute | solution.py:792
  708.1 14.5 %collective-permute-start.10 = (bf16[256,512]{1,0:T(8,128)(2,1)S(1)}, bf16[256,512]{1,0:T(8,128)(2,1)S(1)}, u32[]{:S(2)}, u32[]{:S(2)}) collective-permute-start(bf16[256,512]{1,0:T(8,128)(2,1)S(1)} %get-tuple-element.272), channel_id=1, source_target_pairs={{0,24},{8,0},{16,8},{24,16},{1,25},{9,1},{17,9},{25,17},{2,26},{10... | collective-permute-start | bytes 786440 | tf_op jit(solution)/shard_map/ppermute | solution.py:792
  715.8 585.3 %reduce-scatter.14.cloned.1.call-start = ((), (), s32[]{:S(2)}) async-start(), calls=%async_computation.14 | async-start | bytes 7520256 | tf_op jit(solution)/shard_map/reduce_scatter | solution.py:1031
  795.7 561.2 %reduce-scatter.12.cloned.1.call-start = ((), (), s32[]{:S(2)}) async-start(), calls=%async_computation.13 | async-start | bytes 5242880 | tf_op jit(solution)/shard_map/reduce_scatter | solution.py:1034
  796.4 565.6 %reduce-scatter.10.cloned.1.call-start = ((), (), s32[]{:S(2)}) async-start(), calls=%async_computation.12 | async-start | bytes 9437184 | tf_op jit(solution)/shard_map/reduce_scatter | solution.py:1035
  797.2 569.0 %all-gather.18.cloned.1.call-start = ((), (), s32[]{:S(2)}) async-start(), calls=%async_computation.17 | async-start | bytes 4177920 | tf_op jit(solution)/shard_map/all_gather | solution.py:1051
  (65 other events, 393.3 us)
Sparse Core Ops, SparseCore 0:
  35.2 46.9 all-gather.13
  84.1 95.9 all-gather.15
  182.1 54.3 all-gather.9
  245.1 54.3 all-gather.11
  623.6 69.4 reduce-scatter.5
  715.9 68.5 reduce-scatter.7
  795.8 94.2 reduce-scatter.13
  892.4 142.1 reduce-scatter.11
  1038.4 75.9 reduce-scatter.9
  1301.3 64.8 all-gather.17

commit v5 on v4

--- a/solution.py
+++ b/solution.py
@@ -704,12 +704,15 @@
     )(*sums, *tiles, *weights, share)
 
 
-def middle_kernel(joined, x, u, w_gate, w_lift, w_down, scale, inner, *outs):
+def middle_kernel(joined, ahead, x, u, w_gate, w_lift, w_down, scale, inner, *outs):
     gate = jnp.dot(x[...], w_gate[...], preferred_element_type=f32)
     lift = jnp.dot(x[...], w_lift[...], preferred_element_type=f32)
-    raw = lax.dot_general(
-        u[...], w_down[...], (((1,), (1,)), ((), ())), preferred_element_type=f32
-    )
+    if ahead:
+        raw = u[...]
+    else:
+        raw = lax.dot_general(
+            u[...], w_down[...], (((1,), (1,)), ((), ())), preferred_element_type=f32
+        )
     sigma = 1.0 / (1.0 + jnp.exp(-gate))
     silu = gate * sigma
     product = silu * lift
@@ -730,18 +733,19 @@
 def middle(x, u, w_gate, w_lift, w_down, scale):
     joined = w_lift is None
     rows, hidden = x.shape[0], w_down.shape[0]
+    ahead = u.shape[1] == hidden
     tile = 256
     whole = dict(pipeline_mode=pl.Buffered(1))
     grads = [hidden * 2] if joined else [hidden, hidden]
     return pl.pallas_call(
-        functools.partial(middle_kernel, joined),
+        functools.partial(middle_kernel, joined, ahead),
         grid=(rows // tile,),
         in_specs=[
             pl.BlockSpec((tile, D), lambda i: (i, 0)),
-            pl.BlockSpec((tile, D), lambda i: (i, 0)),
+            pl.BlockSpec((tile, u.shape[1]), lambda i: (i, 0)),
             pl.BlockSpec((D, hidden), lambda i: (0, 0), **whole),
             pl.BlockSpec((D, hidden), lambda i: (0, 1 if joined else 0), **whole),
-            pl.BlockSpec((hidden, D), lambda i: (0, 0), **whole),
+            pl.BlockSpec((16 if ahead else hidden, D), lambda i: (0, 0), **whole),
             pl.BlockSpec((tile, 1), lambda i: (i, 0)),
         ],
         out_specs=[pl.BlockSpec((tile, w), lambda i: (i, 0)) for w in [hidden] + grads + [1]],
@@ -842,29 +846,26 @@
     offsets = jnp.sum(jnp.where(before, tallies, 0), axis=0)
     earlier = offsets[:, None] + jnp.cumsum(chosen, axis=1) - chosen
     gates = jnp.where((chosen > 0) & (earlier < capacity), gates, 0.0)
-    gates = lax.all_gather(gates, "fsdp", axis=0)
+    vectors = jnp.concatenate([attn_gain, ffn_gain, shared_gate, qkv_bias]).astype(f32)
+    small = lax.all_gather(jnp.concatenate([gates.reshape(-1), vectors]), "fsdp", axis=0)
+    gates = small[:, : EXPERTS * row_count].reshape(fsdp, EXPERTS, row_count)
     share = lax.dynamic_index_in_dim(gates, me // copies, 1, keepdims=False).reshape(-1, 1)
+    vectors = small[:, EXPERTS * row_count :]
+    gain_one = vectors[:, :width].reshape(D)
+    gain_two = vectors[:, width : 2 * width].reshape(D)
+    gate_vector = vectors[:, 2 * width : 3 * width].reshape(D).astype(bf16)
+    bias = vectors[:, 3 * width : 6 * width].reshape(3, seq, group)
+    bias = lax.dynamic_index_in_dim(bias, place, 1, keepdims=False).reshape(-1)
 
     all_tokens = gather_seq(tokens[0])
     own = [
         lax.dynamic_slice_in_dim(qkv_weight, part * D + place * group, group, 1)
         for part in range(3)
     ]
-    vectors = jnp.concatenate([attn_gain, ffn_gain, shared_gate, qkv_bias])
     extra = -(-6 * width // (3 * group) // 16) * 16
-    vectors = jnp.pad(vectors, (0, extra * 3 * group - 6 * width)).reshape(extra, 3 * group)
-    gathered = lax.all_gather(
-        after(jnp.concatenate([jnp.concatenate(own, axis=1), vectors], axis=0), gates),
-        "fsdp",
-        axis=0,
-    )
-    weight_qkv = gathered[:, :width].reshape(D, 3 * group)
-    vectors = gathered[:, width:].reshape(fsdp, -1)
-    gain_one = vectors[:, :width].reshape(D).astype(f32)
-    gain_two = vectors[:, width : 2 * width].reshape(D).astype(f32)
-    gate_vector = vectors[:, 2 * width : 3 * width].reshape(D)
-    bias = vectors[:, 3 * width : 6 * width].reshape(3, seq, group)
-    bias = lax.dynamic_index_in_dim(bias, place, 1, keepdims=False).reshape(-1).astype(f32)
+    weight_qkv = lax.all_gather(
+        after(jnp.concatenate(own, axis=1), small), "fsdp", axis=0, tiled=True
+    )
     weight_out = lax.all_gather(out_weight, "fsdp", axis=0, tiled=True)
     upstream_all = lax.all_gather(cotangent[0], "fsdp", axis=0, tiled=True)
 
@@ -891,19 +892,19 @@
     documents = segments[0]
     mixed, logs = attend(queries, keys, values, documents, factor)
     mixed_rows = exchange_seq(mixed.reshape(length, group), 0, 1)
-    mixed_rows = after(mixed_rows, upstream_all)
     inputs = tokens[0].astype(f32)
     hidden = inputs + dot(mixed_rows, weight_out, ((1,), (0,)))
     scale_two = rms_scale(hidden)
     second = (hidden * scale_two * gain_two).astype(bf16)
-    second_all = lax.all_gather(after(second, fetched), "fsdp", axis=0, tiled=True)
+    second_all = lax.all_gather(after(second, fetched, upstream_all), "fsdp", axis=0, tiled=True)
 
     weight_down = swap(after(down_sent, second_all)).reshape(hidden_own, D)
     by_kernel = seq == 4 and fsdp == 8
     s_gate, s_lift = shared_gate_up[:, 0], shared_gate_up[:, 1]
     opening_all = jax.nn.sigmoid(dot(second_all, gate_vector, ((1,), (0,))))[:, None]
+    raw_s = dot(after(upstream_all, second), shared_down, ((1,), (1,)))
     inner_s, ga_s, gl_s, reach = middle(
-        second_all, upstream_all, s_gate, s_lift, shared_down, opening_all
+        second_all, raw_s, s_gate, s_lift, shared_down, opening_all
     )
     grad_s_down = dot(upstream_all, inner_s, ((0,), (0,)), bf16)
     grad_s_gate = dot(second_all, ga_s, ((0,), (0,)), bf16)

time: 1400 us -> 1390 us (level)
  matrix products: 164 us -> 181 us
    all_gather x1, waiting for transfers between devices: 0.02 us -> 26.4 us  [on_device(): upstream_all = lax.all_gather(cotangent[0], 'fsdp', axis=0, tiled=True)]
    all_gather x1, waiting for transfers between devices: 23.4 us -> 0.01 us  [on_device(): weight_out = lax.all_gather(out_weight, 'fsdp', axis=0, tiled=True)]
    dot_general x13 -> x14, matrix products: 141 us -> 158 us  [dot(): lax.dot_general(a, b, (contract, ((), ())), preferred_element_type=f32)]
    unnamed x185 -> x183, local copies, waits for them, and re-layouts: 55.2 us -> 60.2 us
  transfers between devices with their start and end apart: 26 -> 26, of which waited for: 11 -> 13; matrix products, arithmetic and copies ran while one was open for 23% -> 24% of each run, Pallas kernels for 38% -> 38%
where the time goes in v5:
time: 1390 us; the launch traced here: 1380 us
  Pallas kernels  763 us (55%)
  matrix products  181 us (13%)
  waiting for transfers between devices  165 us (12%)
  local copies, waits for them, and re-layouts  111 us (8%)
  other arithmetic  87.7 us (6%)
  starting transfers between devices  34.7 us (2%)
  blocking collectives  19.1 us (1%)
  between operations  17 us (1%)
    pallas_call x1, Pallas kernels, combine(): pl.pallas_call(functools.partial(combine_kernel, tuple(plan)), out_shape=...  504 us
    pallas_call x1, Pallas kernels, feed_forward(): pl.pallas_call(feed_forward_kernel, out_shape=[jax.ShapeDtypeStruct((rows...  237 us
    dot_general x14, matrix products, dot(): lax.dot_general(a, b, (contract, ((), ())), preferred_element_type=f32)  158 us
    unnamed x183, local copies, waits for them, and re-layouts  60.2 us
    ppermute x3, waiting for transfers between devices, gather_seq(): down = lax.ppermute(down, 'seq', [(i + 1, i) for i in range(seq - 1 - hop)])  42.8 us
    all_gather x1, waiting for transfers between devices, on_device(): lax.all_gather(after(second, fetched, upstream_all), 'fsdp', axis=0, tile...  28.5 us
  transfers between devices with their start and end apart: 26, of which 13 were waited for; matrix products, arithmetic and copies ran while one was open for 24% of the time, Pallas kernels for 38%

profile of v5, /device:TPU:0, one launch (start us, length us, event | category | flops | bytes accessed | tf_op | source)
XLA Modules:
  0.0 1378.8 jit_solution(14958368122842275511)
XLA Ops:
  11.6 9.9 all-reduce.3
  22.9 9.2 all-gather.4
  52.3 9.2 collective-permute-done
  72.2 22.4 %collective-permute-done.4 = bf16[256,2048]{1,0:T(8,128)(2,1)} collective-permute-done((bf16[256,2048]{1,0:T(8,128)(2,1)S(1)}, bf16[256,2048]{1,0:T(8,128)(2,1)}, u32[]{:S(2)}, u32[]{:S(2)}) %collective-permute-start.4) | collective-permute-done | bytes 1048608 | tf_op jit(solution)/shard_map/ppermute | solution.py:777
  101.4 19.4 %collective-permute-done.5 = bf16[256,2048]{1,0:T(8,128)(2,1)S(1)} collective-permute-done((bf16[256,2048]{1,0:T(8,128)(2,1)}, bf16[256,2048]{1,0:T(8,128)(2,1)S(1)}, u32[]{:S(2)}, u32[]{:S(2)}) %collective-permute-start.5) | collective-permute-done | bytes 1048608 | tf_op jit(solution)/shard_map/ppermute | solution.py:777
  126.9 12.3 convolution_add_fusion
  139.2 7.6 reshape.857
  146.8 6.9 copy.236
  180.0 13.5 collective-permute-done.7
  197.8 6.2 multiply_reduce_fusion.6
  206.5 26.4 %all-gather.17.cloned.1.call-done = bf16[1,2048,2048]{2,1,0:T(8,128)(2,1)} async-done(((bf16[1,256,2048]{2,1,0:T(8,128)(2,1)}), bf16[1,2048,2048]{2,1,0:T(8,128)(2,1)}) %all-gather.17.cloned.1.call-update) | async-done | bytes 8388624 | tf_op jit(solution)/shard_map/all_gather | solution.py:870
  249.4 11.7 fusion.138.u
  261.1 28.5 %all-gather.15.cloned.1.call-done.x.refs_3_ = bf16[2048,2048]{1,0:T(8,128)(2,1)} async-done(((bf16[256,2048]{1,0:T(8,128)(2,1)}), bf16[2048,2048]{1,0:T(8,128)(2,1)}) %all-gather.15.cloned.1.call-update) | async-done | bytes 8388624 | tf_op jit(solution)/shard_map/all_gather | solution.py:899
  301.6 21.7 %shard_map.238 = (bf16[2048,704]{1,0:T(8,128)(2,1)}, bf16[2048,704]{1,0:T(8,128)(2,1)}, bf16[2048,704]{1,0:T(8,128)(2,1)}, f32[2048,1]{1,0:T(8,128)S(1)}) custom-call(bf16[2048,2048]{1,0:T(8,128)(2,1)} %all-gather.15.cloned.1.call-done.x.refs_3_, f32[2048,704]{1,0:T(8,128)} %fusion.138.u, bf16[2048,704]{1,0:T(8,128)(2,1)} %bitcast.295, ...), custom_call_target="tpu_custom_call" | custom-call | flops 17716740096 | bytes 34078720 | tf_op jit(solution)/shard_map/pallas_call | solution.py:740
  323.3 10.7 convolution_convert_fusion.6
  338.6 11.6 convolution_convert_fusion.5.refs_1_
  350.1 10.5 convolution_convert_fusion.4.refs_2_
  360.6 14.1 %collective-permute-done.9 = bf16[8,128,2816]{2,1,0:T(8,128)(2,1)} collective-permute-done((bf16[8,128,2816]{2,1,0:T(8,128)(2,1)}, bf16[8,128,2816]{2,1,0:T(8,128)(2,1)}, u32[]{:S(2)}, u32[]{:S(2)}) %collective-permute-start.9) | collective-permute-done | bytes 5767200 | tf_op jit(solution)/shard_map/ppermute | solution.py:878
  374.7 236.9 %shard_map.239 = (bf16[2048,704]{1,0:T(8,128)(2,1)}, bf16[2048,704]{1,0:T(8,128)(2,1)}, bf16[2048,704]{1,0:T(8,128)(2,1)}, bf16[2048,1408]{1,0:T(8,128)(2,1)}, b...) custom-call(bf16[2048,704]{1,0:T(8,128)(2,1)} %bitcast.297, ...), custom_call_target="tpu_custom_call" | custom-call | flops 88583700480 | bytes 838860800 | tf_op jit(solution)/shard_map/pallas_call | solution.py:670
  613.6 19.6 %convolution_convert_fusion.3.refs_1_ = bf16[1408,2048]{1,0:T(8,128)(2,1)} fusion(bf16[2048,1408]{1,0:T(8,128)(2,1)} %get-tuple-element.153, bf16[1,2048,2048]{2,1,0:T(8,128)(2,1)} %all-gather.17.cloned.1.call-done), kind=kOutput, calls=%fused_computation.10 | convolution fusion | flops 11814043648 | bytes 19922944 | tf_op jit(solution)/shard_map/dot_general | solution.py:28
  637.3 31.8 %convolution_convert_fusion.refs_0_ = bf16[2048,2816]{1,0:T(8,128)(2,1)} fusion(bf16[2048,2048]{1,0:T(8,128)(2,1)} %all-gather.15.cloned.1.call-done.x.refs_3_, bf16[2048,2816]{1,0:T(8,128)(2,1)} %get-tuple-element.154), kind=kOutput, calls=%fused_computation | convolution fusion | flops 23628087296 | bytes 31457280 | tf_op jit(solution)/shard_map/dot_general | solution.py:28
  669.1 11.8 reduce-scatter.6.cloned.1.call-done
  697.7 7.0 convolution_convert_fusion.2
  751.1 14.2 %fusion.127 = (bf16[1024,2048]{1,0:T(8,128)(2,1)}, bf16[2048]{0:T(1024)(128)(2,1)S(1)}) fusion(f32[1024]{0:T(1024)S(1)} %copy-done.60, bf16[1792,2048]{1,0:T(8,128)(2,1)} %copy-done.14, s32[]{:T(128)S(6)} %select_n.95, bf16[1024,1536]{0,1:T(8,128)(2,1)} %bitcast.298, bf16[2048,1536]{1,0:T(8,128)(2,1)} %all-gather.11.cloned.1.call-done), kind=kOutput, calls=%fused_computation.301 | convolution fusion | flops 6452934656 | bytes 17833988 | tf_op jit(solution)/shard_map/dot_general | solution.py:28
  765.4 11.0 convolution_convert_fusion.1
  776.5 6.2 pad_maximum_fusion
  784.7 504.4 %combine_1.1 = (bf16[2048,2816]{1,0:T(8,128)(2,1)}, bf16[1408,2048]{1,0:T(8,128)(2,1)}, bf16[256,2048]{1,0:T(8,128)(2,1)S(1)}, bf16[2048,2816]{1,0:T(8,128)(2,1)...) custom-call(bf16[2048,2816]{1,0:T(8,128)(2,1)} %convolution_convert_fusion.refs_0_, ...), custom_call_target="tpu_custom_call" | custom-call | flops 18350080 | bytes 1835008000 | tf_op jit(solution)/shard_map/combine_1/pallas_call | solution.py:364
  1294.3 6.6 copy.286
  1300.8 8.6 maximum_convert_fusion.1
  1309.4 12.2 copy.285
  1323.2 8.7 convert.62
  1332.0 13.0 convert.61
  (378 shorter events, 218.2 us)
Async XLA Ops:
  7.2 119.7 %all-gather.11.cloned.1.call-start = ((), (), s32[]{:S(2)}) async-start(), calls=%async_computation.8 | async-start | bytes 7077888 | tf_op jit(solution)/shard_map/all_gather | solution.py:866
  34.3 163.5 %all-gather.13.cloned.1.call-start = ((), (), s32[]{:S(2)}) async-start(), calls=%async_computation.9 | async-start | bytes 9437184 | tf_op jit(solution)/shard_map/all_gather | solution.py:869
  35.0 26.4 %collective-permute-start = (bf16[256,2048]{1,0:T(8,128)(2,1)S(1)}, bf16[256,2048]{1,0:T(8,128)(2,1)}, u32[]{:S(2)}, u32[]{:S(2)}) collective-permute-start(bf16[256,2048]{1,0:T(8,128)(2,1)S(1)} %bitcast.271), channel_id=1, source_target_pairs={{0,8},{8,16},{16,24},{1,9},{9,17},{17,25},{2,10},{10,18},{18,26},{... | collective-permute-start | bytes 3145736 | tf_op jit(solution)/shard_map/ppermute | solution.py:776
  39.5 27.0 %collective-permute-start.3 = (bf16[256,2048]{1,0:T(8,128)(2,1)S(1)}, bf16[256,2048]{1,0:T(8,128)(2,1)S(1)}, u32[]{:S(2)}, u32[]{:S(2)}) collective-permute-start(bf16[256,2048]{1,0:T(8,128)(2,1)S(1)} %bitcast.272), channel_id=1, source_target_pairs={{8,0},{16,8},{24,16},{9,1},{17,9},{25,17},{10,2},{18,10},{26,18},{... | collective-permute-start | bytes 3145736 | tf_op jit(solution)/shard_map/ppermute | solution.py:777
  46.6 159.9 %all-to-all-start = ((bf16[8,128,2816]{2,1,0:T(8,128)(2,1)}), bf16[8,128,2816]{2,1,0:T(8,128)(2,1)}, u32[]{:S(2)}, u32[]{:S(2)}) async-start(bf16[8,128,2816]{2,1,0:T(8,128)(2,1)} %constant_dynamic-slice_fusion.4), calls=%async_computation | async-start | bytes 11534336 | tf_op jit(solution)/shard_map/all_to_all | solution.py:803
  51.5 181.4 %all-gather.17.cloned.1.call-start = ((), (), s32[]{:S(2)}) async-start(), calls=%async_computation.16 | async-start | bytes 9437184 | tf_op jit(solution)/shard_map/all_gather | solution.py:870
  52.2 237.4 %all-gather.15.cloned.1.call-start = ((), (), s32[]{:S(2)}) async-start(), calls=%async_computation.10 | async-start | bytes 9437184 | tf_op jit(solution)/shard_map/all_gather | solution.py:899
  61.4 6.4 collective-permute-start.1
  65.5 92.4 %copy-start.19 = (f32[1024,128]{1,0:T(8,128)}, f32[1024,128]{1,0:T(8,128)S(1)}, u32[]{:S(2)}) copy-start(f32[1024,128]{1,0:T(8,128)S(1)} %get-tuple-element.280) | copy-start | bytes 1572868
  65.5 92.4 %copy-start.21 = (f32[1024,128]{1,0:T(8,128)}, f32[1024,128]{1,0:T(8,128)S(1)}, u32[]{:S(2)}) copy-start(f32[1024,128]{1,0:T(8,128)S(1)} %get-tuple-element.281) | copy-start | bytes 1572868
  66.5 28.1 %collective-permute-start.4 = (bf16[256,2048]{1,0:T(8,128)(2,1)S(1)}, bf16[256,2048]{1,0:T(8,128)(2,1)}, u32[]{:S(2)}, u32[]{:S(2)}) collective-permute-start(bf16[256,2048]{1,0:T(8,128)(2,1)S(1)} %collective-permute-done.3), channel_id=1, source_target_pairs={{8,0},{16,8},{9,1},{17,9},{10,2},{18,10},{11,3},{19,11},{12,4},{20... | collective-permute-start | bytes 3145736 | tf_op jit(solution)/shard_map/ppermute | solution.py:777
  67.8 28.1 %collective-permute-start.2 = (bf16[256,2048]{1,0:T(8,128)(2,1)}, bf16[256,2048]{1,0:T(8,128)(2,1)}, u32[]{:S(2)}, u32[]{:S(2)}) collective-permute-start(bf16[256,2048]{1,0:T(8,128)(2,1)} %collective-permute-done.1), channel_id=1, source_target_pairs={{16,24},{17,25},{18,26},{19,27},{20,28},{21,29},{22,30},{23,31}} | collective-permute-start | bytes 3145736 | tf_op jit(solution)/shard_map/ppermute | solution.py:776
  69.5 52.3 %copy-start.34 = (f32[1,2,8,128]{3,1,2,0:T(2,128)}, f32[1,2,8,128]{3,1,2,0:T(2,128)S(1)}, u32[]{:S(2)}) copy-start(f32[1,2,8,128]{3,1,2,0:T(2,128)S(1)} %copy.329) | copy-start | bytes 24580
  94.6 26.1 %collective-permute-start.5 = (bf16[256,2048]{1,0:T(8,128)(2,1)}, bf16[256,2048]{1,0:T(8,128)(2,1)S(1)}, u32[]{:S(2)}, u32[]{:S(2)}) collective-permute-start(bf16[256,2048]{1,0:T(8,128)(2,1)} %collective-permute-done.4), channel_id=1, source_target_pairs={{8,0},{9,1},{10,2},{11,3},{12,4},{13,5},{14,6},{15,7}} | collective-permute-start | bytes 3145736 | tf_op jit(solution)/shard_map/ppermute | solution.py:777
  171.3 8.0 collective-permute-start.6
  172.0 21.5 %collective-permute-start.7 = (bf16[256,512]{0,1:T(8,128)(2,1)S(1)}, bf16[256,512]{0,1:T(8,128)(2,1)S(1)}, u32[]{:S(2)}, u32[]{:S(2)}) collective-permute-start(bf16[256,512]{0,1:T(8,128)(2,1)S(1)} %get-tuple-element.274), channel_id=1, source_target_pairs={{0,16},{8,24},{16,0},{24,8},{1,17},{9,25},{17,1},{25,9},{2,18},{10... | collective-permute-start | bytes 786440 | tf_op jit(solution)/shard_map/ppermute | solution.py:796
  172.0 22.2 %collective-permute-start.8 = (bf16[256,512]{0,1:T(8,128)(2,1)S(1)}, bf16[256,512]{0,1:T(8,128)(2,1)S(1)}, u32[]{:S(2)}, u32[]{:S(2)}) collective-permute-start(bf16[256,512]{0,1:T(8,128)(2,1)S(1)} %get-tuple-element.273), channel_id=1, source_target_pairs={{0,8},{8,16},{16,24},{24,0},{1,9},{9,17},{17,25},{25,1},{2,10},{10... | collective-permute-start | bytes 786440 | tf_op jit(solution)/shard_map/ppermute | solution.py:796
  247.9 126.8 %collective-permute-start.9 = (bf16[8,128,2816]{2,1,0:T(8,128)(2,1)}, bf16[8,128,2816]{2,1,0:T(8,128)(2,1)}, u32[]{:S(2)}, u32[]{:S(2)}) collective-permute-start(bf16[8,128,2816]{2,1,0:T(8,128)(2,1)} %all-to-all-done), channel_id=1, source_target_pairs={{0,8},{8,0},{16,24},{24,16},{1,9},{9,1},{17,25},{25,17},{2,10},{10... | collective-permute-start | bytes 17301512 | tf_op jit(solution)/shard_map/ppermute | solution.py:878
  295.3 79.4 %all-to-all-start.1 = ((bf16[8,176,2048]{2,1,0:T(8,128)(2,1)}), bf16[8,176,2048]{2,1,0:T(8,128)(2,1)}, u32[]{:S(2)}, u32[]{:S(2)}) async-start(bf16[8,176,2048]{2,1,0:T(8,128)(2,1)} %param.44), calls=%async_computation.1 | async-start | bytes 11534336 | tf_op jit(solution)/shard_map/all_to_all | solution.py:803
  300.0 380.9 %reduce-scatter.6.cloned.1.call-start = ((), (), s32[]{:S(2)}) async-start(), calls=%async_computation.11 | async-start | bytes 9437184 | tf_op jit(solution)/shard_map/reduce_scatter | solution.py:807
  633.8 35.2 %all-to-all-start.2 = ((f32[8,1,256]{2,1,0:T(1,128)}), f32[8,1,256]{2,1,0:T(1,128)S(1)}, u32[]{:S(2)}, u32[]{:S(2)}) async-start(f32[8,1,256]{2,1,0:T(1,128)} %copy.248), calls=%async_computation.3 | async-start | bytes 16384 | tf_op jit(solution)/shard_map/all_to_all | solution.py:803
  637.2 43.7 %copy-start.2 = (f32[256,2048]{1,0:T(8,128)S(1)}, f32[256,2048]{1,0:T(8,128)}, u32[]{:S(2)}) copy-start(f32[256,2048]{1,0:T(8,128)} %copy-done.1) | copy-start | bytes 6291460
  637.2 43.7 %copy-start.37 = (f32[1,2,8,128]{3,1,2,0:T(2,128)S(1)}, f32[1,2,8,128]{3,1,2,0:T(2,128)}, u32[]{:S(2)}) copy-start(f32[1,2,8,128]{3,1,2,0:T(2,128)} %copy-done.36) | copy-start | bytes 24580
  637.2 43.7 %copy-start.39 = (f32[2048]{0:T(1024)S(1)}, f32[2048]{0:T(1024)}, u32[]{:S(2)}) copy-start(f32[2048]{0:T(1024)} %convert_element_type.292) | copy-start | bytes 24580
  637.2 145.5 %reduce-scatter.8.cloned.1.call-start = ((), (), s32[]{:S(2)}) async-start(), calls=%async_computation.12 | async-start | bytes 9437184 | tf_op jit(solution)/shard_map/reduce_scatter | solution.py:807
  691.9 21.3 %collective-permute-start.12 = (bf16[256,512]{1,0:T(8,128)(2,1)S(1)}, bf16[256,512]{1,0:T(8,128)(2,1)S(1)}, u32[]{:S(2)}, u32[]{:S(2)}) collective-permute-start(bf16[256,512]{1,0:T(8,128)(2,1)S(1)} %get-tuple-element.270), channel_id=1, source_target_pairs={{0,8},{8,16},{16,24},{24,0},{1,9},{9,17},{17,25},{25,1},{2,10},{10... | collective-permute-start | bytes 786440 | tf_op jit(solution)/shard_map/ppermute | solution.py:796
  693.5 19.7 %collective-permute-start.11 = (bf16[256,512]{1,0:T(8,128)(2,1)S(1)}, bf16[256,512]{1,0:T(8,128)(2,1)S(1)}, u32[]{:S(2)}, u32[]{:S(2)}) collective-permute-start(bf16[256,512]{1,0:T(8,128)(2,1)S(1)} %get-tuple-element.271), channel_id=1, source_target_pairs={{0,16},{8,24},{16,0},{24,8},{1,17},{9,25},{17,1},{25,9},{2,18},{10... | collective-permute-start | bytes 786440 | tf_op jit(solution)/shard_map/ppermute | solution.py:796
  695.9 14.4 %collective-permute-start.10 = (bf16[256,512]{1,0:T(8,128)(2,1)S(1)}, bf16[256,512]{1,0:T(8,128)(2,1)S(1)}, u32[]{:S(2)}, u32[]{:S(2)}) collective-permute-start(bf16[256,512]{1,0:T(8,128)(2,1)S(1)} %get-tuple-element.272), channel_id=1, source_target_pairs={{0,24},{8,0},{16,8},{24,16},{1,25},{9,1},{17,9},{25,17},{2,26},{10... | collective-permute-start | bytes 786440 | tf_op jit(solution)/shard_map/ppermute | solution.py:796
  704.7 584.4 %reduce-scatter.14.cloned.1.call-start = ((), (), s32[]{:S(2)}) async-start(), calls=%async_computation.15 | async-start | bytes 7520256 | tf_op jit(solution)/shard_map/reduce_scatter | solution.py:1032
  782.7 562.2 %reduce-scatter.12.cloned.1.call-start = ((), (), s32[]{:S(2)}) async-start(), calls=%async_computation.14 | async-start | bytes 5242880 | tf_op jit(solution)/shard_map/reduce_scatter | solution.py:1035
  783.5 566.6 %reduce-scatter.10.cloned.1.call-start = ((), (), s32[]{:S(2)}) async-start(), calls=%async_computation.13 | async-start | bytes 9437184 | tf_op jit(solution)/shard_map/reduce_scatter | solution.py:1036
  784.2 569.9 %all-gather.19.cloned.1.call-start = ((), (), s32[]{:S(2)}) async-start(), calls=%async_computation.17 | async-start | bytes 4177920 | tf_op jit(solution)/shard_map/all_gather | solution.py:1052
  (60 other events, 385.6 us)
Sparse Core Ops, SparseCore 0:
  34.4 76.2 all-gather.10
  112.6 63.9 all-gather.12
  178.4 54.3 all-gather.16
  235.2 54.3 all-gather.14
  611.8 69.0 reduce-scatter.5
  704.9 68.5 reduce-scatter.7
  782.8 95.0 reduce-scatter.13
  880.3 142.1 reduce-scatter.11
  1026.3 76.6 reduce-scatter.9
  1289.3 64.6 all-gather.18

commit v6 on v5

--- a/solution.py
+++ b/solution.py
@@ -221,7 +221,10 @@
             return
         if block > 0:
             arrivals[index, ORDER[block]].wait_recv()
-        if block in LEAVE:
+        if index > 0:
+            for k in (3, 5, 6, 7) if block == 0 else ():
+                arrivals[index, k].start()
+        elif block in LEAVE:
             left, leaving = LEAVE[block]
             for k in left:
                 arrivals[index, k].wait_send()
@@ -336,8 +339,8 @@
             keep(c).wait()
             outward(c).wait_send()
 
-    for (_, k), copy in arrivals.items():
-        if k in (1, 6, 7):
+    for (index, k), copy in arrivals.items():
+        if index > 0 or k in (1, 6, 7):
             copy.wait_send()
 
 

time: 1390 us -> 1390 us (level)
  no operation moved by 1% of the time
where the time goes in v6:
time: 1390 us; the launch traced here: 1380 us
  Pallas kernels  763 us (55%)
  matrix products  181 us (13%)
  waiting for transfers between devices  165 us (12%)
  local copies, waits for them, and re-layouts  111 us (8%)
  other arithmetic  87.7 us (6%)
  starting transfers between devices  34.7 us (2%)
  blocking collectives  19.1 us (1%)
  between operations  17 us (1%)
    pallas_call x1, Pallas kernels, combine(): pl.pallas_call(functools.partial(combine_kernel, tuple(plan)), out_shape=...  505 us
    pallas_call x1, Pallas kernels, feed_forward(): pl.pallas_call(feed_forward_kernel, out_shape=[jax.ShapeDtypeStruct((rows...  237 us
    dot_general x14, matrix products, dot(): lax.dot_general(a, b, (contract, ((), ())), preferred_element_type=f32)  158 us
    unnamed x183, local copies, waits for them, and re-layouts  60.2 us
    ppermute x3, waiting for transfers between devices, gather_seq(): down = lax.ppermute(down, 'seq', [(i + 1, i) for i in range(seq - 1 - hop)])  42.8 us
    all_gather x1, waiting for transfers between devices, on_device(): lax.all_gather(after(second, fetched, upstream_all), 'fsdp', axis=0, tile...  28.5 us
  transfers between devices with their start and end apart: 26, of which 13 were waited for; matrix products, arithmetic and copies ran while one was open for 24% of the time, Pallas kernels for 38%

profile of v6, /device:TPU:0, one launch (start us, length us, event | category | flops | bytes accessed | tf_op | source)
XLA Modules:
  0.0 1378.8 jit_solution(797090108247332340)
XLA Ops:
  11.6 9.9 all-reduce.3
  22.9 9.2 all-gather.4
  52.3 9.2 collective-permute-done
  72.2 22.4 %collective-permute-done.4 = bf16[256,2048]{1,0:T(8,128)(2,1)} collective-permute-done((bf16[256,2048]{1,0:T(8,128)(2,1)S(1)}, bf16[256,2048]{1,0:T(8,128)(2,1)}, u32[]{:S(2)}, u32[]{:S(2)}) %collective-permute-start.4) | collective-permute-done | bytes 1048608 | tf_op jit(solution)/shard_map/ppermute | solution.py:780
  101.4 19.4 %collective-permute-done.5 = bf16[256,2048]{1,0:T(8,128)(2,1)S(1)} collective-permute-done((bf16[256,2048]{1,0:T(8,128)(2,1)}, bf16[256,2048]{1,0:T(8,128)(2,1)S(1)}, u32[]{:S(2)}, u32[]{:S(2)}) %collective-permute-start.5) | collective-permute-done | bytes 1048608 | tf_op jit(solution)/shard_map/ppermute | solution.py:780
  126.9 12.3 convolution_add_fusion
  139.2 7.6 reshape.857
  146.8 6.9 copy.236
  180.0 13.5 collective-permute-done.7
  197.8 6.2 multiply_reduce_fusion.6
  206.5 26.4 %all-gather.17.cloned.1.call-done = bf16[1,2048,2048]{2,1,0:T(8,128)(2,1)} async-done(((bf16[1,256,2048]{2,1,0:T(8,128)(2,1)}), bf16[1,2048,2048]{2,1,0:T(8,128)(2,1)}) %all-gather.17.cloned.1.call-update) | async-done | bytes 8388624 | tf_op jit(solution)/shard_map/all_gather | solution.py:873
  249.4 11.7 fusion.138.u
  261.1 28.5 %all-gather.15.cloned.1.call-done.x.refs_3_ = bf16[2048,2048]{1,0:T(8,128)(2,1)} async-done(((bf16[256,2048]{1,0:T(8,128)(2,1)}), bf16[2048,2048]{1,0:T(8,128)(2,1)}) %all-gather.15.cloned.1.call-update) | async-done | bytes 8388624 | tf_op jit(solution)/shard_map/all_gather | solution.py:902
  301.6 21.7 %shard_map.238 = (bf16[2048,704]{1,0:T(8,128)(2,1)}, bf16[2048,704]{1,0:T(8,128)(2,1)}, bf16[2048,704]{1,0:T(8,128)(2,1)}, f32[2048,1]{1,0:T(8,128)S(1)}) custom-call(bf16[2048,2048]{1,0:T(8,128)(2,1)} %all-gather.15.cloned.1.call-done.x.refs_3_, f32[2048,704]{1,0:T(8,128)} %fusion.138.u, bf16[2048,704]{1,0:T(8,128)(2,1)} %bitcast.295, ...), custom_call_target="tpu_custom_call" | custom-call | flops 17716740096 | bytes 34078720 | tf_op jit(solution)/shard_map/pallas_call | solution.py:743
  323.3 10.7 convolution_convert_fusion.6
  338.6 11.6 convolution_convert_fusion.5.refs_1_
  350.1 10.5 convolution_convert_fusion.4.refs_2_
  360.6 14.1 %collective-permute-done.9 = bf16[8,128,2816]{2,1,0:T(8,128)(2,1)} collective-permute-done((bf16[8,128,2816]{2,1,0:T(8,128)(2,1)}, bf16[8,128,2816]{2,1,0:T(8,128)(2,1)}, u32[]{:S(2)}, u32[]{:S(2)}) %collective-permute-start.9) | collective-permute-done | bytes 5767200 | tf_op jit(solution)/shard_map/ppermute | solution.py:881
  374.7 236.9 %shard_map.239 = (bf16[2048,704]{1,0:T(8,128)(2,1)}, bf16[2048,704]{1,0:T(8,128)(2,1)}, bf16[2048,704]{1,0:T(8,128)(2,1)}, bf16[2048,1408]{1,0:T(8,128)(2,1)}, b...) custom-call(bf16[2048,704]{1,0:T(8,128)(2,1)} %bitcast.297, ...), custom_call_target="tpu_custom_call" | custom-call | flops 88583700480 | bytes 838860800 | tf_op jit(solution)/shard_map/pallas_call | solution.py:673
  613.6 19.6 %convolution_convert_fusion.3.refs_1_ = bf16[1408,2048]{1,0:T(8,128)(2,1)} fusion(bf16[2048,1408]{1,0:T(8,128)(2,1)} %get-tuple-element.153, bf16[1,2048,2048]{2,1,0:T(8,128)(2,1)} %all-gather.17.cloned.1.call-done), kind=kOutput, calls=%fused_computation.10 | convolution fusion | flops 11814043648 | bytes 19922944 | tf_op jit(solution)/shard_map/dot_general | solution.py:28
  637.3 31.8 %convolution_convert_fusion.refs_0_ = bf16[2048,2816]{1,0:T(8,128)(2,1)} fusion(bf16[2048,2048]{1,0:T(8,128)(2,1)} %all-gather.15.cloned.1.call-done.x.refs_3_, bf16[2048,2816]{1,0:T(8,128)(2,1)} %get-tuple-element.154), kind=kOutput, calls=%fused_computation | convolution fusion | flops 23628087296 | bytes 31457280 | tf_op jit(solution)/shard_map/dot_general | solution.py:28
  669.1 11.8 reduce-scatter.6.cloned.1.call-done
  697.7 7.0 convolution_convert_fusion.2
  751.1 14.2 %fusion.127 = (bf16[1024,2048]{1,0:T(8,128)(2,1)}, bf16[2048]{0:T(1024)(128)(2,1)S(1)}) fusion(f32[1024]{0:T(1024)S(1)} %copy-done.60, bf16[1792,2048]{1,0:T(8,128)(2,1)} %copy-done.14, s32[]{:T(128)S(6)} %select_n.95, bf16[1024,1536]{0,1:T(8,128)(2,1)} %bitcast.298, bf16[2048,1536]{1,0:T(8,128)(2,1)} %all-gather.11.cloned.1.call-done), kind=kOutput, calls=%fused_computation.301 | convolution fusion | flops 6452934656 | bytes 17833988 | tf_op jit(solution)/shard_map/dot_general | solution.py:28
  765.4 11.0 convolution_convert_fusion.1
  776.5 6.2 pad_maximum_fusion
  784.7 504.6 %combine_1.1 = (bf16[2048,2816]{1,0:T(8,128)(2,1)}, bf16[1408,2048]{1,0:T(8,128)(2,1)}, bf16[256,2048]{1,0:T(8,128)(2,1)S(1)}, bf16[2048,2816]{1,0:T(8,128)(2,1)...) custom-call(bf16[2048,2816]{1,0:T(8,128)(2,1)} %convolution_convert_fusion.refs_0_, ...), custom_call_target="tpu_custom_call" | custom-call | flops 18350080 | bytes 1835008000 | tf_op jit(solution)/shard_map/combine_1/pallas_call | solution.py:367
  1294.4 6.5 copy.286
  1300.9 8.6 maximum_convert_fusion.1
  1309.5 12.2 copy.285
  1323.3 8.7 convert.62
  1332.0 13.0 convert.61
  (378 shorter events, 218.1 us)
Async XLA Ops:
  7.2 119.7 %all-gather.11.cloned.1.call-start = ((), (), s32[]{:S(2)}) async-start(), calls=%async_computation.8 | async-start | bytes 7077888 | tf_op jit(solution)/shard_map/all_gather | solution.py:869
  34.3 163.5 %all-gather.13.cloned.1.call-start = ((), (), s32[]{:S(2)}) async-start(), calls=%async_computation.9 | async-start | bytes 9437184 | tf_op jit(solution)/shard_map/all_gather | solution.py:872
  35.0 26.4 %collective-permute-start = (bf16[256,2048]{1,0:T(8,128)(2,1)S(1)}, bf16[256,2048]{1,0:T(8,128)(2,1)}, u32[]{:S(2)}, u32[]{:S(2)}) collective-permute-start(bf16[256,2048]{1,0:T(8,128)(2,1)S(1)} %bitcast.271), channel_id=1, source_target_pairs={{0,8},{8,16},{16,24},{1,9},{9,17},{17,25},{2,10},{10,18},{18,26},{... | collective-permute-start | bytes 3145736 | tf_op jit(solution)/shard_map/ppermute | solution.py:779
  39.5 27.0 %collective-permute-start.3 = (bf16[256,2048]{1,0:T(8,128)(2,1)S(1)}, bf16[256,2048]{1,0:T(8,128)(2,1)S(1)}, u32[]{:S(2)}, u32[]{:S(2)}) collective-permute-start(bf16[256,2048]{1,0:T(8,128)(2,1)S(1)} %bitcast.272), channel_id=1, source_target_pairs={{8,0},{16,8},{24,16},{9,1},{17,9},{25,17},{10,2},{18,10},{26,18},{... | collective-permute-start | bytes 3145736 | tf_op jit(solution)/shard_map/ppermute | solution.py:780
  46.6 159.9 %all-to-all-start = ((bf16[8,128,2816]{2,1,0:T(8,128)(2,1)}), bf16[8,128,2816]{2,1,0:T(8,128)(2,1)}, u32[]{:S(2)}, u32[]{:S(2)}) async-start(bf16[8,128,2816]{2,1,0:T(8,128)(2,1)} %constant_dynamic-slice_fusion.4), calls=%async_computation | async-start | bytes 11534336 | tf_op jit(solution)/shard_map/all_to_all | solution.py:806
  51.5 181.4 %all-gather.17.cloned.1.call-start = ((), (), s32[]{:S(2)}) async-start(), calls=%async_computation.16 | async-start | bytes 9437184 | tf_op jit(solution)/shard_map/all_gather | solution.py:873
  52.2 237.4 %all-gather.15.cloned.1.call-start = ((), (), s32[]{:S(2)}) async-start(), calls=%async_computation.10 | async-start | bytes 9437184 | tf_op jit(solution)/shard_map/all_gather | solution.py:902
  61.4 6.4 collective-permute-start.1
  65.5 92.4 %copy-start.19 = (f32[1024,128]{1,0:T(8,128)}, f32[1024,128]{1,0:T(8,128)S(1)}, u32[]{:S(2)}) copy-start(f32[1024,128]{1,0:T(8,128)S(1)} %get-tuple-element.280) | copy-start | bytes 1572868
  65.5 92.4 %copy-start.21 = (f32[1024,128]{1,0:T(8,128)}, f32[1024,128]{1,0:T(8,128)S(1)}, u32[]{:S(2)}) copy-start(f32[1024,128]{1,0:T(8,128)S(1)} %get-tuple-element.281) | copy-start | bytes 1572868
  66.5 28.1 %collective-permute-start.4 = (bf16[256,2048]{1,0:T(8,128)(2,1)S(1)}, bf16[256,2048]{1,0:T(8,128)(2,1)}, u32[]{:S(2)}, u32[]{:S(2)}) collective-permute-start(bf16[256,2048]{1,0:T(8,128)(2,1)S(1)} %collective-permute-done.3), channel_id=1, source_target_pairs={{8,0},{16,8},{9,1},{17,9},{10,2},{18,10},{11,3},{19,11},{12,4},{20... | collective-permute-start | bytes 3145736 | tf_op jit(solution)/shard_map/ppermute | solution.py:780
  67.8 28.1 %collective-permute-start.2 = (bf16[256,2048]{1,0:T(8,128)(2,1)}, bf16[256,2048]{1,0:T(8,128)(2,1)}, u32[]{:S(2)}, u32[]{:S(2)}) collective-permute-start(bf16[256,2048]{1,0:T(8,128)(2,1)} %collective-permute-done.1), channel_id=1, source_target_pairs={{16,24},{17,25},{18,26},{19,27},{20,28},{21,29},{22,30},{23,31}} | collective-permute-start | bytes 3145736 | tf_op jit(solution)/shard_map/ppermute | solution.py:779
  69.5 52.3 %copy-start.34 = (f32[1,2,8,128]{3,1,2,0:T(2,128)}, f32[1,2,8,128]{3,1,2,0:T(2,128)S(1)}, u32[]{:S(2)}) copy-start(f32[1,2,8,128]{3,1,2,0:T(2,128)S(1)} %copy.329) | copy-start | bytes 24580
  94.6 26.1 %collective-permute-start.5 = (bf16[256,2048]{1,0:T(8,128)(2,1)}, bf16[256,2048]{1,0:T(8,128)(2,1)S(1)}, u32[]{:S(2)}, u32[]{:S(2)}) collective-permute-start(bf16[256,2048]{1,0:T(8,128)(2,1)} %collective-permute-done.4), channel_id=1, source_target_pairs={{8,0},{9,1},{10,2},{11,3},{12,4},{13,5},{14,6},{15,7}} | collective-permute-start | bytes 3145736 | tf_op jit(solution)/shard_map/ppermute | solution.py:780
  171.3 8.0 collective-permute-start.6
  172.0 21.5 %collective-permute-start.7 = (bf16[256,512]{0,1:T(8,128)(2,1)S(1)}, bf16[256,512]{0,1:T(8,128)(2,1)S(1)}, u32[]{:S(2)}, u32[]{:S(2)}) collective-permute-start(bf16[256,512]{0,1:T(8,128)(2,1)S(1)} %get-tuple-element.274), channel_id=1, source_target_pairs={{0,16},{8,24},{16,0},{24,8},{1,17},{9,25},{17,1},{25,9},{2,18},{10... | collective-permute-start | bytes 786440 | tf_op jit(solution)/shard_map/ppermute | solution.py:799
  172.0 22.2 %collective-permute-start.8 = (bf16[256,512]{0,1:T(8,128)(2,1)S(1)}, bf16[256,512]{0,1:T(8,128)(2,1)S(1)}, u32[]{:S(2)}, u32[]{:S(2)}) collective-permute-start(bf16[256,512]{0,1:T(8,128)(2,1)S(1)} %get-tuple-element.273), channel_id=1, source_target_pairs={{0,8},{8,16},{16,24},{24,0},{1,9},{9,17},{17,25},{25,1},{2,10},{10... | collective-permute-start | bytes 786440 | tf_op jit(solution)/shard_map/ppermute | solution.py:799
  247.9 126.8 %collective-permute-start.9 = (bf16[8,128,2816]{2,1,0:T(8,128)(2,1)}, bf16[8,128,2816]{2,1,0:T(8,128)(2,1)}, u32[]{:S(2)}, u32[]{:S(2)}) collective-permute-start(bf16[8,128,2816]{2,1,0:T(8,128)(2,1)} %all-to-all-done), channel_id=1, source_target_pairs={{0,8},{8,0},{16,24},{24,16},{1,9},{9,1},{17,25},{25,17},{2,10},{10... | collective-permute-start | bytes 17301512 | tf_op jit(solution)/shard_map/ppermute | solution.py:881
  295.3 79.4 %all-to-all-start.1 = ((bf16[8,176,2048]{2,1,0:T(8,128)(2,1)}), bf16[8,176,2048]{2,1,0:T(8,128)(2,1)}, u32[]{:S(2)}, u32[]{:S(2)}) async-start(bf16[8,176,2048]{2,1,0:T(8,128)(2,1)} %param.44), calls=%async_computation.1 | async-start | bytes 11534336 | tf_op jit(solution)/shard_map/all_to_all | solution.py:806
  300.0 380.9 %reduce-scatter.6.cloned.1.call-start = ((), (), s32[]{:S(2)}) async-start(), calls=%async_computation.11 | async-start | bytes 9437184 | tf_op jit(solution)/shard_map/reduce_scatter | solution.py:810
  633.8 35.2 %all-to-all-start.2 = ((f32[8,1,256]{2,1,0:T(1,128)}), f32[8,1,256]{2,1,0:T(1,128)S(1)}, u32[]{:S(2)}, u32[]{:S(2)}) async-start(f32[8,1,256]{2,1,0:T(1,128)} %copy.248), calls=%async_computation.3 | async-start | bytes 16384 | tf_op jit(solution)/shard_map/all_to_all | solution.py:806
  637.2 43.7 %copy-start.2 = (f32[256,2048]{1,0:T(8,128)S(1)}, f32[256,2048]{1,0:T(8,128)}, u32[]{:S(2)}) copy-start(f32[256,2048]{1,0:T(8,128)} %copy-done.1) | copy-start | bytes 6291460
  637.2 43.7 %copy-start.37 = (f32[1,2,8,128]{3,1,2,0:T(2,128)S(1)}, f32[1,2,8,128]{3,1,2,0:T(2,128)}, u32[]{:S(2)}) copy-start(f32[1,2,8,128]{3,1,2,0:T(2,128)} %copy-done.36) | copy-start | bytes 24580
  637.2 43.7 %copy-start.39 = (f32[2048]{0:T(1024)S(1)}, f32[2048]{0:T(1024)}, u32[]{:S(2)}) copy-start(f32[2048]{0:T(1024)} %convert_element_type.292) | copy-start | bytes 24580
  637.2 145.5 %reduce-scatter.8.cloned.1.call-start = ((), (), s32[]{:S(2)}) async-start(), calls=%async_computation.12 | async-start | bytes 9437184 | tf_op jit(solution)/shard_map/reduce_scatter | solution.py:810
  691.9 21.3 %collective-permute-start.12 = (bf16[256,512]{1,0:T(8,128)(2,1)S(1)}, bf16[256,512]{1,0:T(8,128)(2,1)S(1)}, u32[]{:S(2)}, u32[]{:S(2)}) collective-permute-start(bf16[256,512]{1,0:T(8,128)(2,1)S(1)} %get-tuple-element.270), channel_id=1, source_target_pairs={{0,8},{8,16},{16,24},{24,0},{1,9},{9,17},{17,25},{25,1},{2,10},{10... | collective-permute-start | bytes 786440 | tf_op jit(solution)/shard_map/ppermute | solution.py:799
  693.5 19.7 %collective-permute-start.11 = (bf16[256,512]{1,0:T(8,128)(2,1)S(1)}, bf16[256,512]{1,0:T(8,128)(2,1)S(1)}, u32[]{:S(2)}, u32[]{:S(2)}) collective-permute-start(bf16[256,512]{1,0:T(8,128)(2,1)S(1)} %get-tuple-element.271), channel_id=1, source_target_pairs={{0,16},{8,24},{16,0},{24,8},{1,17},{9,25},{17,1},{25,9},{2,18},{10... | collective-permute-start | bytes 786440 | tf_op jit(solution)/shard_map/ppermute | solution.py:799
  695.9 14.4 %collective-permute-start.10 = (bf16[256,512]{1,0:T(8,128)(2,1)S(1)}, bf16[256,512]{1,0:T(8,128)(2,1)S(1)}, u32[]{:S(2)}, u32[]{:S(2)}) collective-permute-start(bf16[256,512]{1,0:T(8,128)(2,1)S(1)} %get-tuple-element.272), channel_id=1, source_target_pairs={{0,24},{8,0},{16,8},{24,16},{1,25},{9,1},{17,9},{25,17},{2,26},{10... | collective-permute-start | bytes 786440 | tf_op jit(solution)/shard_map/ppermute | solution.py:799
  704.7 584.6 %reduce-scatter.14.cloned.1.call-start = ((), (), s32[]{:S(2)}) async-start(), calls=%async_computation.15 | async-start | bytes 7520256 | tf_op jit(solution)/shard_map/reduce_scatter | solution.py:1035
  782.7 562.3 %reduce-scatter.12.cloned.1.call-start = ((), (), s32[]{:S(2)}) async-start(), calls=%async_computation.14 | async-start | bytes 5242880 | tf_op jit(solution)/shard_map/reduce_scatter | solution.py:1038
  783.5 566.7 %reduce-scatter.10.cloned.1.call-start = ((), (), s32[]{:S(2)}) async-start(), calls=%async_computation.13 | async-start | bytes 9437184 | tf_op jit(solution)/shard_map/reduce_scatter | solution.py:1039
  784.2 569.9 %all-gather.19.cloned.1.call-start = ((), (), s32[]{:S(2)}) async-start(), calls=%async_computation.17 | async-start | bytes 4177920 | tf_op jit(solution)/shard_map/all_gather | solution.py:1055
  (60 other events, 385.6 us)
Sparse Core Ops, SparseCore 0:
  34.4 76.2 all-gather.10
  112.6 63.9 all-gather.12
  178.4 54.3 all-gather.16
  235.2 54.3 all-gather.14
  611.8 69.0 reduce-scatter.5
  704.9 68.5 reduce-scatter.7
  782.8 95.0 reduce-scatter.13
  880.3 142.1 reduce-scatter.11
  1026.3 85.1 reduce-scatter.9
  1289.4 64.5 all-gather.18
